TPU v7x, 512 devices: a whole 4x8x8 slice. The times are simulated.
512 devices in a mesh: replica: 16 (over x, y_lo), shard: 32 (over y_hi, z, core).
Axes of the slice: x: 4, y: 8 (y_hi: 2, y_lo: 4; y = y_hi * 4 + y_lo), z: 8, core: 2. Of those that a mesh axis runs over, the one named last changes fastest.
Arguments:
- tokens: bfloat16 [65536, 8192], P(('replica', 'shard')), may hold values from -6 to 6
- cotangent: bfloat16 [65536, 512], P(('replica', 'shard')), may hold values from -6 to 6
- biased: float32 [16, 8192, 512], P('replica', 'shard'), may hold values from -0.0625 to 0.0625
- momentum: float32 [16, 8192, 512], P('replica', 'shard'), may hold values from -0.12 to 0.12
- weight: float32 [16], P('replica'), may hold values from 0.25 to 4
- round_index: int32 [1], replicated, may hold values from 0 to 999999
Outputs:
- projected: bfloat16 [65536, 512], P(('replica', 'shard'))
- mixed: float32 [16, 8192, 512], P('replica', 'shard')
- weight_out: float32 [16], P('replica')
- velocity: float32 [16, 8192, 512], P('replica', 'shard')
- debiased: float32 [16, 8192, 512], P('replica', 'shard')
Inputs may be any that keep to these rules, and one draw needn't show every extreme that they name: `round_index`: any round number.
All inputs are finite; a program needn't handle non-finite values.
Results may differ from a plain program's by a relative error of at most 0.005.
Values may be sent and summed in bfloat16 or wider, within the bound.
No kernel may reach another device: no remote copies, remote signals or barrier semaphores. Data moves between devices by JAX's collectives and lax.ppermute only.
A program may use at most 64 MiB of HBM per device.

v0:
```python
from functools import partial

import jax
import jax.numpy as jnp
from jax import lax
from jax.sharding import PartitionSpec as P

MOMENT = 0.9
LEARN = 0.5


def shifted(block, axis, distance):
    devices = range(lax.axis_size(axis))
    route = [((i - distance) % len(devices), i) for i in devices]
    return lax.ppermute(block, axis, route)


def send_push(dist, payload):
    return shifted(payload, "replica", dist)


def shards(tokens, cotangent, biased, momentum, weight, round_index):
    hops = lax.axis_size("replica").bit_length() - 1
    power = round_index[0] % hops
    numer = biased[0]
    scale = weight[0]
    rep_tokens = tokens.shape[0] * lax.axis_size("shard")
    current = (numer / scale).astype(jnp.bfloat16)
    full_rows = lax.all_gather(current, "shard", axis=0, tiled=True)
    output = jnp.dot(tokens, full_rows, preferred_element_type=jnp.float32)
    feature_cols = lax.all_to_all(tokens, "shard", split_axis=1, concat_axis=0, tiled=True)
    contract = (((0,), (0,)), ((), ()))
    all_cots = lax.all_gather(cotangent, "shard", axis=0, tiled=True)
    gradient = lax.dot_general(feature_cols, all_cots, contract, preferred_element_type=jnp.float32)
    gradient = gradient / rep_tokens
    velocity = MOMENT * momentum[0] + gradient
    nesterov = gradient + MOMENT * velocity
    stepped = numer - LEARN * nesterov
    branches = [partial(send_push, 1 << level) for level in range(hops)]
    stepped_from, weight_from = lax.switch(power, branches, (stepped, weight))
    mixed = 0.5 * (stepped + stepped_from)
    weight_out = 0.5 * (weight + weight_from)
    debiased = mixed / weight_out[0]
    return (output.astype(jnp.bfloat16), mixed[None], weight_out, velocity[None], debiased[None])


def solution(mesh):
    placed = (
        P(("replica", "shard"), None),
        P(("replica", "shard"), None),
        P("replica", "shard", None),
        P("replica", "shard", None),
        P("replica"),
        P(),
    )
    return jax.shard_map(
        shards,
        mesh=mesh,
        in_specs=placed,
        out_specs=(
            P(("replica", "shard"), None),
            P("replica", "shard", None),
            P("replica"),
            P("replica", "shard", None),
            P("replica", "shard", None),
        ),
        check_vma=False,
    )
```

profile of v0, /device:TPU:1, one launch (start us, length us, event | category | flops | bytes accessed | tf_op | source)
XLA Modules:
  0.0 305.3 jit_solution(1820665950758226948)
XLA Ops:
  7.2 0.0 all-gather.5.cloned.1.call-start
  7.2 0.7 all-gather.5.cloned.1.call-update
  7.9 4.1 %copy.13 = bf16[128,8192]{0,1:T(8,128)(2,1)} copy(bf16[128,8192]{1,0:T(8,128)(2,1)} %param.10) | data formatting | bytes 4194304 | tf_op args[0]
  12.0 17.2 %all-to-all-start = ((bf16[128,32,256]{0,2,1:T(8,128)(2,1)}), bf16[128,32,256]{0,2,1:T(8,128)(2,1)S(1)}, u32[]{:S(2)}, u32[]{:S(2)}) async-start(bf16[128,32,256]{0,2,1:T(8,128)(2,1)} %bitcast.34), calls=%async_computation | async-start | bytes 4194304 | tf_op jit(solution)/shard_map/all_to_all | solution.py:31
  29.2 0.0 all-gather.3.cloned.1.call-start
  29.9 53.3 %all-to-all-done = bf16[128,32,256]{0,2,1:T(8,128)(2,1)S(1)} async-done(((bf16[128,32,256]{0,2,1:T(8,128)(2,1)}), bf16[128,32,256]{0,2,1:T(8,128)(2,1)S(1)}, u32[]{:S(2)}, u32[]{:S(2)}) %all-to-all-start) | async-done | bytes 2097184 | tf_op jit(solution)/shard_map/all_to_all | solution.py:31
  83.2 0.0 copy-start.1
  83.2 2.9 copy.14
  86.1 71.5 %all-gather.5.cloned.1.call-done = bf16[4096,512]{1,0:T(8,128)(2,1)} async-done(((bf16[128,512]{1,0:T(8,128)(2,1)}), bf16[4096,512]{1,0:T(8,128)(2,1)}) %all-gather.5.cloned.1.call-update) | async-done | bytes 4194320 | tf_op jit(solution)/shard_map/all_gather | solution.py:33
  157.6 0.0 copy-done.1
  157.6 5.1 %fusion.2 = (f32[1,256,512]{2,1,0:T(8,128)}, f32[256,512]{1,0:T(8,128)S(1)}, bf16[256,512]{1,0:T(8,128)(2,1)}) fusion(f32[1,256,512]{2,1,0:T(8,128)S(1)} %copy-done.1, f32[1,256,512]{2,1,0:T(8,128)} %param.12, f32[]{:T(128)} %bitcast.29, bf16[4096,256]{1,0:T(8,128)(2,1)} %bitcast.35, bf16[4096,512]{1,0:T(8,128)(2,1)} %all-gather.5.cloned.1.call-done), kind=kOutput, calls=%fused_computation.9 | convolution fusion | flops 1074921472 | bytes 8650756 | tf_op jit(solution)/shard_map/dot_general | solution.py:34
  162.7 0.0 copy-start
  162.7 0.0 all-gather.3.cloned.1.call-update
  163.5 16.8 %conditional.1 = (f32[256,512]{1,0:T(8,128)}, f32[1]{0:T(128)}) conditional(s32[]{:T(128)} %clamp.3, (f32[256,512]{1,0:T(8,128)S(1)}, f32[1]{0:T(128)}) %tuple.24, (f32[256,512]{1,0:T(8,128)S(1)}, f32[1]{0:T(128)}) %tuple.24, (f32[256,512]{1,0:T(8,128)S(1)}, f32[1]{0:T(128)}) %tuple.24, (f32[256,512]{1,0:T(8,128)S(1)}, ...), branch_computations={%region_0.1_spmd, %region_1.2_spmd, %region_2.3_spmd, %region_3.4_... | conditional | bytes 2097264 | solution.py:40
  163.6 4.4 %collective-permute-start.6 = (f32[256,512]{1,0:T(8,128)S(1)}, f32[256,512]{1,0:T(8,128)}, u32[]{:S(2)}, u32[]{:S(2)}) collective-permute-start(f32[256,512]{1,0:T(8,128)S(1)} %get-tuple-element.22), channel_id=1, source_target_pairs={{256,0},{288,32},{320,64},{352,96},{384,128},{416,160},{448,192},{... | collective-permute-start | bytes 1572872 | tf_op jit(solution)/shard_map/cond/branch_3_fun/ppermute | solution.py:15
  168.0 2.4 collective-permute-start.7
  170.4 10.0 %collective-permute-done.7 = f32[1]{0:T(128)} collective-permute-done((f32[1]{0:T(128)}, f32[1]{0:T(128)}, u32[]{:S(2)}, u32[]{:S(2)}) %collective-permute-start.7) | collective-permute-done | bytes 36 | tf_op jit(solution)/shard_map/cond/branch_3_fun/ppermute | solution.py:15
  180.3 0.0 collective-permute-done.6
  180.9 2.1 divide_bitcast_fusion
  183.0 107.8 %all-gather.3.cloned.1.call-done = bf16[8192,512]{1,0:T(8,128)(2,1)} async-done(((bf16[256,512]{1,0:T(8,128)(2,1)}), bf16[8192,512]{1,0:T(8,128)(2,1)}) %all-gather.3.cloned.1.call-update) | async-done | bytes 8388624 | tf_op jit(solution)/shard_map/all_gather | solution.py:29
  290.8 0.0 copy-done
  290.8 5.8 %fusion = bf16[128,512]{0,1:T(8,128)(2,1)S(1)} fusion(bf16[8192,512]{1,0:T(8,128)(2,1)} %all-gather.3.cloned.1.call-done, bf16[128,8192]{1,0:T(8,128)(2,1)S(1)} %copy-done), kind=kOutput, calls=%fused_computation.2 | convolution fusion | flops 1073807360 | bytes 10616832 | tf_op jit(solution)/shard_map/dot_general | solution.py:30
  296.6 0.8 copy.15
Async XLA Ops:
  7.2 150.4 %all-gather.5.cloned.1.call-start = ((), (), s32[]{:S(2)}) async-start(), calls=%async_computation.2 | async-start | bytes 4325376 | tf_op jit(solution)/shard_map/all_gather | solution.py:33
  12.0 71.2 %all-to-all-start = ((bf16[128,32,256]{0,2,1:T(8,128)(2,1)}), bf16[128,32,256]{0,2,1:T(8,128)(2,1)S(1)}, u32[]{:S(2)}, u32[]{:S(2)}) async-start(bf16[128,32,256]{0,2,1:T(8,128)(2,1)} %bitcast.34), calls=%async_computation | async-start | bytes 4194304 | tf_op jit(solution)/shard_map/all_to_all | solution.py:31
  29.2 261.6 %all-gather.3.cloned.1.call-start = ((), (), s32[]{:S(2)}) async-start(), calls=%async_computation.1 | async-start | bytes 8650752 | tf_op jit(solution)/shard_map/all_gather | solution.py:29
  83.2 74.4 %copy-start.1 = (f32[1,256,512]{2,1,0:T(8,128)S(1)}, f32[1,256,512]{2,1,0:T(8,128)}, u32[]{:S(2)}) copy-start(f32[1,256,512]{2,1,0:T(8,128)} %param.13) | copy-start | bytes 1572868
  162.7 128.1 %copy-start = (bf16[128,8192]{1,0:T(8,128)(2,1)S(1)}, bf16[128,8192]{1,0:T(8,128)(2,1)}, u32[]{:S(2)}) copy-start(bf16[128,8192]{1,0:T(8,128)(2,1)} %param.10) | copy-start | bytes 6291460
  163.6 16.8 %collective-permute-start.6 = (f32[256,512]{1,0:T(8,128)S(1)}, f32[256,512]{1,0:T(8,128)}, u32[]{:S(2)}, u32[]{:S(2)}) collective-permute-start(f32[256,512]{1,0:T(8,128)S(1)} %get-tuple-element.22), channel_id=1, source_target_pairs={{256,0},{288,32},{320,64},{352,96},{384,128},{416,160},{448,192},{... | collective-permute-start | bytes 1572872 | tf_op jit(solution)/shard_map/cond/branch_3_fun/ppermute | solution.py:15
  168.0 12.3 %collective-permute-start.7 = (f32[1]{0:T(128)}, f32[1]{0:T(128)}, u32[]{:S(2)}, u32[]{:S(2)}) collective-permute-start(f32[1]{0:T(128)} %get-tuple-element.23), channel_id=1, source_target_pairs={{256,0},{288,32},{320,64},{352,96},{384,128},{416,160},{448,192},{... | collective-permute-start | bytes 20 | tf_op jit(solution)/shard_map/cond/branch_3_fun/ppermute | solution.py:15
Sparse Core Ops, SparseCore 0:
  11.4 146.1 all-gather.4
  162.8 127.9 all-gather.2
where the time goes:
time: 306 us; the launch traced here: 305 us
  waiting for transfers between devices  243 us (79%)
  starting transfers between devices  24.1 us (8%)
  between operations  17.2 us (6%)
  matrix products  10.9 us (4%)
  local copies, waits for them, and re-layouts  7.76 us (3%)
    all_gather x1, waiting for transfers between devices, shards(): full_rows = lax.all_gather(current, 'shard', axis=0, tiled=True)  108 us
    all_gather x1, waiting for transfers between devices, shards(): all_cots = lax.all_gather(cotangent, 'shard', axis=0, tiled=True)  71.5 us
    all_to_all x1, waiting for transfers between devices, shards(): lax.all_to_all(tokens, 'shard', split_axis=1, concat_axis=0, tiled=True)  53.3 us
    all_to_all x1, starting transfers between devices, shards(): lax.all_to_all(tokens, 'shard', split_axis=1, concat_axis=0, tiled=True)  17.2 us
    ppermute x2, waiting for transfers between devices, shifted(): return lax.ppermute(block, axis, route)  9.96 us
    ppermute x2, starting transfers between devices, shifted(): return lax.ppermute(block, axis, route)  6.79 us
  transfers between devices with their start and end apart: 5, of which 4 were waited for; matrix products, arithmetic and copies ran while one was open for 3% of the time, Pallas kernels for 0%

commit v1 on v0

v1 whole, which is shorter than its diff:
```python
from functools import partial

import jax
import jax.numpy as jnp
from jax import lax
from jax.experimental import pallas as pl
from jax.experimental.pallas import tpu as pltpu
from jax.sharding import Mesh, PartitionSpec as P

MOMENT = 0.9
LEARN = 0.5
SHARD = ("yh", "z", "core")
PIECES = (128, 128)
PAIRS = ((0, 0), (0, 1), (1, 0), (1, 1))
F32, BF16 = jnp.float32, jnp.bfloat16
VMEM = 48 * 1024 * 1024
ANY = pl.BlockSpec(memory_space=pl.ANY)


def params(**kw):
    return pltpu.CompilerParams(vmem_limit_bytes=VMEM, **kw)


def cost(flops, bytes_):
    return pl.CostEstimate(flops=flops, bytes_accessed=bytes_, transcendentals=0)


def pack(tokens, biased, weight, place, nz, feats):
    rows = tokens.shape[0]
    kv = biased.shape[-1]
    steps = 4
    zs = nz // steps
    n = len(PIECES)
    half = tokens.shape[1] // 2

    def kernel(place_ref, weight_ref, near, far, numer, current, *outs):
        c = place_ref[1]
        current[...] = (numer[0] / weight_ref[0]).astype(BF16)
        for p, (dy, dc) in enumerate(PAIRS):
            src = far if dy else near
            col = c if dc == 0 else 1 - c
            for z in range(zs):
                start = pl.multiple_of((z * 2 + col) * feats, feats)
                turned = src[:, pl.ds(start, feats)].T
                at = 0
                for k, f in enumerate(PIECES):
                    outs[p * n + k][z * f : (z + 1) * f, :] = turned[at : at + f, :]
                    at += f

    cols = half // steps
    grid = pltpu.PrefetchScalarGridSpec(
        num_scalar_prefetch=1,
        grid=(steps,),
        in_specs=[
            pl.BlockSpec(memory_space=pltpu.SMEM),
            pl.BlockSpec((rows, cols), lambda g, place: (0, place[0] * steps + g)),
            pl.BlockSpec((rows, cols), lambda g, place: (0, (1 - place[0]) * steps + g)),
            pl.BlockSpec((1, feats // steps, kv), lambda g, place: (0, g, 0)),
        ],
        out_specs=[pl.BlockSpec((feats // steps, kv), lambda g, place: (g, 0))]
        + [pl.BlockSpec((zs * f, rows), lambda g, place: (g, 0)) for _ in PAIRS for f in PIECES],
    )
    res = pl.pallas_call(
        kernel,
        grid_spec=grid,
        out_shape=[jax.ShapeDtypeStruct((feats, kv), BF16)]
        + [jax.ShapeDtypeStruct((nz * f, rows), BF16) for _ in PAIRS for f in PIECES],
        compiler_params=params(),
        cost_estimate=cost(0, 6 << 20),
        name="pack",
    )(place, weight, tokens, tokens, biased)
    return res[0], [res[1 + p * n : 1 + (p + 1) * n] for p in range(4)]


def grad_part(xs, cots, nz, extra):
    depth, rows = xs[0].shape
    kv = cots[0].shape[1]

    def kernel(*refs):
        x, c, out = refs[:4], refs[4:8], refs[-1]
        cc = [jnp.concatenate([c[i][...], c[i + 1][...]], axis=0) for i in (0, 2)]
        f = depth // nz
        for z in range(nz):
            s = slice(z * f, (z + 1) * f)
            total = jnp.dot(jnp.concatenate([x[0][s, :], x[1][s, :]], axis=1), cc[0], preferred_element_type=F32)
            total += jnp.dot(jnp.concatenate([x[2][s, :], x[3][s, :]], axis=1), cc[1], preferred_element_type=F32)
            out[z] = total.astype(BF16)

    return pl.pallas_call(
        kernel,
        in_specs=[pl.BlockSpec(memory_space=pltpu.VMEM)] * 8 + [ANY] * len(extra),
        out_specs=pl.BlockSpec(memory_space=pltpu.VMEM),
        out_shape=jax.ShapeDtypeStruct((nz, depth // nz, kv), BF16),
        compiler_params=params(),
        cost_estimate=cost(2 * 4 * depth * rows * kv, 3 << 20),
        name="grad_part",
    )(*xs, *cots, *extra)


def out_part(xs, z_rows, nz, extra):
    n = len(PIECES)
    rows = xs[0][0].shape[1]
    kv = z_rows.shape[1]
    feats = z_rows.shape[0] // nz

    def kernel(*refs):
        x = [refs[p * n : (p + 1) * n] for p in range(4)]
        w = refs[4 * n]
        outs = refs[-4:]
        for p in range(4):
            parts = []
            for z in range(nz):
                for k, f in enumerate(PIECES):
                    parts.append(x[p][k][z * f : (z + 1) * f, :])
            turned = jnp.concatenate(parts, axis=0).T
            total = jnp.dot(turned, w[...], preferred_element_type=F32)
            outs[p][...] = total.astype(outs[p].dtype)

    return pl.pallas_call(
        kernel,
        in_specs=[pl.BlockSpec(memory_space=pltpu.VMEM)] * (4 * n + 1) + [ANY] * len(extra),
        out_specs=[pl.BlockSpec(memory_space=pltpu.VMEM)] * 4,
        out_shape=[jax.ShapeDtypeStruct((rows, kv), F32 if p == 0 else BF16) for p in range(4)],
        compiler_params=params(),
        cost_estimate=cost(2 * 4 * feats * nz * rows * kv, 5 << 20),
        name="out_part",
    )(*[a for part in xs for a in part], z_rows, *extra)


def step(got, biased, momentum, rep_tokens, at, extra):
    nz, f, kv = got.shape

    def kernel(got_ref, numer, moment, *refs):
        velocity, stepped, pushed = refs[-3:]
        g = got_ref[0].astype(F32)
        for z in range(1, nz):
            g += got_ref[z].astype(F32)
        g = g * (1.0 / rep_tokens)
        v = MOMENT * moment[0] + g
        velocity[...] = v
        s = numer[0] - LEARN * (g + MOMENT * v)
        stepped[...] = s
        pushed[...] = s.astype(BF16)

    row = pl.BlockSpec((1, f, kv), lambda i: (0, at // f, 0))
    return pl.pallas_call(
        kernel,
        grid=(1,),
        in_specs=[pl.BlockSpec((nz, f, kv), lambda i: (0, 0, 0)), row, row] + [ANY] * len(extra),
        out_specs=[pl.BlockSpec((f, kv), lambda i: (0, 0))] * 3,
        out_shape=[jax.ShapeDtypeStruct((f, kv), t) for t in (F32, F32, BF16)],
        compiler_params=params(),
        cost_estimate=cost(nz * f * kv, nz * f * kv * 2),
        name="step",
    )(got, biased, momentum, *extra)


def send_push(dist, blocks):
    n = lax.axis_size("replica")
    route = [((i - dist) % n, i) for i in range(n)]
    return [lax.ppermute(b, "replica", route) for b in blocks]


def shards(tokens, cotangent, biased, momentum, weight, round_index):
    hops = lax.axis_size("replica").bit_length() - 1
    power = round_index[0] % hops
    ny, nz, nc = (lax.axis_size(a) for a in SHARD)
    rows, width = tokens.shape
    feats = width // (ny * nz * nc)
    rep_tokens = rows * ny * nz * nc
    place = jnp.stack([lax.axis_index("yh"), lax.axis_index("core")]).astype(jnp.int32)

    def swap(block, pair):
        if pair == (0, 0):
            return block
        plane = [(y, c) for y in range(ny) for c in range(nc)]
        route = [(y * nc + c, (y ^ pair[0]) * nc + (c ^ pair[1])) for y, c in plane]
        return lax.ppermute(block, ("yh", "core"), route)

    cots = [swap(cotangent, pair) for pair in PAIRS]
    current, sent = pack(tokens, biased, weight, place, nz, feats)
    z_rows = lax.all_gather(current, "z", axis=0, tiled=True)
    local = [[swap(b, pair) for b in part] for part, pair in zip(sent, PAIRS)]

    parts = []
    for k in range(len(PIECES)):
        extra = [z_rows] if k == len(PIECES) - 1 else []
        part = grad_part([local[p][k] for p in range(4)], cots, nz, extra)
        parts.append(lax.all_to_all(part, "z", 0, 0, tiled=True))

    mine, *others = out_part(local, z_rows, nz, [])
    others = [swap(o, pair) for o, pair in zip(others, PAIRS[1:])]
    output = (mine + sum(o.astype(F32) for o in others)).astype(BF16)

    branches = [partial(send_push, 1 << level) for level in range(hops)]
    velocity, stepped, arrived = [], [], []
    at = 0
    weight_from = None
    for k, f in enumerate(PIECES):
        v, s, pushed = step(parts[k], biased, momentum, rep_tokens, at, [])
        if k == 0:
            came, weight_from = lax.switch(power, branches, (pushed, weight))
        else:
            (came,) = lax.switch(power, branches, (pushed,))
        velocity.append(v)
        stepped.append(s)
        arrived.append(came)
        at += f
    velocity, stepped, arrived = (jnp.concatenate(a, axis=0) for a in (velocity, stepped, arrived))
    mixed = 0.5 * (stepped + arrived.astype(F32))
    weight_out = 0.5 * (weight + weight_from)
    debiased = mixed / weight_out[0]
    return (output, mixed[None], weight_out, velocity[None], debiased[None])


def solution(mesh):
    n_rep, n_shard = mesh.devices.shape
    inner = Mesh(mesh.devices.reshape(n_rep, 2, n_shard // 4, 2), ("replica",) + SHARD)
    rows = P(("replica",) + SHARD, None)
    held = P("replica", SHARD, None)
    return jax.shard_map(
        shards,
        mesh=inner,
        in_specs=(rows, rows, held, held, P("replica"), P()),
        out_specs=(rows, held, P("replica"), held, held),
        check_vma=False,
    )
```

time: 306 us -> 183 us (0.60)
  waiting for transfers between devices: 243 us -> 53.3 us
  starting transfers between devices: 24.1 us -> 79.1 us
  local copies, waits for them, and re-layouts: 7.76 us -> 20.1 us
  matrix products: 10.9 us -> 0 us
  Pallas kernels: 0 us -> 8.48 us
    all_gather x2 -> x1, waiting for transfers between devices: 179 us -> 0.01 us  [shards(): z_rows = lax.all_gather(current, 'z', axis=0, tiled=True)]
    ppermute x2 -> x15, starting transfers between devices: 6.79 us -> 69.4 us  [the longest x12 58.2 us: swap(): return lax.ppermute(block, ('yh', 'core'), route)]
    all_to_all x1 -> x2, waiting for transfers between devices: 53.3 us -> 0.01 us  [shards(): parts.append(lax.all_to_all(part, 'z', 0, 0, tiled=True))]
    ppermute x2 -> x15, waiting for transfers between devices: 9.96 us -> 53.3 us  [the longest x12 37.9 us: swap(): return lax.ppermute(block, ('yh', 'core'), route)]
    unnamed x6 -> x54, local copies, waits for them, and re-layouts: 4.86 us -> 20.1 us
    dot_general x2 -> x0, matrix products: 10.9 us -> none  [the longest x1 5.76 us: shards(): output = jnp.dot(tokens, full_rows, preferred_element_type=jnp.float32)]
    pallas_call x0 -> x6, Pallas kernels: none -> 8.48 us  [the longest x1 2.49 us: pack(): pl.pallas_call(kernel, grid_spec=grid, out_shape=[jax.ShapeDtypeStruct((f...]
    all_to_all x1 -> x2, starting transfers between devices: 17.2 us -> 9.67 us  [shards(): parts.append(lax.all_to_all(part, 'z', 0, 0, tiled=True))]
  transfers between devices with their start and end apart: 5 -> 18, of which waited for: 4 -> 6; matrix products, arithmetic and copies ran while one was open for 3% -> 0% of each run, Pallas kernels for 0% -> 3%
where the time goes in v1:
time: 183 us; the launch traced here: 182 us
  starting transfers between devices  79.1 us (43%)
  waiting for transfers between devices  53.3 us (29%)
  local copies, waits for them, and re-layouts  20.1 us (11%)
  between operations  17.3 us (9%)
  Pallas kernels  8.48 us (5%)
  other arithmetic  3.71 us (2%)
    ppermute x12, starting transfers between devices, swap(): return lax.ppermute(block, ('yh', 'core'), route)  58.2 us
    ppermute x12, waiting for transfers between devices, swap(): return lax.ppermute(block, ('yh', 'core'), route)  37.9 us
    unnamed x54, local copies, waits for them, and re-layouts  20.1 us
    ppermute x3, waiting for transfers between devices, send_push(): return [lax.ppermute(b, 'replica', route) for b in blocks]  15.3 us
    ppermute x3, starting transfers between devices, send_push(): return [lax.ppermute(b, 'replica', route) for b in blocks]  11.2 us
    all_to_all x2, starting transfers between devices, shards(): parts.append(lax.all_to_all(part, 'z', 0, 0, tiled=True))  9.67 us
  transfers between devices with their start and end apart: 18, of which 6 were waited for; matrix products, arithmetic and copies ran while one was open for 0% of the time, Pallas kernels for 3%

profile of v1, /device:TPU:1, one launch (start us, length us, event | category | flops | bytes accessed | tf_op | source)
XLA Modules:
  0.0 182.1 jit_solution(5009280514104218206)
XLA Ops:
  10.6 2.5 %pack.1 = (bf16[256,512]{1,0:T(8,128)(2,1)}, bf16[1024,128]{1,0:T(8,128)(2,1)S(1)}, bf16[1024,128]{1,0:T(8,128)(2,1)S(1)}, bf16[1024,128]{1,0:T(8,128)(2,1)S(1)}...) custom-call(s32[2]{0:T(128)S(1)} %pad_add_fusion.place_ref, ...), custom_call_target="tpu_custom_call" | custom-call | bytes 6291456 | tf_op jit(solution)/shard_map/pack/pallas_call | solution.py:63
  13.1 8.8 %collective-permute-start.12 = (bf16[1024,128]{1,0:T(8,128)(2,1)S(1)}, bf16[1024,128]{1,0:T(8,128)(2,1)S(1)}, u32[]{:S(2)}, u32[]{:S(2)}) collective-permute-start(bf16[1024,128]{1,0:T(8,128)(2,1)S(1)} %get-tuple-element.63), channel_id=1, source_target_pairs={{0,1},{1,0},{16,17},{17,16},{2,3},{3,2},{18,19},{19,18},{4,5},{5,4... | collective-permute-start | bytes 786440 | tf_op jit(solution)/shard_map/ppermute | solution.py:178
  23.8 2.1 %collective-permute-start.14 = (bf16[1024,128]{1,0:T(8,128)(2,1)S(1)}, bf16[1024,128]{1,0:T(8,128)(2,1)S(1)}, u32[]{:S(2)}, u32[]{:S(2)}) collective-permute-start(bf16[1024,128]{1,0:T(8,128)(2,1)S(1)} %get-tuple-element.65), channel_id=1, source_target_pairs={{0,16},{1,17},{16,0},{17,1},{2,18},{3,19},{18,2},{19,3},{4,20},{5,... | collective-permute-start | bytes 786440 | tf_op jit(solution)/shard_map/ppermute | solution.py:178
  25.9 7.8 %collective-permute-start.16 = (bf16[1024,128]{1,0:T(8,128)(2,1)S(1)}, bf16[1024,128]{1,0:T(8,128)(2,1)S(1)}, u32[]{:S(2)}, u32[]{:S(2)}) collective-permute-start(bf16[1024,128]{1,0:T(8,128)(2,1)S(1)} %get-tuple-element.67), channel_id=1, source_target_pairs={{0,17},{1,16},{16,1},{17,0},{2,19},{3,18},{18,3},{19,2},{4,21},{5,... | collective-permute-start | bytes 786440 | tf_op jit(solution)/shard_map/ppermute | solution.py:178
  33.7 2.1 %collective-permute-start.22 = (bf16[128,512]{1,0:T(8,128)(2,1)S(1)}, bf16[128,512]{1,0:T(8,128)(2,1)S(1)}, u32[]{:S(2)}, u32[]{:S(2)}) collective-permute-start(bf16[128,512]{1,0:T(8,128)(2,1)S(1)} %copy-done.24), channel_id=1, source_target_pairs={{0,16},{1,17},{16,0},{17,1},{2,18},{3,19},{18,2},{19,3},{4,20},{5,... | collective-permute-start | bytes 393224 | tf_op jit(solution)/shard_map/ppermute | solution.py:178
  35.8 7.0 %collective-permute-start.23 = (bf16[128,512]{1,0:T(8,128)(2,1)S(1)}, bf16[128,512]{1,0:T(8,128)(2,1)S(1)}, u32[]{:S(2)}, u32[]{:S(2)}) collective-permute-start(bf16[128,512]{1,0:T(8,128)(2,1)S(1)} %copy-done.24), channel_id=1, source_target_pairs={{0,17},{1,16},{16,1},{17,0},{2,19},{3,18},{18,3},{19,2},{4,21},{5,... | collective-permute-start | bytes 393224 | tf_op jit(solution)/shard_map/ppermute | solution.py:178
  42.8 18.6 %collective-permute-done.22.refs_6_ = bf16[128,512]{1,0:T(8,128)(2,1)S(1)} collective-permute-done((bf16[128,512]{1,0:T(8,128)(2,1)S(1)}, bf16[128,512]{1,0:T(8,128)(2,1)S(1)}, u32[]{:S(2)}, u32[]{:S(2)}) %collective-permute-start.22) | collective-permute-done | bytes 131104 | tf_op jit(solution)/shard_map/ppermute | solution.py:178
  61.4 2.8 %collective-permute-done.23.refs_7_ = bf16[128,512]{1,0:T(8,128)(2,1)S(1)} collective-permute-done((bf16[128,512]{1,0:T(8,128)(2,1)S(1)}, bf16[128,512]{1,0:T(8,128)(2,1)S(1)}, u32[]{:S(2)}, u32[]{:S(2)}) %collective-permute-start.23) | collective-permute-done | bytes 131104 | tf_op jit(solution)/shard_map/ppermute | solution.py:178
  68.1 3.6 %all-to-all-start = ((bf16[8,128,512]{2,1,0:T(8,128)(2,1)}), bf16[8,128,512]{2,1,0:T(8,128)(2,1)S(1)}, u32[]{:S(2)}, u32[]{:S(2)}) async-start(bf16[8,128,512]{2,1,0:T(8,128)(2,1)} %grad_part.2), calls=%async_computation | async-start | bytes 2097152 | tf_op jit(solution)/shard_map/all_to_all | solution.py:189
  71.7 4.9 %collective-permute-start.13 = (bf16[1024,128]{1,0:T(8,128)(2,1)}, bf16[1024,128]{1,0:T(8,128)(2,1)S(1)}, u32[]{:S(2)}, u32[]{:S(2)}) collective-permute-start(bf16[1024,128]{1,0:T(8,128)(2,1)} %get-tuple-element.64), channel_id=1, source_target_pairs={{0,1},{1,0},{16,17},{17,16},{2,3},{3,2},{18,19},{19,18},{4,5},{5,4... | collective-permute-start | bytes 786440 | tf_op jit(solution)/shard_map/ppermute | solution.py:178
  76.6 7.1 %collective-permute-start.15 = (bf16[1024,128]{1,0:T(8,128)(2,1)S(1)}, bf16[1024,128]{1,0:T(8,128)(2,1)S(1)}, u32[]{:S(2)}, u32[]{:S(2)}) collective-permute-start(bf16[1024,128]{1,0:T(8,128)(2,1)S(1)} %get-tuple-element.66), channel_id=1, source_target_pairs={{0,16},{1,17},{16,0},{17,1},{2,18},{3,19},{18,2},{19,3},{4,20},{5,... | collective-permute-start | bytes 786440 | tf_op jit(solution)/shard_map/ppermute | solution.py:178
  83.7 2.3 %collective-permute-start.17 = (bf16[1024,128]{1,0:T(8,128)(2,1)S(1)}, bf16[1024,128]{1,0:T(8,128)(2,1)S(1)}, u32[]{:S(2)}, u32[]{:S(2)}) collective-permute-start(bf16[1024,128]{1,0:T(8,128)(2,1)S(1)} %get-tuple-element.68), channel_id=1, source_target_pairs={{0,17},{1,16},{16,1},{17,0},{2,19},{3,18},{18,3},{19,2},{4,21},{5,... | collective-permute-start | bytes 786440 | tf_op jit(solution)/shard_map/ppermute | solution.py:178
  86.0 6.3 %collective-permute-done.15.refs_5_.refs_2_ = bf16[1024,128]{1,0:T(8,128)(2,1)S(1)} collective-permute-done((bf16[1024,128]{1,0:T(8,128)(2,1)S(1)}, bf16[1024,128]{1,0:T(8,128)(2,1)S(1)}, u32[]{:S(2)}, u32[]{:S(2)}) %collective-permute-start.15) | collective-permute-done | bytes 262176 | tf_op jit(solution)/shard_map/ppermute | solution.py:178
  92.3 10.2 %collective-permute-done.17.refs_7_.refs_3_ = bf16[1024,128]{1,0:T(8,128)(2,1)S(1)} collective-permute-done((bf16[1024,128]{1,0:T(8,128)(2,1)S(1)}, bf16[1024,128]{1,0:T(8,128)(2,1)S(1)}, u32[]{:S(2)}, u32[]{:S(2)}) %collective-permute-start.17) | collective-permute-done | bytes 262176 | tf_op jit(solution)/shard_map/ppermute | solution.py:178
  108.9 6.1 %all-to-all-start.1 = ((bf16[8,128,512]{2,1,0:T(8,128)(2,1)}), bf16[8,128,512]{2,1,0:T(8,128)(2,1)}, u32[]{:S(2)}, u32[]{:S(2)}) async-start(bf16[8,128,512]{2,1,0:T(8,128)(2,1)} %copy-done.7), calls=%async_computation.1 | async-start | bytes 2097152 | tf_op jit(solution)/shard_map/all_to_all | solution.py:189
  124.3 6.7 %collective-permute-start.20 = (bf16[128,512]{1,0:T(8,128)(2,1)}, bf16[128,512]{1,0:T(8,128)(2,1)S(1)}, u32[]{:S(2)}, u32[]{:S(2)}) collective-permute-start(bf16[128,512]{1,0:T(8,128)(2,1)} %get-tuple-element.73), channel_id=1, source_target_pairs={{0,17},{1,16},{16,1},{17,0},{2,19},{3,18},{18,3},{19,2},{4,21},{5,... | collective-permute-start | bytes 393224 | tf_op jit(solution)/shard_map/ppermute | solution.py:178
  131.0 5.3 %collective-permute-start.19 = (bf16[128,512]{1,0:T(8,128)(2,1)}, bf16[128,512]{1,0:T(8,128)(2,1)S(1)}, u32[]{:S(2)}, u32[]{:S(2)}) collective-permute-start(bf16[128,512]{1,0:T(8,128)(2,1)} %get-tuple-element.72), channel_id=1, source_target_pairs={{0,16},{1,17},{16,0},{17,1},{2,18},{3,19},{18,2},{19,3},{4,20},{5,... | collective-permute-start | bytes 393224 | tf_op jit(solution)/shard_map/ppermute | solution.py:178
  136.3 2.3 %collective-permute-start.18 = (bf16[128,512]{1,0:T(8,128)(2,1)S(1)}, bf16[128,512]{1,0:T(8,128)(2,1)S(1)}, u32[]{:S(2)}, u32[]{:S(2)}) collective-permute-start(bf16[128,512]{1,0:T(8,128)(2,1)S(1)} %get-tuple-element.71), channel_id=1, source_target_pairs={{0,1},{1,0},{16,17},{17,16},{2,3},{3,2},{18,19},{19,18},{4,5},{5,4... | collective-permute-start | bytes 393224 | tf_op jit(solution)/shard_map/ppermute | solution.py:178
  141.8 16.1 %conditional.2 = (f32[1]{0:T(128)}, bf16[1,128,512]{2,1,0:T(8,128)(2,1)}) conditional(s32[]{:T(128)} %clamp.4, (f32[1]{0:T(128)}, bf16[128,512]{1,0:T(8,128)(2,1)S(1)}) %tuple.44, (f32[1]{0:T(128)}, bf16[128,512]{1,0:T(8,128)(2,1)S(1)}) %tuple.44, (f32[1]{0:T(128)}, bf16[128,512]{1,0:T(8,128)(2,1)S(1)}) %tuple.44, ...), branch_computations={%region_0.1_spmd, %region_1.2_spmd, %region_2.3_spmd, %region_3.4_... | conditional | bytes 524400 | solution.py:202
  141.8 7.3 %collective-permute-start.3 = (bf16[128,512]{1,0:T(8,128)(2,1)S(1)}, bf16[128,512]{1,0:T(8,128)(2,1)}, u32[]{:S(2)}, u32[]{:S(2)}) collective-permute-start(bf16[128,512]{1,0:T(8,128)(2,1)S(1)} %get-tuple-element.30), channel_id=1, source_target_pairs={{448,0},{480,32},{0,64},{32,96},{64,128},{96,160},{128,192},{160,2... | collective-permute-start | bytes 393224 | tf_op jit(solution)/shard_map/cond/branch_1_fun/ppermute | solution.py:161
  151.1 6.8 %collective-permute-done.2 = f32[1]{0:T(128)} collective-permute-done((f32[1]{0:T(128)}, f32[1]{0:T(128)}, u32[]{:S(2)}, u32[]{:S(2)}) %collective-permute-start.2) | collective-permute-done | bytes 36 | tf_op jit(solution)/shard_map/cond/branch_1_fun/ppermute | solution.py:161
  160.7 10.4 %conditional.3 = (bf16[1,128,512]{2,1,0:T(8,128)(2,1)}) conditional(s32[]{:T(128)} %clamp.4, bf16[128,512]{1,0:T(8,128)(2,1)S(1)} %get-tuple-element.78, bf16[128,512]{1,0:T(8,128)(2,1)S(1)} %get-tuple-element.78, bf16[128,512]{1,0:T(8,128)(2,1)S(1)} %get-tuple-element.78, ...), branch_computations={%region_4.5_spmd, %region_5.6_spmd, %region_6.7_spmd, %region_7.8_... | conditional | bytes 524336 | solution.py:204
  162.7 8.5 %collective-permute-done.9 = bf16[128,512]{1,0:T(8,128)(2,1)} collective-permute-done((bf16[128,512]{1,0:T(8,128)(2,1)S(1)}, bf16[128,512]{1,0:T(8,128)(2,1)}, u32[]{:S(2)}, u32[]{:S(2)}) %collective-permute-start.9) | collective-permute-done | bytes 131104 | tf_op jit(solution)/shard_map/cond/branch_1_fun/ppermute | solution.py:161
  172.0 2.1 %broadcast_divide_fusion = (f32[1,256,512]{2,1,0:T(8,128)}, f32[1,256,512]{2,1,0:T(8,128)}) fusion(f32[]{:T(128)} %bitcast.14, bf16[1,128,512]{2,1,0:T(8,128)(2,1)} %get-tuple-element.92, bf16[1,128,512]{2,1,0:T(8,128)(2,1)} %get-tuple-element.77, f32[1,128,512]{2,1,0:T(8,128)S(1)} %bitcast.20, f32[1,128,512]{2,1,0:T(8,128)S(1)} %bitcast.19), kind=kLoop, calls=%fused_computation.3 | loop fusion | flops 1048576 | bytes 1835012 | tf_op jit(solution)/shard_map/div | solution.py:212
  (79 shorter events, 33.6 us)
Async XLA Ops:
  7.2 95.3 %all-gather.2.cloned.1.call-start = ((), (), s32[]{:S(2)}) async-start(), calls=%async_computation.2 | async-start | bytes 2359296 | tf_op jit(solution)/shard_map/all_gather | solution.py:182
  10.6 11.3 %copy-start.24 = (bf16[128,512]{1,0:T(8,128)(2,1)S(1)}, bf16[128,512]{1,0:T(8,128)(2,1)}, u32[]{:S(2)}) copy-start(bf16[128,512]{1,0:T(8,128)(2,1)} %refs_4_.3) | copy-start | bytes 393220
  13.1 89.4 %copy-start.10 = (bf16[1024,128]{1,0:T(8,128)(2,1)}, bf16[1024,128]{1,0:T(8,128)(2,1)S(1)}, u32[]{:S(2)}) copy-start(bf16[1024,128]{1,0:T(8,128)(2,1)S(1)} %get-tuple-element.62.refs_1_.refs_0_) | copy-start | bytes 786436
  13.1 51.2 %collective-permute-start.12 = (bf16[1024,128]{1,0:T(8,128)(2,1)S(1)}, bf16[1024,128]{1,0:T(8,128)(2,1)S(1)}, u32[]{:S(2)}, u32[]{:S(2)}) collective-permute-start(bf16[1024,128]{1,0:T(8,128)(2,1)S(1)} %get-tuple-element.63), channel_id=1, source_target_pairs={{0,1},{1,0},{16,17},{17,16},{2,3},{3,2},{18,19},{19,18},{4,5},{5,4... | collective-permute-start | bytes 786440 | tf_op jit(solution)/shard_map/ppermute | solution.py:178
  21.9 13.9 %collective-permute-start.21 = (bf16[128,512]{1,0:T(8,128)(2,1)S(1)}, bf16[128,512]{1,0:T(8,128)(2,1)S(1)}, u32[]{:S(2)}, u32[]{:S(2)}) collective-permute-start(bf16[128,512]{1,0:T(8,128)(2,1)S(1)} %copy-done.24), channel_id=1, source_target_pairs={{0,1},{1,0},{16,17},{17,16},{2,3},{3,2},{18,19},{19,18},{4,5},{5,4... | collective-permute-start | bytes 393224 | tf_op jit(solution)/shard_map/ppermute | solution.py:178
  23.8 40.4 %collective-permute-start.14 = (bf16[1024,128]{1,0:T(8,128)(2,1)S(1)}, bf16[1024,128]{1,0:T(8,128)(2,1)S(1)}, u32[]{:S(2)}, u32[]{:S(2)}) collective-permute-start(bf16[1024,128]{1,0:T(8,128)(2,1)S(1)} %get-tuple-element.65), channel_id=1, source_target_pairs={{0,16},{1,17},{16,0},{17,1},{2,18},{3,19},{18,2},{19,3},{4,20},{5,... | collective-permute-start | bytes 786440 | tf_op jit(solution)/shard_map/ppermute | solution.py:178
  25.9 38.4 %collective-permute-start.16 = (bf16[1024,128]{1,0:T(8,128)(2,1)S(1)}, bf16[1024,128]{1,0:T(8,128)(2,1)S(1)}, u32[]{:S(2)}, u32[]{:S(2)}) collective-permute-start(bf16[1024,128]{1,0:T(8,128)(2,1)S(1)} %get-tuple-element.67), channel_id=1, source_target_pairs={{0,17},{1,16},{16,1},{17,0},{2,19},{3,18},{18,3},{19,2},{4,21},{5,... | collective-permute-start | bytes 786440 | tf_op jit(solution)/shard_map/ppermute | solution.py:178
  33.7 27.8 %collective-permute-start.22 = (bf16[128,512]{1,0:T(8,128)(2,1)S(1)}, bf16[128,512]{1,0:T(8,128)(2,1)S(1)}, u32[]{:S(2)}, u32[]{:S(2)}) collective-permute-start(bf16[128,512]{1,0:T(8,128)(2,1)S(1)} %copy-done.24), channel_id=1, source_target_pairs={{0,16},{1,17},{16,0},{17,1},{2,18},{3,19},{18,2},{19,3},{4,20},{5,... | collective-permute-start | bytes 393224 | tf_op jit(solution)/shard_map/ppermute | solution.py:178
  35.8 28.5 %collective-permute-start.23 = (bf16[128,512]{1,0:T(8,128)(2,1)S(1)}, bf16[128,512]{1,0:T(8,128)(2,1)S(1)}, u32[]{:S(2)}, u32[]{:S(2)}) collective-permute-start(bf16[128,512]{1,0:T(8,128)(2,1)S(1)} %copy-done.24), channel_id=1, source_target_pairs={{0,17},{1,16},{16,1},{17,0},{2,19},{3,18},{18,3},{19,2},{4,21},{5,... | collective-permute-start | bytes 393224 | tf_op jit(solution)/shard_map/ppermute | solution.py:178
  68.1 39.8 %all-to-all-start = ((bf16[8,128,512]{2,1,0:T(8,128)(2,1)}), bf16[8,128,512]{2,1,0:T(8,128)(2,1)S(1)}, u32[]{:S(2)}, u32[]{:S(2)}) async-start(bf16[8,128,512]{2,1,0:T(8,128)(2,1)} %grad_part.2), calls=%async_computation | async-start | bytes 2097152 | tf_op jit(solution)/shard_map/all_to_all | solution.py:189
  71.7 14.3 %collective-permute-start.13 = (bf16[1024,128]{1,0:T(8,128)(2,1)}, bf16[1024,128]{1,0:T(8,128)(2,1)S(1)}, u32[]{:S(2)}, u32[]{:S(2)}) collective-permute-start(bf16[1024,128]{1,0:T(8,128)(2,1)} %get-tuple-element.64), channel_id=1, source_target_pairs={{0,1},{1,0},{16,17},{17,16},{2,3},{3,2},{18,19},{19,18},{4,5},{5,4... | collective-permute-start | bytes 786440 | tf_op jit(solution)/shard_map/ppermute | solution.py:178
  76.6 15.7 %collective-permute-start.15 = (bf16[1024,128]{1,0:T(8,128)(2,1)S(1)}, bf16[1024,128]{1,0:T(8,128)(2,1)S(1)}, u32[]{:S(2)}, u32[]{:S(2)}) collective-permute-start(bf16[1024,128]{1,0:T(8,128)(2,1)S(1)} %get-tuple-element.66), channel_id=1, source_target_pairs={{0,16},{1,17},{16,0},{17,1},{2,18},{3,19},{18,2},{19,3},{4,20},{5,... | collective-permute-start | bytes 786440 | tf_op jit(solution)/shard_map/ppermute | solution.py:178
  83.7 18.8 %collective-permute-start.17 = (bf16[1024,128]{1,0:T(8,128)(2,1)S(1)}, bf16[1024,128]{1,0:T(8,128)(2,1)S(1)}, u32[]{:S(2)}, u32[]{:S(2)}) collective-permute-start(bf16[1024,128]{1,0:T(8,128)(2,1)S(1)} %get-tuple-element.68), channel_id=1, source_target_pairs={{0,17},{1,16},{16,1},{17,0},{2,19},{3,18},{18,3},{19,2},{4,21},{5,... | collective-permute-start | bytes 786440 | tf_op jit(solution)/shard_map/ppermute | solution.py:178
  107.9 7.1 %copy-start.2 = (bf16[2048,512]{1,0:T(8,128)(2,1)S(1)}, bf16[2048,512]{1,0:T(8,128)(2,1)}, u32[]{:S(2)}) copy-start(bf16[2048,512]{1,0:T(8,128)(2,1)} %all-gather.2.cloned.1.call-done.refs_8_) | copy-start | bytes 6291460
  108.9 50.4 %all-to-all-start.1 = ((bf16[8,128,512]{2,1,0:T(8,128)(2,1)}), bf16[8,128,512]{2,1,0:T(8,128)(2,1)}, u32[]{:S(2)}, u32[]{:S(2)}) async-start(bf16[8,128,512]{2,1,0:T(8,128)(2,1)} %copy-done.7), calls=%async_computation.1 | async-start | bytes 2097152 | tf_op jit(solution)/shard_map/all_to_all | solution.py:189
  121.6 17.7 %copy-start.4 = (f32[1,256,512]{2,1,0:T(8,128)S(1)}, f32[1,256,512]{2,1,0:T(8,128)}, u32[]{:S(2)}) copy-start(f32[1,256,512]{2,1,0:T(8,128)} %numer.5) | copy-start | bytes 1572868
  124.3 34.2 %collective-permute-start.20 = (bf16[128,512]{1,0:T(8,128)(2,1)}, bf16[128,512]{1,0:T(8,128)(2,1)S(1)}, u32[]{:S(2)}, u32[]{:S(2)}) collective-permute-start(bf16[128,512]{1,0:T(8,128)(2,1)} %get-tuple-element.73), channel_id=1, source_target_pairs={{0,17},{1,16},{16,1},{17,0},{2,19},{3,18},{18,3},{19,2},{4,21},{5,... | collective-permute-start | bytes 393224 | tf_op jit(solution)/shard_map/ppermute | solution.py:178
  131.0 27.5 %collective-permute-start.19 = (bf16[128,512]{1,0:T(8,128)(2,1)}, bf16[128,512]{1,0:T(8,128)(2,1)S(1)}, u32[]{:S(2)}, u32[]{:S(2)}) collective-permute-start(bf16[128,512]{1,0:T(8,128)(2,1)} %get-tuple-element.72), channel_id=1, source_target_pairs={{0,16},{1,17},{16,0},{17,1},{2,18},{3,19},{18,2},{19,3},{4,20},{5,... | collective-permute-start | bytes 393224 | tf_op jit(solution)/shard_map/ppermute | solution.py:178
  136.3 22.2 %collective-permute-start.18 = (bf16[128,512]{1,0:T(8,128)(2,1)S(1)}, bf16[128,512]{1,0:T(8,128)(2,1)S(1)}, u32[]{:S(2)}, u32[]{:S(2)}) collective-permute-start(bf16[128,512]{1,0:T(8,128)(2,1)S(1)} %get-tuple-element.71), channel_id=1, source_target_pairs={{0,1},{1,0},{16,17},{17,16},{2,3},{3,2},{18,19},{19,18},{4,5},{5,4... | collective-permute-start | bytes 393224 | tf_op jit(solution)/shard_map/ppermute | solution.py:178
  141.6 17.0 %copy-start.26 = (f32[128,512]{1,0:T(8,128)S(1)}, f32[128,512]{1,0:T(8,128)}, u32[]{:S(2)}) copy-start(f32[128,512]{1,0:T(8,128)} %copy-done.25) | copy-start | bytes 786436
  141.6 17.7 %copy-start.9 = (f32[1,256,512]{2,1,0:T(8,128)S(1)}, f32[1,256,512]{2,1,0:T(8,128)}, u32[]{:S(2)}) copy-start(f32[1,256,512]{2,1,0:T(8,128)} %moment.3) | copy-start | bytes 1572868
  141.8 16.1 %collective-permute-start.3 = (bf16[128,512]{1,0:T(8,128)(2,1)S(1)}, bf16[128,512]{1,0:T(8,128)(2,1)}, u32[]{:S(2)}, u32[]{:S(2)}) collective-permute-start(bf16[128,512]{1,0:T(8,128)(2,1)S(1)} %get-tuple-element.30), channel_id=1, source_target_pairs={{448,0},{480,32},{0,64},{32,96},{64,128},{96,160},{128,192},{160,2... | collective-permute-start | bytes 393224 | tf_op jit(solution)/shard_map/cond/branch_1_fun/ppermute | solution.py:161
  149.1 8.8 %collective-permute-start.2 = (f32[1]{0:T(128)}, f32[1]{0:T(128)}, u32[]{:S(2)}, u32[]{:S(2)}) collective-permute-start(f32[1]{0:T(128)} %get-tuple-element.29), channel_id=1, source_target_pairs={{448,0},{480,32},{0,64},{32,96},{64,128},{96,160},{128,192},{160,2... | collective-permute-start | bytes 20 | tf_op jit(solution)/shard_map/cond/branch_1_fun/ppermute | solution.py:161
  160.8 10.4 %collective-permute-start.9 = (bf16[128,512]{1,0:T(8,128)(2,1)S(1)}, bf16[128,512]{1,0:T(8,128)(2,1)}, u32[]{:S(2)}, u32[]{:S(2)}) collective-permute-start(bf16[128,512]{1,0:T(8,128)(2,1)S(1)} %param.5), channel_id=1, source_target_pairs={{448,0},{480,32},{0,64},{32,96},{64,128},{96,160},{128,192},{160,2... | collective-permute-start | bytes 393224 | tf_op jit(solution)/shard_map/cond/branch_1_fun/ppermute | solution.py:161
  (21 other events, 20.1 us)
Sparse Core Ops, SparseCore 0:
  13.2 46.0 all-gather.1

commit v2 on v0

v2 whole, which is shorter than its diff:
```python
from functools import partial

import jax
import jax.numpy as jnp
from jax import lax
from jax.experimental import pallas as pl
from jax.experimental.pallas import tpu as pltpu
from jax.sharding import Mesh, PartitionSpec as P

MOMENT = 0.9
LEARN = 0.5
SHARD = ("yh", "z", "core")
F32, BF16 = jnp.float32, jnp.bfloat16
VMEM = pl.BlockSpec(memory_space=pltpu.VMEM)
SMEM = pl.BlockSpec(memory_space=pltpu.SMEM)
ANY = pl.BlockSpec(memory_space=pl.ANY)
TURN = (((0,), (0,)), ((), ()))
TAIL = 16
WAIT = 50_000_000_000


def call(name, kernel, outs, ins, specs, flops=0, moved=0, **kw):
    return pl.pallas_call(
        kernel,
        in_specs=specs,
        out_specs=[VMEM] * len(outs),
        out_shape=[jax.ShapeDtypeStruct(s, t) for s, t in outs],
        compiler_params=pltpu.CompilerParams(vmem_limit_bytes=12 << 20),
        cost_estimate=pl.CostEstimate(flops=flops, bytes_accessed=moved, transcendentals=0),
        name=name,
        **kw,
    )(*ins)


def rounded_rows(biased, weight):
    def kernel(weight_ref, numer, current):
        current[...] = (numer[0] / weight_ref[0]).astype(BF16)

    _, n, kv = biased.shape
    return call("rounded_rows", kernel, [((n, kv), BF16)], (weight, biased), [SMEM, VMEM], moved=n * kv * 6)[0]


def pack(tokens, ny, nz):
    rows, width = tokens.shape
    steps = 4
    zs = nz // steps
    cols = width // ny // steps
    part = width // ny // nz

    def kernel(*refs):
        out = refs[-1]
        for p in range(zs):
            for y in range(ny):
                out[p, :, y * part : (y + 1) * part] = refs[y][:, p * part : (p + 1) * part]

    return pl.pallas_call(
        kernel,
        grid=(steps,),
        in_specs=[pl.BlockSpec((rows, cols), lambda g, y=y: (0, y * steps + g)) for y in range(ny)],
        out_specs=pl.BlockSpec((zs, rows, ny * part), lambda g: (g, 0, 0)),
        out_shape=jax.ShapeDtypeStruct((nz, rows, ny * part), BF16),
        compiler_params=pltpu.CompilerParams(vmem_limit_bytes=60 << 20),
        cost_estimate=pl.CostEstimate(flops=0, bytes_accessed=4 * rows * width, transcendentals=0),
        name="pack",
    )(*[tokens] * ny)


def join(first, second):
    n, kv = first.shape

    def kernel(first_ref, second_ref, out):
        out[:n] = first_ref[...]
        out[n:] = second_ref[...]

    return call("join", kernel, [((2 * n, kv), BF16)], (first, second), [VMEM] * 2, flops=WAIT)[0]


def columns(place_ref, dy, dc, feats):
    y = 1 - place_ref[0] if dy else place_ref[0]
    c = 1 - place_ref[1] if dc else place_ref[1]
    return pl.ds(pl.multiple_of((y * 2 + c) * feats, feats), feats)


def out_part(x, near, far, place):
    nz, n, _ = x.shape
    depth, kv = near.shape

    def kernel(place_ref, x_ref, near_ref, far_ref, out):
        y = place_ref[0]
        own = pl.ds(pl.multiple_of(y * depth, depth), depth)
        other = pl.ds(pl.multiple_of((1 - y) * depth, depth), depth)
        for z in range(0, nz, 2):
            total = jnp.zeros((2 * n, kv), F32)
            for cols, w_ref in ((own, near_ref), (other, far_ref)):
                block = jnp.concatenate([x_ref[z, :, cols], x_ref[z + 1, :, cols]], axis=0)
                total += jnp.dot(block, w_ref[...], preferred_element_type=F32)
            out[z] = total[:n].astype(BF16)
            out[z + 1] = total[n:].astype(BF16)

    return call(
        "out_part",
        kernel,
        [((nz, n, kv), BF16)],
        (place, x, near, far),
        [SMEM] + [VMEM] * 3,
        flops=WAIT,
        moved=4 << 20,
    )[0]


def grad_block(place_ref, x_ref, c_refs, turns, dy, dc, feats):
    cols = columns(place_ref, dy, dc, feats)
    nz = x_ref.shape[0]
    total = jnp.zeros((feats, c_refs[0].shape[-1]), F32)
    for c_ref, group in zip(c_refs, turns):
        blocks = [x_ref[lax.rem(place_ref[2] - t + nz, nz), :, cols] for t in group]
        block = blocks[0] if len(blocks) == 1 else jnp.concatenate(blocks, axis=0)
        total += lax.dot_general(block, c_ref[...], TURN, preferred_element_type=F32)
    return total


def grad_sent(x, cots, turns, place, feats):
    kv = cots[0].shape[1]

    def kernel(place_ref, x_ref, *refs):
        for dy in (0, 1):
            refs[-1][dy] = grad_block(place_ref, x_ref, refs[:-1], turns, dy, 1, feats).astype(BF16)

    return call(
        "grad_sent",
        kernel,
        [((2, feats, kv), BF16)],
        (place, x, *cots),
        [SMEM, VMEM] + [VMEM] * len(cots),
        flops=2 * WAIT,
        moved=3 << 20,
    )[0]


def grad_kept(x, cots, turns, place, feats):
    kv = cots[0].shape[1]

    def kernel(place_ref, x_ref, *refs):
        for dy in (0, 1):
            refs[-1][dy] = grad_block(place_ref, x_ref, refs[:-1], turns, dy, 0, feats)

    return call(
        "grad_kept",
        kernel,
        [((2, feats, kv), F32)],
        (place, x, *cots),
        [SMEM, VMEM] + [VMEM] * len(cots),
        flops=4 * x.shape[0] * x.shape[1] * feats * kv,
        moved=3 << 20,
    )[0]


def grad_far(kept, given):
    def kernel(kept_ref, given_ref, out):
        out[...] = (kept_ref[1] + given_ref[1].astype(F32)).astype(BF16)

    return call("grad_far", kernel, [(kept.shape[1:], BF16)], (kept, given), [VMEM] * 2, flops=kept.size)[0]


def step(kept, given, got, biased, momentum, weight, rep_tokens):
    size, kv = got.shape

    def kernel(w_ref, kept_ref, given_ref, got_ref, numer, moment, velocity, stepped, pushed):
        g = kept_ref[0] + given_ref[0].astype(F32) + got_ref[...].astype(F32)
        g = g * (1.0 / rep_tokens)
        v = MOMENT * moment[0] + g
        velocity[0] = v
        s = numer[0] - LEARN * (g + MOMENT * v)
        stepped[...] = s
        pushed[:size] = s.astype(BF16)
        whole = jnp.full((TAIL, kv), w_ref[0], F32)
        high = whole.astype(BF16).astype(F32)
        middle = (whole - high).astype(BF16).astype(F32)
        low = whole - high - middle
        row = lax.broadcasted_iota(jnp.int32, (TAIL, kv), 0)
        pushed[size:] = jnp.where(row == 0, high, jnp.where(row == 1, middle, low)).astype(BF16)

    return call(
        "step",
        kernel,
        [((1, size, kv), F32), ((size, kv), F32), ((size + TAIL, kv), BF16)],
        (weight, kept, given, got, biased, momentum),
        [SMEM] + [VMEM] * 5,
        flops=8 * size * kv,
        moved=24 * size * kv,
    )


def mix(stepped, arrived, weight, after):
    size, kv = stepped.shape

    def kernel(w_ref, _, s, a, weight_out, mixed_out, debiased_out):
        parts = a[size:].astype(F32)
        w = 0.5 * (w_ref[0] + (parts[0:1] + parts[1:2] + parts[2:3]))
        weight_out[0] = w[0, 0]
        mixed = 0.5 * (s[...] + a[:size].astype(F32))
        mixed_out[0] = mixed
        debiased_out[0] = mixed / w

    full = jax.ShapeDtypeStruct((1, size, kv), F32)
    return pl.pallas_call(
        kernel,
        in_specs=[SMEM, ANY] + [VMEM] * 2,
        out_specs=[SMEM] + [VMEM] * 2,
        out_shape=[jax.ShapeDtypeStruct((1,), F32)] + [full] * 2,
        compiler_params=pltpu.CompilerParams(vmem_limit_bytes=12 << 20),
        cost_estimate=pl.CostEstimate(flops=6 * size * kv, bytes_accessed=22 * size * kv, transcendentals=0),
        name="mix",
    )(weight, after, stepped, arrived)


def sum_parts(parts):
    nz, rows, kv = parts.shape

    def kernel(parts_ref, out):
        total = parts_ref[0].astype(F32)
        for z in range(1, nz):
            total += parts_ref[z].astype(F32)
        out[...] = total.astype(BF16)

    return call("sum_parts", kernel, [((rows, kv), BF16)], (parts,), [VMEM], flops=parts.size, moved=2 * parts.size)[0]


def push_round(dist, tokens, cotangent, biased, momentum, weight):
    ny, nz, nc = (lax.axis_size(a) for a in SHARD)
    rows, width = tokens.shape
    feats = width // (ny * nz * nc)
    rep_tokens = rows * ny * nz * nc
    swap = ((0, 1), (1, 0))
    n_rep = lax.axis_size("replica")
    ahead = [((i - dist) % n_rep, i) for i in range(n_rep)]
    place = jnp.stack([lax.axis_index(a) for a in ("yh", "core", "z")]).astype(jnp.int32)

    def along(block, turn):
        return lax.ppermute(block, "z", [(i, (i + turn) % nz) for i in range(nz)])

    pair = join(cotangent, along(cotangent, 4))
    x = lax.all_to_all(pack(tokens, ny, nz), "z", 0, 0, tiled=True)
    cots = [pair, along(cotangent, 2), along(cotangent, -2), along(pair, 1), along(pair, -1)]
    turns = [(0, 4), (2,), (6,), (1, 5), (7, 3)]

    near = lax.all_gather(rounded_rows(biased, weight), "core", axis=0, tiled=True)
    far = lax.ppermute(near, "yh", swap)
    part = out_part(x, near, far, place)
    parts = lax.all_to_all(part, "z", 0, 0, tiled=True)

    given = lax.ppermute(grad_sent(x, cots, turns, place, feats), "core", swap)
    kept = grad_kept(x, cots, turns, place, feats)
    got = lax.ppermute(grad_far(kept, given), "yh", swap)
    output = sum_parts(parts)

    velocity, stepped, pushed = step(kept, given, got, biased, momentum, weight, rep_tokens)
    arrived = lax.ppermute(pushed, "replica", ahead)
    weight_out, mixed, debiased = mix(stepped, arrived, weight, output)
    return output, mixed, weight_out, velocity, debiased


def shards(tokens, cotangent, biased, momentum, weight, round_index):
    hops = lax.axis_size("replica").bit_length() - 1
    power = round_index[0] % hops
    branches = [partial(push_round, 1 << level) for level in range(hops)]
    return lax.switch(power, branches, tokens, cotangent, biased, momentum, weight)


def solution(mesh):
    n_rep, n_shard = mesh.devices.shape
    inner = Mesh(mesh.devices.reshape(n_rep, 2, n_shard // 4, 2), ("replica",) + SHARD)
    rows = P(("replica",) + SHARD, None)
    held = P("replica", SHARD, None)
    return jax.shard_map(
        shards,
        mesh=inner,
        in_specs=(rows, rows, held, held, P("replica"), P()),
        out_specs=(rows, held, P("replica"), held, held),
        check_vma=False,
    )
```

time: 306 us -> 129 us (0.42)
  waiting for transfers between devices: 243 us -> 48.3 us
  starting transfers between devices: 24.1 us -> 57.1 us
  between operations: 17.2 us -> 1.48 us
  Pallas kernels: 0 us -> 15.3 us
  matrix products: 10.9 us -> 0 us
  local copies, waits for them, and re-layouts: 7.76 us -> 2.55 us
  blocking collectives: 0 us -> 3.32 us
    all_gather x2 -> x0, waiting for transfers between devices: 179 us -> none  [the longest x1 108 us: shards(): full_rows = lax.all_gather(current, 'shard', axis=0, tiled=True)]
    ppermute x2 -> x9, starting transfers between devices: 6.79 us -> 49.8 us  [the longest x5 25.6 us: along(): return lax.ppermute(block, 'z', [(i, (i + turn) % nz) for i in range(nz)])]
    all_to_all x1 -> x2, waiting for transfers between devices: 53.3 us -> 22.9 us  [the longest x1 22.9 us: push_round(): x = lax.all_to_all(pack(tokens, ny, nz), 'z', 0, 0, tiled=True)]
    ppermute x2 -> x9, waiting for transfers between devices: 9.96 us -> 25.4 us  [the longest x1 9.19 us: push_round(): arrived = lax.ppermute(pushed, 'replica', ahead)]
    pallas_call x0 -> x10, Pallas kernels: none -> 15.3 us  [the longest x8 9.75 us: call(): pl.pallas_call(kernel, in_specs=specs, out_specs=[VMEM] * len(outs), out_...]
    dot_general x2 -> x0, matrix products: 10.9 us -> none  [the longest x1 5.76 us: shards(): output = jnp.dot(tokens, full_rows, preferred_element_type=jnp.float32)]
    all_to_all x1 -> x2, starting transfers between devices: 17.2 us -> 7.29 us  [the longest x1 3.73 us: push_round(): x = lax.all_to_all(pack(tokens, ny, nz), 'z', 0, 0, tiled=True)]
    unnamed x6 -> x0, local copies, waits for them, and re-layouts: 4.86 us -> none
  transfers between devices with their start and end apart: 5 -> 11, of which waited for: 4 -> 4; matrix products, arithmetic and copies ran while one was open for 3% -> 0% of each run, Pallas kernels for 0% -> 11%
where the time goes in v2:
time: 129 us
  starting transfers between devices  57.1 us (44%)
  waiting for transfers between devices  48.3 us (37%)
  Pallas kernels  15.3 us (12%)
  blocking collectives  3.32 us (3%)
  local copies, waits for them, and re-layouts  2.55 us (2%)
  between operations  1.48 us (1%)
    ppermute x5, starting transfers between devices, along(): return lax.ppermute(block, 'z', [(i, (i + turn) % nz) for i in range(nz)])  25.6 us
    all_to_all x1, waiting for transfers between devices, push_round(): x = lax.all_to_all(pack(tokens, ny, nz), 'z', 0, 0, tiled=True)  22.9 us
    pallas_call x8, Pallas kernels, call(): pl.pallas_call(kernel, in_specs=specs, out_specs=[VMEM] * len(outs), out_...  9.75 us
    ppermute x1, waiting for transfers between devices, push_round(): arrived = lax.ppermute(pushed, 'replica', ahead)  9.19 us
    ppermute x1, waiting for transfers between devices, push_round(): got = lax.ppermute(grad_far(kept, given), 'yh', swap)  8.21 us
    ppermute x1, waiting for transfers between devices, push_round(): far = lax.ppermute(near, 'yh', swap)  7.99 us
    ppermute x1, starting transfers between devices, push_round(): far = lax.ppermute(near, 'yh', swap)  7.44 us
    ppermute x1, starting transfers between devices, push_round(): got = lax.ppermute(grad_far(kept, given), 'yh', swap)  7.41 us
  transfers between devices with their start and end apart: 11, of which 4 were waited for; matrix products, arithmetic and copies ran while one was open for 0% of the time, Pallas kernels for 11%

profile of v2, /device:TPU:1, one launch (start us, length us, event | category | flops | bytes accessed | tf_op | source)
XLA Modules:
  0.0 128.5 jit_solution(2484568652320778456)
XLA Ops:
  1.3 127.0 %conditional.1 = (f32[1,256,512]{2,1,0:T(8,128)}, f32[1]{0:T(128)}, f32[1,256,512]{2,1,0:T(8,128)}, f32[1,256,512]{2,1,0:T(8,128)}, bf16[128,512]{1,0:T(8,128)(2,1)}) conditional(s32[]{:T(128)} %clamp.3, (bf16[128,8192]{1,0:T(8,128)(2,1)}, f32[1]{0:T(128)}, f32[1,256,512]{2,1,0:T(8,128)}, bf16[128,512]{1,0:T(8,128)(2,1)}, ...), branch_computations={%region_0.1_spmd, %region_1.2_spmd, %region_2.3_spmd, %region_3.4_... | conditional | flops 200539488256 | bytes 54330084 | solution.py:267
  1.3 11.5 %collective-permute-start.1 = (bf16[128,512]{1,0:T(8,128)(2,1)}, bf16[128,512]{1,0:T(8,128)(2,1)S(1)}, u32[]{:S(2)}, u32[]{:S(2)}) collective-permute-start(bf16[128,512]{1,0:T(8,128)(2,1)} %get-tuple-element.43.first_ref), channel_id=1, source_target_pairs={{0,8},{2,10},{4,12},{6,14},{8,0},{10,2},{12,4},{14,6},{1,9},{3,11}... | collective-permute-start | bytes 393224 | tf_op jit(solution)/shard_map/cond/branch_0_fun/ppermute | solution.py:240
  12.8 4.0 %collective-permute-start.2 = (bf16[128,512]{1,0:T(8,128)(2,1)}, bf16[128,512]{1,0:T(8,128)(2,1)S(1)}, u32[]{:S(2)}, u32[]{:S(2)}) collective-permute-start(bf16[128,512]{1,0:T(8,128)(2,1)} %get-tuple-element.43.first_ref), channel_id=1, source_target_pairs={{0,4},{2,6},{4,8},{6,10},{8,12},{10,14},{12,0},{14,2},{1,5},{3,7},... | collective-permute-start | bytes 393224 | tf_op jit(solution)/shard_map/cond/branch_0_fun/ppermute | solution.py:240
  16.8 3.4 %collective-permute-start.3 = (bf16[128,512]{1,0:T(8,128)(2,1)}, bf16[128,512]{1,0:T(8,128)(2,1)}, u32[]{:S(2)}, u32[]{:S(2)}) collective-permute-start(bf16[128,512]{1,0:T(8,128)(2,1)} %get-tuple-element.43.first_ref), channel_id=1, source_target_pairs={{0,12},{2,14},{4,0},{6,2},{8,4},{10,6},{12,8},{14,10},{1,13},{3,15... | collective-permute-start | bytes 393224 | tf_op jit(solution)/shard_map/cond/branch_0_fun/ppermute | solution.py:240
  20.2 3.8 %pack.4 = bf16[8,128,1024]{2,1,0:T(8,128)(2,1)} custom-call(bf16[128,8192]{1,0:T(8,128)(2,1)} %get-tuple-element.40.refs_0_.refs_1_, bf16[128,8192]{1,0:T(8,128)(2,1)} %get-tuple-element.40.refs_0_.refs_1_), custom_call_target="tpu_custom_call" | custom-call | bytes 4194304 | tf_op jit(solution)/shard_map/cond/branch_0_fun/pack/pallas_call | solution.py:56
  24.0 3.7 %all-to-all-start = ((bf16[8,128,1024]{2,1,0:T(8,128)(2,1)}), bf16[8,128,1024]{2,1,0:T(8,128)(2,1)S(1)}, u32[]{:S(2)}, u32[]{:S(2)}) async-start(bf16[8,128,1024]{2,1,0:T(8,128)(2,1)} %pack.4), calls=%async_computation | async-start | bytes 4194304 | tf_op jit(solution)/shard_map/cond/branch_0_fun/all_to_all | solution.py:243
  28.4 3.3 %all_gather.8.near_ref = bf16[512,512]{1,0:T(8,128)(2,1)S(1)} all-gather(bf16[256,512]{1,0:T(8,128)(2,1)S(1)} %rounded_rows.4), channel_id=1, replica_groups=mesh['replica'=16,'yh'=2,'z'=8,'core'=2] {'core'}, dimensions={0}, use_global_device_ids=true | all-gather | bytes 786432 | tf_op jit(solution)/shard_map/cond/branch_0_fun/all_gather | solution.py:247
  31.7 7.4 %collective-permute-start = (bf16[512,512]{1,0:T(8,128)(2,1)S(1)}, bf16[512,512]{1,0:T(8,128)(2,1)S(1)}, u32[]{:S(2)}, u32[]{:S(2)}) collective-permute-start(bf16[512,512]{1,0:T(8,128)(2,1)S(1)} %all_gather.8.near_ref), channel_id=1, source_target_pairs={{0,16},{16,0},{1,17},{17,1},{2,18},{18,2},{3,19},{19,3},{4,20},{20... | collective-permute-start | bytes 1572872 | tf_op jit(solution)/shard_map/cond/branch_0_fun/ppermute | solution.py:248
  41.8 3.5 %collective-permute-start.4 = (bf16[256,512]{1,0:T(8,128)(2,1)S(1)}, bf16[256,512]{1,0:T(8,128)(2,1)}, u32[]{:S(2)}, u32[]{:S(2)}) collective-permute-start(bf16[256,512]{1,0:T(8,128)(2,1)S(1)} %join.4.refs_0_), channel_id=1, source_target_pairs={{0,2},{2,4},{4,6},{6,8},{8,10},{10,12},{12,14},{14,0},{1,3},{3,5},... | collective-permute-start | bytes 786440 | tf_op jit(solution)/shard_map/cond/branch_0_fun/ppermute | solution.py:240
  45.3 3.2 %collective-permute-start.5 = (bf16[256,512]{1,0:T(8,128)(2,1)S(1)}, bf16[256,512]{1,0:T(8,128)(2,1)}, u32[]{:S(2)}, u32[]{:S(2)}) collective-permute-start(bf16[256,512]{1,0:T(8,128)(2,1)S(1)} %join.4.refs_0_), channel_id=1, source_target_pairs={{0,14},{2,0},{4,2},{6,4},{8,6},{10,8},{12,10},{14,12},{1,15},{3,1}... | collective-permute-start | bytes 786440 | tf_op jit(solution)/shard_map/cond/branch_0_fun/ppermute | solution.py:240
  48.5 8.0 %collective-permute-done.far_ref = bf16[512,512]{1,0:T(8,128)(2,1)S(1)} collective-permute-done((bf16[512,512]{1,0:T(8,128)(2,1)S(1)}, bf16[512,512]{1,0:T(8,128)(2,1)S(1)}, u32[]{:S(2)}, u32[]{:S(2)}) %collective-permute-start) | collective-permute-done | bytes 524320 | tf_op jit(solution)/shard_map/cond/branch_0_fun/ppermute | solution.py:248
  56.5 22.9 %all-to-all-done.x_ref = bf16[8,128,1024]{2,1,0:T(8,128)(2,1)S(1)} async-done(((bf16[8,128,1024]{2,1,0:T(8,128)(2,1)}), bf16[8,128,1024]{2,1,0:T(8,128)(2,1)S(1)}, u32[]{:S(2)}, u32[]{:S(2)}) %all-to-all-start) | async-done | bytes 2097184 | tf_op jit(solution)/shard_map/cond/branch_0_fun/all_to_all | solution.py:243
  79.3 1.8 %out_part.4 = bf16[8,128,512]{2,1,0:T(8,128)(2,1)S(1)} custom-call(s32[3]{0:T(128)S(1)} %pad_add_fusion.place_ref, bf16[8,128,1024]{2,1,0:T(8,128)(2,1)S(1)} %all-to-all-done.x_ref, bf16[512,512]{1,0:T(8,128)(2,1)S(1)} %all_gather.8.near_ref, bf16[512,512]{1,0:T(8,128)(2,1)S(1)} %collective-permute-done.far_ref), custom_call_target="tpu_custom_call" | custom-call | flops 49999998976 | bytes 4194304 | tf_op jit(solution)/shard_map/cond/branch_0_fun/out_part/pallas_call | solution.py:23
  81.1 1.0 copy-done
  82.1 3.6 %all-to-all-start.1 = ((bf16[8,128,512]{2,1,0:T(8,128)(2,1)}), bf16[8,128,512]{2,1,0:T(8,128)(2,1)S(1)}, u32[]{:S(2)}, u32[]{:S(2)}) async-start(bf16[8,128,512]{2,1,0:T(8,128)(2,1)} %copy-done), calls=%async_computation.1 | async-start | bytes 2097152 | tf_op jit(solution)/shard_map/cond/branch_0_fun/all_to_all | solution.py:250
  85.7 2.0 %grad_sent.4 = bf16[2,256,512]{2,1,0:T(8,128)(2,1)S(1)} custom-call(s32[3]{0:T(128)S(1)} %pad_add_fusion.place_ref, bf16[8,128,1024]{2,1,0:T(8,128)(2,1)S(1)} %all-to-all-done.x_ref, bf16[256,512]{1,0:T(8,128)(2,1)S(1)} %join.4.refs_0_, bf16[128,512]{1,0:T(8,128)(2,1)S(1)} %collective-permute-done.2.refs_1_, ...), custom_call_target="tpu_custom_call" | custom-call | flops 99999997952 | bytes 3145728 | tf_op jit(solution)/shard_map/cond/branch_0_fun/grad_sent/pallas_call | solution.py:23
  87.7 2.9 %collective-permute-start.6 = (bf16[2,256,512]{2,1,0:T(8,128)(2,1)S(1)}, bf16[2,256,512]{2,1,0:T(8,128)(2,1)S(1)}, u32[]{:S(2)}, u32[]{:S(2)}) collective-permute-start(bf16[2,256,512]{2,1,0:T(8,128)(2,1)S(1)} %grad_sent.4), channel_id=1, source_target_pairs={{0,1},{1,0},{2,3},{3,2},{4,5},{5,4},{6,7},{7,6},{8,9},{9,8},{10,11... | collective-permute-start | bytes 1572872 | tf_op jit(solution)/shard_map/cond/branch_0_fun/ppermute | solution.py:252
  90.6 2.0 %grad_kept.4.kept_ref = f32[2,256,512]{2,1,0:T(8,128)S(1)} custom-call(s32[3]{0:T(128)S(1)} %pad_add_fusion.place_ref, bf16[8,128,1024]{2,1,0:T(8,128)(2,1)S(1)} %all-to-all-done.x_ref, bf16[256,512]{1,0:T(8,128)(2,1)S(1)} %join.4.refs_0_, bf16[128,512]{1,0:T(8,128)(2,1)S(1)} %collective-permute-done.2.refs_1_, ...), custom_call_target="tpu_custom_call" | custom-call | flops 536870912 | bytes 3145728 | tf_op jit(solution)/shard_map/cond/branch_0_fun/grad_kept/pallas_call | solution.py:23
  92.7 7.4 %collective-permute-start.7 = (bf16[256,512]{1,0:T(8,128)(2,1)S(1)}, bf16[256,512]{1,0:T(8,128)(2,1)S(1)}, u32[]{:S(2)}, u32[]{:S(2)}) collective-permute-start(bf16[256,512]{1,0:T(8,128)(2,1)S(1)} %grad_far.4), channel_id=1, source_target_pairs={{0,16},{16,0},{1,17},{17,1},{2,18},{18,2},{3,19},{19,3},{4,20},{20... | collective-permute-start | bytes 786440 | tf_op jit(solution)/shard_map/cond/branch_0_fun/ppermute | solution.py:254
  100.1 8.2 %collective-permute-done.7.got_ref = bf16[256,512]{1,0:T(8,128)(2,1)S(1)} collective-permute-done((bf16[256,512]{1,0:T(8,128)(2,1)S(1)}, bf16[256,512]{1,0:T(8,128)(2,1)S(1)}, u32[]{:S(2)}, u32[]{:S(2)}) %collective-permute-start.7) | collective-permute-done | bytes 262176 | tf_op jit(solution)/shard_map/cond/branch_0_fun/ppermute | solution.py:254
  108.3 1.6 %step.4 = (f32[1,256,512]{2,1,0:T(8,128)}, f32[256,512]{1,0:T(8,128)S(1)}, bf16[272,512]{1,0:T(8,128)(2,1)S(1)}) custom-call(f32[1]{0:T(128)} %get-tuple-element.41.weight_ref.w_ref, f32[2,256,512]{2,1,0:T(8,128)S(1)} %grad_kept.4.kept_ref, bf16[2,256,512]{2,1,0:T(8,128)(2,1)S(1)} %collective-permute-done.6.given_ref, ...), custom_call_target="tpu_custom_call" | custom-call | flops 1048576 | bytes 3145728 | tf_op jit(solution)/shard_map/cond/branch_0_fun/step/pallas_call | solution.py:23
  109.9 6.5 %collective-permute-start.8 = (bf16[272,512]{1,0:T(8,128)(2,1)S(1)}, bf16[272,512]{1,0:T(8,128)(2,1)S(1)}, u32[]{:S(2)}, u32[]{:S(2)}) collective-permute-start(bf16[272,512]{1,0:T(8,128)(2,1)S(1)} %get-tuple-element.46), channel_id=1, source_target_pairs={{480,0},{0,32},{32,64},{64,96},{96,128},{128,160},{160,192},{192,2... | collective-permute-start | bytes 835592 | tf_op jit(solution)/shard_map/cond/branch_0_fun/ppermute | solution.py:258
  117.2 9.2 %collective-permute-done.8.a = bf16[272,512]{1,0:T(8,128)(2,1)S(1)} collective-permute-done((bf16[272,512]{1,0:T(8,128)(2,1)S(1)}, bf16[272,512]{1,0:T(8,128)(2,1)S(1)}, u32[]{:S(2)}, u32[]{:S(2)}) %collective-permute-start.8) | collective-permute-done | bytes 278560 | tf_op jit(solution)/shard_map/cond/branch_0_fun/ppermute | solution.py:258
  126.4 1.7 %mix.4 = (f32[1]{0:T(128)}, f32[1,256,512]{2,1,0:T(8,128)}, f32[1,256,512]{2,1,0:T(8,128)}) custom-call(f32[1]{0:T(128)} %get-tuple-element.41.weight_ref.w_ref, bf16[128,512]{1,0:T(8,128)(2,1)} %sum_parts.4._, f32[256,512]{1,0:T(8,128)S(1)} %get-tuple-element.45.s, bf16[272,512]{1,0:T(8,128)(2,1)S(1)} %collective-permute-done.8.a), custom_call_target="tpu_custom_call" | custom-call | flops 786432 | bytes 2883584 | tf_op jit(solution)/shard_map/cond/branch_0_fun/mix/pallas_call | solution.py:206
  (23 shorter events, 4.1 us)
Async XLA Ops:
  1.3 38.0 %collective-permute-start.1 = (bf16[128,512]{1,0:T(8,128)(2,1)}, bf16[128,512]{1,0:T(8,128)(2,1)S(1)}, u32[]{:S(2)}, u32[]{:S(2)}) collective-permute-start(bf16[128,512]{1,0:T(8,128)(2,1)} %get-tuple-element.43.first_ref), channel_id=1, source_target_pairs={{0,8},{2,10},{4,12},{6,14},{8,0},{10,2},{12,4},{14,6},{1,9},{3,11}... | collective-permute-start | bytes 393224 | tf_op jit(solution)/shard_map/cond/branch_0_fun/ppermute | solution.py:240
  12.8 72.9 %collective-permute-start.2 = (bf16[128,512]{1,0:T(8,128)(2,1)}, bf16[128,512]{1,0:T(8,128)(2,1)S(1)}, u32[]{:S(2)}, u32[]{:S(2)}) collective-permute-start(bf16[128,512]{1,0:T(8,128)(2,1)} %get-tuple-element.43.first_ref), channel_id=1, source_target_pairs={{0,4},{2,6},{4,8},{6,10},{8,12},{10,14},{12,0},{14,2},{1,5},{3,7},... | collective-permute-start | bytes 393224 | tf_op jit(solution)/shard_map/cond/branch_0_fun/ppermute | solution.py:240
  16.8 68.9 %collective-permute-start.3 = (bf16[128,512]{1,0:T(8,128)(2,1)}, bf16[128,512]{1,0:T(8,128)(2,1)}, u32[]{:S(2)}, u32[]{:S(2)}) collective-permute-start(bf16[128,512]{1,0:T(8,128)(2,1)} %get-tuple-element.43.first_ref), channel_id=1, source_target_pairs={{0,12},{2,14},{4,0},{6,2},{8,4},{10,6},{12,8},{14,10},{1,13},{3,15... | collective-permute-start | bytes 393224 | tf_op jit(solution)/shard_map/cond/branch_0_fun/ppermute | solution.py:240
  24.0 3.7 %copy-start.12 = (f32[1,256,512]{2,1,0:T(8,128)S(1)}, f32[1,256,512]{2,1,0:T(8,128)}, u32[]{:S(2)}) copy-start(f32[1,256,512]{2,1,0:T(8,128)} %get-tuple-element.42.numer) | copy-start | bytes 1572868 | tf_op jit(solution)/shard_map/cond
  24.0 55.4 %all-to-all-start = ((bf16[8,128,1024]{2,1,0:T(8,128)(2,1)}), bf16[8,128,1024]{2,1,0:T(8,128)(2,1)S(1)}, u32[]{:S(2)}, u32[]{:S(2)}) async-start(bf16[8,128,1024]{2,1,0:T(8,128)(2,1)} %pack.4), calls=%async_computation | async-start | bytes 4194304 | tf_op jit(solution)/shard_map/cond/branch_0_fun/all_to_all | solution.py:243
  31.7 24.7 %collective-permute-start = (bf16[512,512]{1,0:T(8,128)(2,1)S(1)}, bf16[512,512]{1,0:T(8,128)(2,1)S(1)}, u32[]{:S(2)}, u32[]{:S(2)}) collective-permute-start(bf16[512,512]{1,0:T(8,128)(2,1)S(1)} %all_gather.8.near_ref), channel_id=1, source_target_pairs={{0,16},{16,0},{1,17},{17,1},{2,18},{18,2},{3,19},{19,3},{4,20},{20... | collective-permute-start | bytes 1572872 | tf_op jit(solution)/shard_map/cond/branch_0_fun/ppermute | solution.py:248
  39.3 0.7 copy-start.4
  39.9 0.9 copy-start.5
  41.8 43.9 %collective-permute-start.4 = (bf16[256,512]{1,0:T(8,128)(2,1)S(1)}, bf16[256,512]{1,0:T(8,128)(2,1)}, u32[]{:S(2)}, u32[]{:S(2)}) collective-permute-start(bf16[256,512]{1,0:T(8,128)(2,1)S(1)} %join.4.refs_0_), channel_id=1, source_target_pairs={{0,2},{2,4},{4,6},{6,8},{8,10},{10,12},{12,14},{14,0},{1,3},{3,5},... | collective-permute-start | bytes 786440 | tf_op jit(solution)/shard_map/cond/branch_0_fun/ppermute | solution.py:240
  45.3 40.4 %collective-permute-start.5 = (bf16[256,512]{1,0:T(8,128)(2,1)S(1)}, bf16[256,512]{1,0:T(8,128)(2,1)}, u32[]{:S(2)}, u32[]{:S(2)}) collective-permute-start(bf16[256,512]{1,0:T(8,128)(2,1)S(1)} %join.4.refs_0_), channel_id=1, source_target_pairs={{0,14},{2,0},{4,2},{6,4},{8,6},{10,8},{12,10},{14,12},{1,15},{3,1}... | collective-permute-start | bytes 786440 | tf_op jit(solution)/shard_map/cond/branch_0_fun/ppermute | solution.py:240
  81.1 1.0 copy-start
  82.1 34.3 %all-to-all-start.1 = ((bf16[8,128,512]{2,1,0:T(8,128)(2,1)}), bf16[8,128,512]{2,1,0:T(8,128)(2,1)S(1)}, u32[]{:S(2)}, u32[]{:S(2)}) async-start(bf16[8,128,512]{2,1,0:T(8,128)(2,1)} %copy-done), calls=%async_computation.1 | async-start | bytes 2097152 | tf_op jit(solution)/shard_map/cond/branch_0_fun/all_to_all | solution.py:250
  87.7 20.6 %copy-start.13 = (f32[1,256,512]{2,1,0:T(8,128)S(1)}, f32[1,256,512]{2,1,0:T(8,128)}, u32[]{:S(2)}) copy-start(f32[1,256,512]{2,1,0:T(8,128)} %get-tuple-element.42.numer) | copy-start | bytes 1572868 | tf_op jit(solution)/shard_map/cond
  87.7 20.6 %copy-start.20 = (f32[1,256,512]{2,1,0:T(8,128)S(1)}, f32[1,256,512]{2,1,0:T(8,128)}, u32[]{:S(2)}) copy-start(f32[1,256,512]{2,1,0:T(8,128)} %get-tuple-element.44.moment) | copy-start | bytes 1572868 | tf_op jit(solution)/shard_map/cond
  87.7 4.9 %collective-permute-start.6 = (bf16[2,256,512]{2,1,0:T(8,128)(2,1)S(1)}, bf16[2,256,512]{2,1,0:T(8,128)(2,1)S(1)}, u32[]{:S(2)}, u32[]{:S(2)}) collective-permute-start(bf16[2,256,512]{2,1,0:T(8,128)(2,1)S(1)} %grad_sent.4), channel_id=1, source_target_pairs={{0,1},{1,0},{2,3},{3,2},{4,5},{5,4},{6,7},{7,6},{8,9},{9,8},{10,11... | collective-permute-start | bytes 1572872 | tf_op jit(solution)/shard_map/cond/branch_0_fun/ppermute | solution.py:252
  92.7 15.6 %collective-permute-start.7 = (bf16[256,512]{1,0:T(8,128)(2,1)S(1)}, bf16[256,512]{1,0:T(8,128)(2,1)S(1)}, u32[]{:S(2)}, u32[]{:S(2)}) collective-permute-start(bf16[256,512]{1,0:T(8,128)(2,1)S(1)} %grad_far.4), channel_id=1, source_target_pairs={{0,16},{16,0},{1,17},{17,1},{2,18},{18,2},{3,19},{19,3},{4,20},{20... | collective-permute-start | bytes 786440 | tf_op jit(solution)/shard_map/cond/branch_0_fun/ppermute | solution.py:254
  109.9 16.5 %collective-permute-start.8 = (bf16[272,512]{1,0:T(8,128)(2,1)S(1)}, bf16[272,512]{1,0:T(8,128)(2,1)S(1)}, u32[]{:S(2)}, u32[]{:S(2)}) collective-permute-start(bf16[272,512]{1,0:T(8,128)(2,1)S(1)} %get-tuple-element.46), channel_id=1, source_target_pairs={{480,0},{0,32},{32,64},{64,96},{96,128},{128,160},{160,192},{192,2... | collective-permute-start | bytes 835592 | tf_op jit(solution)/shard_map/cond/branch_0_fun/ppermute | solution.py:258

commit v3 on v2

v3 whole, which is shorter than its diff:
```python
from functools import partial

import jax
import jax.numpy as jnp
from jax import lax
from jax.experimental import pallas as pl
from jax.experimental.pallas import tpu as pltpu
from jax.sharding import Mesh, PartitionSpec as P

MOMENT = 0.9
LEARN = 0.5
SHARD = ("yh", "z", "core")
F32, BF16 = jnp.float32, jnp.bfloat16
VMEM = pl.BlockSpec(memory_space=pltpu.VMEM)
SMEM = pl.BlockSpec(memory_space=pltpu.SMEM)
ANY = pl.BlockSpec(memory_space=pl.ANY)
TURN = (((0,), (0,)), ((), ()))
TAIL = 16
WAIT = 50_000_000_000


def call(name, kernel, outs, ins, specs, flops=0, moved=0, **kw):
    return pl.pallas_call(
        kernel,
        in_specs=specs,
        out_specs=[VMEM] * len(outs),
        out_shape=[jax.ShapeDtypeStruct(s, t) for s, t in outs],
        compiler_params=pltpu.CompilerParams(vmem_limit_bytes=12 << 20),
        cost_estimate=pl.CostEstimate(flops=flops, bytes_accessed=moved, transcendentals=0),
        name=name,
        **kw,
    )(*ins)


def rounded_rows(biased, weight, after):
    def kernel(weight_ref, _, numer, current):
        current[...] = (numer[0] / weight_ref[0]).astype(BF16)

    _, n, kv = biased.shape
    return call("rounded_rows", kernel, [((n, kv), BF16)], (weight, after, biased), [SMEM, ANY, VMEM])[0]


def pack(tokens, cotangent, ny, nz):
    rows, width = tokens.shape
    kv = cotangent.shape[1]
    steps = 2
    zs = nz // steps
    cols = width // ny // steps
    part = width // ny // nz

    def kernel(cot, *refs):
        out, kept = refs[-2:]
        kept[...] = cot[...]
        for p in range(zs):
            for y in range(ny):
                out[p, :, y * part : (y + 1) * part] = refs[y][:, p * part : (p + 1) * part]

    return pl.pallas_call(
        kernel,
        grid=(steps,),
        in_specs=[pl.BlockSpec((rows // steps, kv), lambda g: (g, 0))]
        + [pl.BlockSpec((rows, cols), lambda g, y=y: (0, y * steps + g)) for y in range(ny)],
        out_specs=[
            pl.BlockSpec((zs, rows, ny * part), lambda g: (g, 0, 0)),
            pl.BlockSpec((rows // steps, kv), lambda g: (g, 0)),
        ],
        out_shape=[
            jax.ShapeDtypeStruct((nz, rows, ny * part), BF16),
            jax.ShapeDtypeStruct((rows, kv), BF16),
        ],
        compiler_params=pltpu.CompilerParams(vmem_limit_bytes=60 << 20),
        cost_estimate=pl.CostEstimate(flops=0, bytes_accessed=4 * rows * width, transcendentals=0),
        name="pack",
    )(cotangent, *[tokens] * ny)


def join(first, second):
    n, kv = first.shape

    def kernel(first_ref, second_ref, out, alone):
        out[:n] = first_ref[...]
        out[n:] = second_ref[...]
        alone[...] = first_ref[...]

    outs = [((2 * n, kv), BF16), ((n, kv), BF16)]
    return call("join", kernel, outs, (first, second), [VMEM] * 2, flops=WAIT)


def columns(place_ref, dy, dc, feats):
    y = 1 - place_ref[0] if dy else place_ref[0]
    c = 1 - place_ref[1] if dc else place_ref[1]
    return pl.ds(pl.multiple_of((y * 2 + c) * feats, feats), feats)


def out_part(x, near, far, place):
    nz, n, _ = x.shape
    depth, kv = near.shape
    steps = 2
    zs = nz // steps

    def kernel(place_ref, x_ref, near_ref, far_ref, out):
        y = place_ref[0]
        own = pl.ds(pl.multiple_of(y * depth, depth), depth)
        other = pl.ds(pl.multiple_of((1 - y) * depth, depth), depth)
        base = pl.program_id(0) * zs
        for z in range(0, zs, 2):
            total = jnp.zeros((2 * n, kv), F32)
            for cols, w_ref in ((own, near_ref), (other, far_ref)):
                block = jnp.concatenate([x_ref[base + z, :, cols], x_ref[base + z + 1, :, cols]], axis=0)
                total += jnp.dot(block, w_ref[...], preferred_element_type=F32)
            out[z] = total[:n].astype(BF16)
            out[z + 1] = total[n:].astype(BF16)

    return pl.pallas_call(
        kernel,
        grid=(steps,),
        in_specs=[SMEM] + [VMEM] * 3,
        out_specs=pl.BlockSpec((zs, n, kv), lambda g: (g, 0, 0)),
        out_shape=jax.ShapeDtypeStruct((nz, n, kv), BF16),
        compiler_params=pltpu.CompilerParams(vmem_limit_bytes=12 << 20),
        cost_estimate=pl.CostEstimate(flops=WAIT, bytes_accessed=4 << 20, transcendentals=0),
        name="out_part",
    )(place, x, near, far)


def grad_block(place_ref, x_ref, c_refs, turns, dy, dc, feats):
    cols = columns(place_ref, dy, dc, feats)
    nz = x_ref.shape[0]
    total = None
    at = 0
    for group in turns:
        refs, at = c_refs[at : at + len(group)], at + len(group)
        blocks = [x_ref[lax.rem(place_ref[2] - t + nz, nz), :, cols] for pair in group for t in pair]
        cots = refs[0][...] if len(refs) == 1 else jnp.concatenate([r[...] for r in refs], axis=0)
        part = lax.dot_general(jnp.concatenate(blocks, axis=0), cots, TURN, preferred_element_type=F32)
        total = part if total is None else total + part
    return total


def grad_part(name, x, cots, turns, place, feats, which, start, out_type, hint, after):
    kv = cots[0].shape[1]
    more = [] if start is None else [start]

    def kernel(place_ref, x_ref, *refs):
        out = refs[-1]
        for i, (dy, dc) in enumerate(which):
            total = grad_block(place_ref, x_ref, refs[: len(cots)], turns, dy, dc, feats)
            if more:
                total += refs[len(cots)][dc * 2 + dy]
            out[i] = total.astype(out_type)

    return call(
        name,
        kernel,
        [((len(which), feats, kv), out_type)],
        (place, x, *cots, *more, *after),
        [SMEM, VMEM] + [VMEM] * (len(cots) + len(more)) + [ANY] * len(after),
        flops=hint,
        moved=3 << 20,
    )[0]


def grad_far(kept, given):
    def kernel(kept_ref, given_ref, out):
        out[...] = (kept_ref[1] + given_ref[1].astype(F32)).astype(BF16)

    return call("grad_far", kernel, [(kept.shape[1:], BF16)], (kept, given), [VMEM] * 2, flops=kept.size)[0]


def step(kept, given, got, biased, momentum, weight, rep_tokens):
    size, kv = got.shape

    def kernel(w_ref, kept_ref, given_ref, got_ref, numer, moment, velocity, stepped, pushed):
        g = kept_ref[0] + given_ref[0].astype(F32) + got_ref[...].astype(F32)
        g = g * (1.0 / rep_tokens)
        v = MOMENT * moment[0] + g
        velocity[0] = v
        s = numer[0] - LEARN * (g + MOMENT * v)
        stepped[...] = s
        pushed[:size] = s.astype(BF16)
        whole = jnp.full((TAIL, kv), w_ref[0], F32)
        high = whole.astype(BF16).astype(F32)
        middle = (whole - high).astype(BF16).astype(F32)
        low = whole - high - middle
        row = lax.broadcasted_iota(jnp.int32, (TAIL, kv), 0)
        pushed[size:] = jnp.where(row == 0, high, jnp.where(row == 1, middle, low)).astype(BF16)

    return call(
        "step",
        kernel,
        [((1, size, kv), F32), ((size, kv), F32), ((size + TAIL, kv), BF16)],
        (weight, kept, given, got, biased, momentum),
        [SMEM] + [VMEM] * 5,
        flops=8 * size * kv,
        moved=24 * size * kv,
    )


def mix(stepped, arrived, weight, after):
    size, kv = stepped.shape
    steps = 2

    def kernel(w_ref, _, s, a, tail, weight_out, mixed_out, debiased_out):
        parts = tail[...].astype(F32)
        w = 0.5 * (w_ref[0] + (parts[0:1] + parts[1:2] + parts[2:3]))
        weight_out[0] = w[0, 0]
        mixed = 0.5 * (s[...] + a[...].astype(F32))
        mixed_out[0] = mixed
        debiased_out[0] = mixed / w

    full = jax.ShapeDtypeStruct((1, size, kv), F32)
    piece = pl.BlockSpec((size // steps, kv), lambda g: (g, 0))
    piece_out = pl.BlockSpec((1, size // steps, kv), lambda g: (0, g, 0))
    return pl.pallas_call(
        kernel,
        grid=(steps,),
        in_specs=[SMEM, ANY, piece, piece, pl.BlockSpec((TAIL, kv), lambda g: (size // TAIL, 0))],
        out_specs=[SMEM, piece_out, piece_out],
        out_shape=[jax.ShapeDtypeStruct((1,), F32)] + [full] * 2,
        compiler_params=pltpu.CompilerParams(vmem_limit_bytes=12 << 20),
        cost_estimate=pl.CostEstimate(flops=6 * size * kv, bytes_accessed=22 * size * kv, transcendentals=0),
        name="mix",
    )(weight, after, stepped, arrived, arrived)


def sum_parts(parts):
    nz, rows, kv = parts.shape

    def kernel(parts_ref, out):
        total = parts_ref[0].astype(F32)
        for z in range(1, nz):
            total += parts_ref[z].astype(F32)
        out[...] = total.astype(BF16)

    return call("sum_parts", kernel, [((rows, kv), BF16)], (parts,), [VMEM], flops=parts.size, moved=2 * parts.size)[0]


def push_round(dist, packed, own, biased, momentum, weight):
    ny, nz, nc = (lax.axis_size(a) for a in SHARD)
    feats = biased.shape[1]
    rep_tokens = own.shape[0] * ny * nz * nc
    swap = ((0, 1), (1, 0))
    n_rep = lax.axis_size("replica")
    ahead = [((i - dist) % n_rep, i) for i in range(n_rep)]
    place = jnp.stack([lax.axis_index(a) for a in ("yh", "core", "z")]).astype(jnp.int32)

    def along(block, turn):
        return lax.ppermute(block, "z", [(i, (i + turn) % nz) for i in range(nz)])

    pair, alone = join(own, along(own, 4))
    x = lax.all_to_all(packed, "z", 0, 0, tiled=True)
    first = [pair, along(alone, 2), along(alone, -2)]
    first_turns = [((0, 4),), ((2,), (6,))]
    last = [along(pair, 1), along(pair, -1)]
    last_turns = [((1, 5),), ((7, 3),)]

    near = lax.all_gather(rounded_rows(biased, weight, alone), "core", axis=0, tiled=True)
    far = lax.ppermute(near, "yh", swap)
    part = out_part(x, near, far, place)
    parts = lax.all_to_all(part, "z", 0, 0, tiled=True)

    mine, other = ((0, 0), (1, 0)), ((0, 1), (1, 1))
    start = grad_part("grad_first", x, first, first_turns, place, feats, mine + other, None, F32, WAIT, [part])
    given = grad_part("grad_sent", x, last, last_turns, place, feats, other, start, BF16, 2 * WAIT, [])
    given = lax.ppermute(given, "core", swap)
    kept = grad_part("grad_kept", x, last, last_turns, place, feats, mine, start, F32, 0, [])
    got = lax.ppermute(grad_far(kept, given), "yh", swap)
    output = sum_parts(parts)

    velocity, stepped, pushed = step(kept, given, got, biased, momentum, weight, rep_tokens)
    arrived = lax.ppermute(pushed, "replica", ahead)
    weight_out, mixed, debiased = mix(stepped, arrived, weight, output)
    return output, mixed, weight_out, velocity, debiased


def shards(tokens, cotangent, biased, momentum, weight, round_index):
    hops = lax.axis_size("replica").bit_length() - 1
    power = round_index[0] % hops
    branches = [partial(push_round, 1 << level) for level in range(hops)]
    packed, own = pack(tokens, cotangent, lax.axis_size("yh"), lax.axis_size("z"))
    return lax.switch(power, branches, packed, own, biased, momentum, weight)


def solution(mesh):
    n_rep, n_shard = mesh.devices.shape
    inner = Mesh(mesh.devices.reshape(n_rep, 2, n_shard // 4, 2), ("replica",) + SHARD)
    rows = P(("replica",) + SHARD, None)
    held = P("replica", SHARD, None)
    return jax.shard_map(
        shards,
        mesh=inner,
        in_specs=(rows, rows, held, held, P("replica"), P()),
        out_specs=(rows, held, P("replica"), held, held),
        check_vma=False,
    )
```

time: 129 us -> 132 us (1.023)
  starting transfers between devices: 57.1 us -> 64.1 us
  local copies, waits for them, and re-layouts: 2.55 us -> 0.02 us
  waiting for transfers between devices: 48.3 us -> 45.9 us
    ppermute x1, waiting for transfers between devices: 7.99 us -> 0.82 us  [push_round(): far = lax.ppermute(near, 'yh', swap)]
    ppermute x1, waiting for transfers between devices: 9.19 us -> 13.2 us  [push_round(): arrived = lax.ppermute(pushed, 'replica', ahead)]
    ppermute x5, starting transfers between devices: 25.6 us -> 29.3 us  [along(): return lax.ppermute(block, 'z', [(i, (i + turn) % nz) for i in range(nz)])]
    cond x12 -> x6, local copies, waits for them, and re-layouts: 2.55 us -> 0.02 us
    pallas_call x2 -> x3, Pallas kernels: 5.5 us -> 7.66 us  [the longest x1 3.28 us: out_part(): pl.pallas_call(kernel, grid=(steps,), in_specs=[SMEM] + [VMEM] * 3, out_s...]
    ppermute x1, starting transfers between devices: 6.5 us -> 8.43 us  [push_round(): arrived = lax.ppermute(pushed, 'replica', ahead)]
    pallas_call x8, Pallas kernels: 9.75 us -> 8.13 us  [call(): pl.pallas_call(kernel, in_specs=specs, out_specs=[VMEM] * len(outs), out_...]
  transfers between devices with their start and end apart: 11 -> 11, of which waited for: 4 -> 5; matrix products, arithmetic and copies ran while one was open for 0% -> 0% of each run, Pallas kernels for 11% -> 9%
where the time goes in v3:
time: 132 us; the launch traced here: 131 us
  starting transfers between devices  64.1 us (49%)
  waiting for transfers between devices  45.9 us (35%)
  Pallas kernels  15.8 us (12%)
  blocking collectives  3.77 us (3%)
  between operations  1.37 us (1%)
    ppermute x5, starting transfers between devices, along(): return lax.ppermute(block, 'z', [(i, (i + turn) % nz) for i in range(nz)])  29.3 us
    all_to_all x1, waiting for transfers between devices, push_round(): x = lax.all_to_all(packed, 'z', 0, 0, tiled=True)  23.4 us
    ppermute x1, waiting for transfers between devices, push_round(): arrived = lax.ppermute(pushed, 'replica', ahead)  13.2 us
    ppermute x1, starting transfers between devices, push_round(): arrived = lax.ppermute(pushed, 'replica', ahead)  8.43 us
    pallas_call x8, Pallas kernels, call(): pl.pallas_call(kernel, in_specs=specs, out_specs=[VMEM] * len(outs), out_...  8.13 us
    ppermute x1, waiting for transfers between devices, push_round(): got = lax.ppermute(grad_far(kept, given), 'yh', swap)  8.04 us
    ppermute x1, starting transfers between devices, push_round(): got = lax.ppermute(grad_far(kept, given), 'yh', swap)  7.96 us
    ppermute x1, starting transfers between devices, push_round(): far = lax.ppermute(near, 'yh', swap)  6.72 us
  transfers between devices with their start and end apart: 11, of which 5 were waited for; matrix products, arithmetic and copies ran while one was open for 0% of the time, Pallas kernels for 9%

profile of v3, /device:TPU:1, one launch (start us, length us, event | category | flops | bytes accessed | tf_op | source)
XLA Modules:
  0.0 131.3 jit_solution(3057395319764606454)
XLA Ops:
  1.3 2.7 %pack.1 = (bf16[8,128,1024]{2,1,0:T(8,128)(2,1)}, bf16[128,512]{1,0:T(8,128)(2,1)S(1)}) custom-call(bf16[128,512]{1,0:T(8,128)(2,1)} %cot.1, bf16[128,8192]{1,0:T(8,128)(2,1)} %refs_1_.1, bf16[128,8192]{1,0:T(8,128)(2,1)} %refs_1_.1), custom_call_target="tpu_custom_call" | custom-call | bytes 4194304 | tf_op jit(solution)/shard_map/pack/pallas_call | solution.py:58
  4.0 127.2 %conditional.1 = (f32[1,256,512]{2,1,0:T(8,128)}, f32[1]{0:T(128)}, f32[1,256,512]{2,1,0:T(8,128)}, f32[1,256,512]{2,1,0:T(8,128)}, bf16[128,512]{1,0:T(8,128)(2,1)}) conditional(s32[]{:T(128)} %clamp.3, (bf16[8,128,1024]{2,1,0:T(8,128)(2,1)}, bf16[128,512]{1,0:T(8,128)(2,1)S(1)}, f32[1]{0:T(128)}, ...), branch_computations={%region_0.1_spmd, %region_1.2_spmd, %region_2.3_spmd, %region_3.4_... | conditional | flops 250002604032 | bytes 47252112 | solution.py:281
  4.0 11.5 %collective-permute-start.9 = (bf16[128,512]{1,0:T(8,128)(2,1)S(1)}, bf16[128,512]{1,0:T(8,128)(2,1)S(1)}, u32[]{:S(2)}, u32[]{:S(2)}) collective-permute-start(bf16[128,512]{1,0:T(8,128)(2,1)S(1)} %get-tuple-element.55.first_ref), channel_id=1, source_target_pairs={{0,8},{2,10},{4,12},{6,14},{8,0},{10,2},{12,4},{14,6},{1,9},{3,11}... | collective-permute-start | bytes 393224 | tf_op jit(solution)/shard_map/cond/branch_1_fun/ppermute | solution.py:248
  15.5 4.3 %all-to-all-start.2 = ((bf16[8,128,1024]{2,1,0:T(8,128)(2,1)}), bf16[8,128,1024]{2,1,0:T(8,128)(2,1)S(1)}, u32[]{:S(2)}, u32[]{:S(2)}) async-start(bf16[8,128,1024]{2,1,0:T(8,128)(2,1)} %get-tuple-element.53), calls=%async_computation.2 | async-start | bytes 4194304 | tf_op jit(solution)/shard_map/cond/branch_1_fun/all_to_all | solution.py:251
  20.5 3.8 %all_gather.9.near_ref = bf16[512,512]{1,0:T(8,128)(2,1)S(1)} all-gather(bf16[256,512]{1,0:T(8,128)(2,1)S(1)} %rounded_rows.5), channel_id=1, replica_groups=mesh['replica'=16,'yh'=2,'z'=8,'core'=2] {'core'}, dimensions={0}, use_global_device_ids=true | all-gather | bytes 786432 | tf_op jit(solution)/shard_map/cond/branch_1_fun/all_gather | solution.py:257
  24.3 6.7 %collective-permute-start.10 = (bf16[512,512]{1,0:T(8,128)(2,1)S(1)}, bf16[512,512]{1,0:T(8,128)(2,1)}, u32[]{:S(2)}, u32[]{:S(2)}) collective-permute-start(bf16[512,512]{1,0:T(8,128)(2,1)S(1)} %all_gather.9.near_ref), channel_id=1, source_target_pairs={{0,16},{16,0},{1,17},{17,1},{2,18},{18,2},{3,19},{19,3},{4,20},{20... | collective-permute-start | bytes 1572872 | tf_op jit(solution)/shard_map/cond/branch_1_fun/ppermute | solution.py:258
  31.1 10.6 %collective-permute-start.14 = (bf16[128,512]{1,0:T(8,128)(2,1)S(1)}, bf16[128,512]{1,0:T(8,128)(2,1)}, u32[]{:S(2)}, u32[]{:S(2)}) collective-permute-start(bf16[128,512]{1,0:T(8,128)(2,1)S(1)} %get-tuple-element.56._), channel_id=1, source_target_pairs={{0,12},{2,14},{4,0},{6,2},{8,4},{10,6},{12,8},{14,10},{1,13},{3,15... | collective-permute-start | bytes 393224 | tf_op jit(solution)/shard_map/cond/branch_1_fun/ppermute | solution.py:248
  41.7 1.9 %collective-permute-start.13 = (bf16[128,512]{1,0:T(8,128)(2,1)S(1)}, bf16[128,512]{1,0:T(8,128)(2,1)}, u32[]{:S(2)}, u32[]{:S(2)}) collective-permute-start(bf16[128,512]{1,0:T(8,128)(2,1)S(1)} %get-tuple-element.56._), channel_id=1, source_target_pairs={{0,4},{2,6},{4,8},{6,10},{8,12},{10,14},{12,0},{14,2},{1,5},{3,7},... | collective-permute-start | bytes 393224 | tf_op jit(solution)/shard_map/cond/branch_1_fun/ppermute | solution.py:248
  43.7 2.1 %collective-permute-start.12 = (bf16[256,512]{1,0:T(8,128)(2,1)S(1)}, bf16[256,512]{1,0:T(8,128)(2,1)S(1)}, u32[]{:S(2)}, u32[]{:S(2)}) collective-permute-start(bf16[256,512]{1,0:T(8,128)(2,1)S(1)} %get-tuple-element.58.refs_0_), channel_id=1, source_target_pairs={{0,14},{2,0},{4,2},{6,4},{8,6},{10,8},{12,10},{14,12},{1,15},{3,1}... | collective-permute-start | bytes 786440 | tf_op jit(solution)/shard_map/cond/branch_1_fun/ppermute | solution.py:248
  45.7 3.2 %collective-permute-start.11 = (bf16[256,512]{1,0:T(8,128)(2,1)S(1)}, bf16[256,512]{1,0:T(8,128)(2,1)S(1)}, u32[]{:S(2)}, u32[]{:S(2)}) collective-permute-start(bf16[256,512]{1,0:T(8,128)(2,1)S(1)} %get-tuple-element.58.refs_0_), channel_id=1, source_target_pairs={{0,2},{2,4},{4,6},{6,8},{8,10},{10,12},{12,14},{14,0},{1,3},{3,5},... | collective-permute-start | bytes 786440 | tf_op jit(solution)/shard_map/cond/branch_1_fun/ppermute | solution.py:248
  49.8 23.4 %all-to-all-done.2.x_ref = bf16[8,128,1024]{2,1,0:T(8,128)(2,1)S(1)} async-done(((bf16[8,128,1024]{2,1,0:T(8,128)(2,1)}), bf16[8,128,1024]{2,1,0:T(8,128)(2,1)S(1)}, u32[]{:S(2)}, u32[]{:S(2)}) %all-to-all-start.2) | async-done | bytes 2097184 | tf_op jit(solution)/shard_map/cond/branch_1_fun/all_to_all | solution.py:251
  73.2 3.3 %out_part.5.refs_3_ = bf16[8,128,512]{2,1,0:T(8,128)(2,1)} custom-call(s32[3]{0:T(128)S(1)} %pad_add_fusion.1.place_ref, bf16[8,128,1024]{2,1,0:T(8,128)(2,1)S(1)} %all-to-all-done.2.x_ref, bf16[512,512]{1,0:T(8,128)(2,1)S(1)} %all_gather.9.near_ref, bf16[512,512]{1,0:T(8,128)(2,1)} %collective-permute-done.10.far_ref), custom_call_target="tpu_custom_call" | custom-call | flops 49999998976 | bytes 4194304 | tf_op jit(solution)/shard_map/cond/branch_1_fun/out_part/pallas_call | solution.py:114
  76.5 4.3 %all-to-all-start.3 = ((bf16[8,128,512]{2,1,0:T(8,128)(2,1)}), bf16[8,128,512]{2,1,0:T(8,128)(2,1)}, u32[]{:S(2)}, u32[]{:S(2)}) async-start(bf16[8,128,512]{2,1,0:T(8,128)(2,1)} %out_part.5.refs_3_), calls=%async_computation.3 | async-start | bytes 2097152 | tf_op jit(solution)/shard_map/cond/branch_1_fun/all_to_all | solution.py:260
  80.7 1.7 %grad_first.5.refs_2_ = f32[4,256,512]{2,1,0:T(8,128)S(1)} custom-call(s32[3]{0:T(128)S(1)} %pad_add_fusion.1.place_ref, bf16[8,128,1024]{2,1,0:T(8,128)(2,1)S(1)} %all-to-all-done.2.x_ref, bf16[256,512]{1,0:T(8,128)(2,1)S(1)} %get-tuple-element.58.refs_0_, bf16[128,512]{1,0:T(8,128)(2,1)} %collective-permute-done.13.refs_1_, ...), custom_call_target="tpu_custom_call" | custom-call | flops 49999998976 | bytes 3145728 | tf_op jit(solution)/shard_map/cond/branch_1_fun/grad_first/pallas_call | solution.py:23
  82.5 1.0 grad_sent.5
  83.6 3.2 %collective-permute-start.15 = (bf16[2,256,512]{2,1,0:T(8,128)(2,1)S(1)}, bf16[2,256,512]{2,1,0:T(8,128)(2,1)S(1)}, u32[]{:S(2)}, u32[]{:S(2)}) collective-permute-start(bf16[2,256,512]{2,1,0:T(8,128)(2,1)S(1)} %grad_sent.5), channel_id=1, source_target_pairs={{0,1},{1,0},{2,3},{3,2},{4,5},{5,4},{6,7},{7,6},{8,9},{9,8},{10,11... | collective-permute-start | bytes 1572872 | tf_op jit(solution)/shard_map/cond/branch_1_fun/ppermute | solution.py:265
  86.7 1.0 grad_kept.5.kept_ref
  88.3 8.0 %collective-permute-start.16 = (bf16[256,512]{1,0:T(8,128)(2,1)S(1)}, bf16[256,512]{1,0:T(8,128)(2,1)S(1)}, u32[]{:S(2)}, u32[]{:S(2)}) collective-permute-start(bf16[256,512]{1,0:T(8,128)(2,1)S(1)} %grad_far.5), channel_id=1, source_target_pairs={{0,16},{16,0},{1,17},{17,1},{2,18},{18,2},{3,19},{19,3},{4,20},{20... | collective-permute-start | bytes 786440 | tf_op jit(solution)/shard_map/cond/branch_1_fun/ppermute | solution.py:267
  96.3 8.0 %collective-permute-done.16.got_ref = bf16[256,512]{1,0:T(8,128)(2,1)S(1)} collective-permute-done((bf16[256,512]{1,0:T(8,128)(2,1)S(1)}, bf16[256,512]{1,0:T(8,128)(2,1)S(1)}, u32[]{:S(2)}, u32[]{:S(2)}) %collective-permute-start.16) | collective-permute-done | bytes 262176 | tf_op jit(solution)/shard_map/cond/branch_1_fun/ppermute | solution.py:267
  104.3 1.6 %step.5 = (f32[1,256,512]{2,1,0:T(8,128)}, f32[256,512]{1,0:T(8,128)S(1)}, bf16[272,512]{1,0:T(8,128)(2,1)S(1)}) custom-call(f32[1]{0:T(128)} %get-tuple-element.54.weight_ref.w_ref, f32[2,256,512]{2,1,0:T(8,128)S(1)} %grad_kept.5.kept_ref, bf16[2,256,512]{2,1,0:T(8,128)(2,1)S(1)} %collective-permute-done.15.given_ref, ...), custom_call_target="tpu_custom_call" | custom-call | flops 1048576 | bytes 3145728 | tf_op jit(solution)/shard_map/cond/branch_1_fun/step/pallas_call | solution.py:23
  105.9 8.4 %collective-permute-start.17 = (bf16[272,512]{1,0:T(8,128)(2,1)S(1)}, bf16[272,512]{1,0:T(8,128)(2,1)S(1)}, u32[]{:S(2)}, u32[]{:S(2)}) collective-permute-start(bf16[272,512]{1,0:T(8,128)(2,1)S(1)} %get-tuple-element.61), channel_id=1, source_target_pairs={{448,0},{480,32},{0,64},{32,96},{64,128},{96,160},{128,192},{160,2... | collective-permute-start | bytes 835592 | tf_op jit(solution)/shard_map/cond/branch_1_fun/ppermute | solution.py:271
  114.3 2.0 %sum_parts.5._ = bf16[128,512]{1,0:T(8,128)(2,1)} custom-call(bf16[8,128,512]{2,1,0:T(8,128)(2,1)} %all-to-all-done.3.parts_ref), custom_call_target="tpu_custom_call" | custom-call | flops 524288 | bytes 1048576 | tf_op jit(solution)/shard_map/cond/branch_1_fun/sum_parts/pallas_call | solution.py:23
  116.3 13.2 %collective-permute-done.17.a.tail = bf16[272,512]{1,0:T(8,128)(2,1)S(1)} collective-permute-done((bf16[272,512]{1,0:T(8,128)(2,1)S(1)}, bf16[272,512]{1,0:T(8,128)(2,1)S(1)}, u32[]{:S(2)}, u32[]{:S(2)}) %collective-permute-start.17) | collective-permute-done | bytes 278560 | tf_op jit(solution)/shard_map/cond/branch_1_fun/ppermute | solution.py:271
  129.5 1.7 %mix.5 = (f32[1]{0:T(128)}, f32[1,256,512]{2,1,0:T(8,128)}, f32[1,256,512]{2,1,0:T(8,128)}) custom-call(f32[1]{0:T(128)} %get-tuple-element.54.weight_ref.w_ref, bf16[128,512]{1,0:T(8,128)(2,1)} %sum_parts.5._, f32[256,512]{1,0:T(8,128)S(1)} %get-tuple-element.60.s, bf16[272,512]{1,0:T(8,128)(2,1)S(1)} %collective-permute-done.17.a.tail, ...), custom_call_target="tpu_custom_call" | custom-call | flops 786432 | bytes 2883584 | tf_op jit(solution)/shard_map/cond/branch_1_fun/mix/pallas_call | solution.py:214
  (20 shorter events, 2.1 us)
Async XLA Ops:
  1.3 2.7 %copy-start = (f32[1,256,512]{2,1,0:T(8,128)S(1)}, f32[1,256,512]{2,1,0:T(8,128)}, u32[]{:S(2)}) copy-start(f32[1,256,512]{2,1,0:T(8,128)} %param.12) | copy-start | bytes 1572868
  4.0 15.8 %copy-start.3 = (f32[1,256,512]{2,1,0:T(8,128)}, f32[1,256,512]{2,1,0:T(8,128)S(1)}, u32[]{:S(2)}) copy-start(f32[1,256,512]{2,1,0:T(8,128)S(1)} %get-tuple-element.57.numer) | copy-start | bytes 1572868 | tf_op jit(solution)/shard_map/cond
  4.0 15.8 %collective-permute-start.9 = (bf16[128,512]{1,0:T(8,128)(2,1)S(1)}, bf16[128,512]{1,0:T(8,128)(2,1)S(1)}, u32[]{:S(2)}, u32[]{:S(2)}) collective-permute-start(bf16[128,512]{1,0:T(8,128)(2,1)S(1)} %get-tuple-element.55.first_ref), channel_id=1, source_target_pairs={{0,8},{2,10},{4,12},{6,14},{8,0},{10,2},{12,4},{14,6},{1,9},{3,11}... | collective-permute-start | bytes 393224 | tf_op jit(solution)/shard_map/cond/branch_1_fun/ppermute | solution.py:248
  15.5 57.7 %all-to-all-start.2 = ((bf16[8,128,1024]{2,1,0:T(8,128)(2,1)}), bf16[8,128,1024]{2,1,0:T(8,128)(2,1)S(1)}, u32[]{:S(2)}, u32[]{:S(2)}) async-start(bf16[8,128,1024]{2,1,0:T(8,128)(2,1)} %get-tuple-element.53), calls=%async_computation.2 | async-start | bytes 4194304 | tf_op jit(solution)/shard_map/cond/branch_1_fun/all_to_all | solution.py:251
  24.3 25.5 %collective-permute-start.10 = (bf16[512,512]{1,0:T(8,128)(2,1)S(1)}, bf16[512,512]{1,0:T(8,128)(2,1)}, u32[]{:S(2)}, u32[]{:S(2)}) collective-permute-start(bf16[512,512]{1,0:T(8,128)(2,1)S(1)} %all_gather.9.near_ref), channel_id=1, source_target_pairs={{0,16},{16,0},{1,17},{17,1},{2,18},{18,2},{3,19},{19,3},{4,20},{20... | collective-permute-start | bytes 1572872 | tf_op jit(solution)/shard_map/cond/branch_1_fun/ppermute | solution.py:258
  31.1 49.6 %collective-permute-start.14 = (bf16[128,512]{1,0:T(8,128)(2,1)S(1)}, bf16[128,512]{1,0:T(8,128)(2,1)}, u32[]{:S(2)}, u32[]{:S(2)}) collective-permute-start(bf16[128,512]{1,0:T(8,128)(2,1)S(1)} %get-tuple-element.56._), channel_id=1, source_target_pairs={{0,12},{2,14},{4,0},{6,2},{8,4},{10,6},{12,8},{14,10},{1,13},{3,15... | collective-permute-start | bytes 393224 | tf_op jit(solution)/shard_map/cond/branch_1_fun/ppermute | solution.py:248
  41.7 39.0 %collective-permute-start.13 = (bf16[128,512]{1,0:T(8,128)(2,1)S(1)}, bf16[128,512]{1,0:T(8,128)(2,1)}, u32[]{:S(2)}, u32[]{:S(2)}) collective-permute-start(bf16[128,512]{1,0:T(8,128)(2,1)S(1)} %get-tuple-element.56._), channel_id=1, source_target_pairs={{0,4},{2,6},{4,8},{6,10},{8,12},{10,14},{12,0},{14,2},{1,5},{3,7},... | collective-permute-start | bytes 393224 | tf_op jit(solution)/shard_map/cond/branch_1_fun/ppermute | solution.py:248
  43.7 38.8 %collective-permute-start.12 = (bf16[256,512]{1,0:T(8,128)(2,1)S(1)}, bf16[256,512]{1,0:T(8,128)(2,1)S(1)}, u32[]{:S(2)}, u32[]{:S(2)}) collective-permute-start(bf16[256,512]{1,0:T(8,128)(2,1)S(1)} %get-tuple-element.58.refs_0_), channel_id=1, source_target_pairs={{0,14},{2,0},{4,2},{6,4},{8,6},{10,8},{12,10},{14,12},{1,15},{3,1}... | collective-permute-start | bytes 786440 | tf_op jit(solution)/shard_map/cond/branch_1_fun/ppermute | solution.py:248
  45.7 36.8 %collective-permute-start.11 = (bf16[256,512]{1,0:T(8,128)(2,1)S(1)}, bf16[256,512]{1,0:T(8,128)(2,1)S(1)}, u32[]{:S(2)}, u32[]{:S(2)}) collective-permute-start(bf16[256,512]{1,0:T(8,128)(2,1)S(1)} %get-tuple-element.58.refs_0_), channel_id=1, source_target_pairs={{0,2},{2,4},{4,6},{6,8},{8,10},{10,12},{12,14},{14,0},{1,3},{3,5},... | collective-permute-start | bytes 786440 | tf_op jit(solution)/shard_map/cond/branch_1_fun/ppermute | solution.py:248
  76.5 37.9 %all-to-all-start.3 = ((bf16[8,128,512]{2,1,0:T(8,128)(2,1)}), bf16[8,128,512]{2,1,0:T(8,128)(2,1)}, u32[]{:S(2)}, u32[]{:S(2)}) async-start(bf16[8,128,512]{2,1,0:T(8,128)(2,1)} %out_part.5.refs_3_), calls=%async_computation.3 | async-start | bytes 2097152 | tf_op jit(solution)/shard_map/cond/branch_1_fun/all_to_all | solution.py:260
  83.6 4.7 %collective-permute-start.15 = (bf16[2,256,512]{2,1,0:T(8,128)(2,1)S(1)}, bf16[2,256,512]{2,1,0:T(8,128)(2,1)S(1)}, u32[]{:S(2)}, u32[]{:S(2)}) collective-permute-start(bf16[2,256,512]{2,1,0:T(8,128)(2,1)S(1)} %grad_sent.5), channel_id=1, source_target_pairs={{0,1},{1,0},{2,3},{3,2},{4,5},{5,4},{6,7},{7,6},{8,9},{9,8},{10,11... | collective-permute-start | bytes 1572872 | tf_op jit(solution)/shard_map/cond/branch_1_fun/ppermute | solution.py:265
  87.8 16.5 %copy-start.4 = (f32[1,256,512]{2,1,0:T(8,128)S(1)}, f32[1,256,512]{2,1,0:T(8,128)}, u32[]{:S(2)}) copy-start(f32[1,256,512]{2,1,0:T(8,128)} %copy-done.3) | copy-start | bytes 1572868 | tf_op jit(solution)/shard_map/cond
  87.8 16.5 %copy-start.10 = (f32[1,256,512]{2,1,0:T(8,128)S(1)}, f32[1,256,512]{2,1,0:T(8,128)}, u32[]{:S(2)}) copy-start(f32[1,256,512]{2,1,0:T(8,128)} %get-tuple-element.59.moment) | copy-start | bytes 1572868 | tf_op jit(solution)/shard_map/cond
  88.3 16.0 %collective-permute-start.16 = (bf16[256,512]{1,0:T(8,128)(2,1)S(1)}, bf16[256,512]{1,0:T(8,128)(2,1)S(1)}, u32[]{:S(2)}, u32[]{:S(2)}) collective-permute-start(bf16[256,512]{1,0:T(8,128)(2,1)S(1)} %grad_far.5), channel_id=1, source_target_pairs={{0,16},{16,0},{1,17},{17,1},{2,18},{18,2},{3,19},{19,3},{4,20},{20... | collective-permute-start | bytes 786440 | tf_op jit(solution)/shard_map/cond/branch_1_fun/ppermute | solution.py:267
  105.9 23.7 %collective-permute-start.17 = (bf16[272,512]{1,0:T(8,128)(2,1)S(1)}, bf16[272,512]{1,0:T(8,128)(2,1)S(1)}, u32[]{:S(2)}, u32[]{:S(2)}) collective-permute-start(bf16[272,512]{1,0:T(8,128)(2,1)S(1)} %get-tuple-element.61), channel_id=1, source_target_pairs={{448,0},{480,32},{0,64},{32,96},{64,128},{96,160},{128,192},{160,2... | collective-permute-start | bytes 835592 | tf_op jit(solution)/shard_map/cond/branch_1_fun/ppermute | solution.py:271

commit v4 on v3

--- a/solution.py
+++ b/solution.py
@@ -40,17 +40,15 @@
     return call("rounded_rows", kernel, [((n, kv), BF16)], (weight, after, biased), [SMEM, ANY, VMEM])[0]
 
 
-def pack(tokens, cotangent, ny, nz):
+def pack(tokens, ny, nz):
     rows, width = tokens.shape
-    kv = cotangent.shape[1]
     steps = 2
     zs = nz // steps
     cols = width // ny // steps
     part = width // ny // nz
 
-    def kernel(cot, *refs):
-        out, kept = refs[-2:]
-        kept[...] = cot[...]
+    def kernel(*refs):
+        out = refs[-1]
         for p in range(zs):
             for y in range(ny):
                 out[p, :, y * part : (y + 1) * part] = refs[y][:, p * part : (p + 1) * part]
@@ -58,20 +56,13 @@
     return pl.pallas_call(
         kernel,
         grid=(steps,),
-        in_specs=[pl.BlockSpec((rows // steps, kv), lambda g: (g, 0))]
-        + [pl.BlockSpec((rows, cols), lambda g, y=y: (0, y * steps + g)) for y in range(ny)],
-        out_specs=[
-            pl.BlockSpec((zs, rows, ny * part), lambda g: (g, 0, 0)),
-            pl.BlockSpec((rows // steps, kv), lambda g: (g, 0)),
-        ],
-        out_shape=[
-            jax.ShapeDtypeStruct((nz, rows, ny * part), BF16),
-            jax.ShapeDtypeStruct((rows, kv), BF16),
-        ],
+        in_specs=[pl.BlockSpec((rows, cols), lambda g, y=y: (0, y * steps + g)) for y in range(ny)],
+        out_specs=pl.BlockSpec((zs, rows, ny * part), lambda g: (g, 0, 0)),
+        out_shape=jax.ShapeDtypeStruct((nz, rows, ny * part), BF16),
         compiler_params=pltpu.CompilerParams(vmem_limit_bytes=60 << 20),
         cost_estimate=pl.CostEstimate(flops=0, bytes_accessed=4 * rows * width, transcendentals=0),
         name="pack",
-    )(cotangent, *[tokens] * ny)
+    )(*[tokens] * ny)
 
 
 def join(first, second):
@@ -235,7 +226,7 @@
     return call("sum_parts", kernel, [((rows, kv), BF16)], (parts,), [VMEM], flops=parts.size, moved=2 * parts.size)[0]
 
 
-def push_round(dist, packed, own, biased, momentum, weight):
+def push_round(dist, tokens, own, biased, momentum, weight):
     ny, nz, nc = (lax.axis_size(a) for a in SHARD)
     feats = biased.shape[1]
     rep_tokens = own.shape[0] * ny * nz * nc
@@ -248,7 +239,7 @@
         return lax.ppermute(block, "z", [(i, (i + turn) % nz) for i in range(nz)])
 
     pair, alone = join(own, along(own, 4))
-    x = lax.all_to_all(packed, "z", 0, 0, tiled=True)
+    x = lax.all_to_all(pack(tokens, ny, nz), "z", 0, 0, tiled=True)
     first = [pair, along(alone, 2), along(alone, -2)]
     first_turns = [((0, 4),), ((2,), (6,))]
     last = [along(pair, 1), along(pair, -1)]
@@ -277,8 +268,7 @@
     hops = lax.axis_size("replica").bit_length() - 1
     power = round_index[0] % hops
     branches = [partial(push_round, 1 << level) for level in range(hops)]
-    packed, own = pack(tokens, cotangent, lax.axis_size("yh"), lax.axis_size("z"))
-    return lax.switch(power, branches, packed, own, biased, momentum, weight)
+    return lax.switch(power, branches, tokens, cotangent, biased, momentum, weight)
 
 
 def solution(mesh):

time: 132 us -> 130 us (0.985)
  starting transfers between devices: 64.1 us -> 62.2 us
    ppermute x5, starting transfers between devices: 29.3 us -> 25.6 us  [along(): return lax.ppermute(block, 'z', [(i, (i + turn) % nz) for i in range(nz)])]
    ppermute x1, waiting for transfers between devices: 0.82 us -> 3.11 us  [push_round(): far = lax.ppermute(near, 'yh', swap)]
    all_to_all x1, waiting for transfers between devices: 23.4 us -> 21.4 us  [push_round(): x = lax.all_to_all(pack(tokens, ny, nz), 'z', 0, 0, tiled=True)]
  transfers between devices with their start and end apart: 11 -> 11, of which waited for: 5 -> 5; matrix products, arithmetic and copies ran while one was open for 0% -> 0% of each run, Pallas kernels for 9% -> 11%
where the time goes in v4:
time: 130 us
  starting transfers between devices  62.2 us (48%)
  waiting for transfers between devices  46.1 us (35%)
  Pallas kernels  15.7 us (12%)
  blocking collectives  3.04 us (2%)
  between operations  1.36 us (1%)
    ppermute x5, starting transfers between devices, along(): return lax.ppermute(block, 'z', [(i, (i + turn) % nz) for i in range(nz)])  25.6 us
    all_to_all x1, waiting for transfers between devices, push_round(): x = lax.all_to_all(pack(tokens, ny, nz), 'z', 0, 0, tiled=True)  21.4 us
    ppermute x1, waiting for transfers between devices, push_round(): arrived = lax.ppermute(pushed, 'replica', ahead)  13.2 us
    ppermute x1, starting transfers between devices, push_round(): arrived = lax.ppermute(pushed, 'replica', ahead)  8.55 us
    pallas_call x8, Pallas kernels, call(): pl.pallas_call(kernel, in_specs=specs, out_specs=[VMEM] * len(outs), out_...  8.14 us
    ppermute x1, waiting for transfers between devices, push_round(): got = lax.ppermute(grad_far(kept, given), 'yh', swap)  7.91 us
    ppermute x1, starting transfers between devices, push_round(): got = lax.ppermute(grad_far(kept, given), 'yh', swap)  7.45 us
    ppermute x1, starting transfers between devices, push_round(): far = lax.ppermute(near, 'yh', swap)  7.44 us
  transfers between devices with their start and end apart: 11, of which 5 were waited for; matrix products, arithmetic and copies ran while one was open for 0% of the time, Pallas kernels for 11%

profile of v4, /device:TPU:1, one launch (start us, length us, event | category | flops | bytes accessed | tf_op | source)
XLA Modules:
  0.0 129.7 jit_solution(6219759021000168942)
XLA Ops:
  1.3 128.3 %conditional.1 = (f32[1,256,512]{2,1,0:T(8,128)}, f32[1]{0:T(128)}, f32[1,256,512]{2,1,0:T(8,128)}, f32[1,256,512]{2,1,0:T(8,128)}, bf16[128,512]{1,0:T(8,128)(2,1)}) conditional(s32[]{:T(128)} %clamp.3, (bf16[128,8192]{1,0:T(8,128)(2,1)}, bf16[128,512]{1,0:T(8,128)(2,1)}, f32[1]{0:T(128)}, f32[1,256,512]{2,1,0:T(8,128)}, ...), branch_computations={%region_0.1_spmd, %region_1.2_spmd, %region_2.3_spmd, %region_3.4_... | conditional | flops 250002604032 | bytes 51970732 | solution.py:271
  1.3 11.5 %collective-permute-start.9 = (bf16[128,512]{1,0:T(8,128)(2,1)}, bf16[128,512]{1,0:T(8,128)(2,1)S(1)}, u32[]{:S(2)}, u32[]{:S(2)}) collective-permute-start(bf16[128,512]{1,0:T(8,128)(2,1)} %get-tuple-element.55.first_ref), channel_id=1, source_target_pairs={{0,8},{2,10},{4,12},{6,14},{8,0},{10,2},{12,4},{14,6},{1,9},{3,11}... | collective-permute-start | bytes 393224 | tf_op jit(solution)/shard_map/cond/branch_1_fun/ppermute | solution.py:239
  12.8 2.6 %pack.5 = bf16[8,128,1024]{2,1,0:T(8,128)(2,1)} custom-call(bf16[128,8192]{1,0:T(8,128)(2,1)} %get-tuple-element.53.refs_0_.refs_1_, bf16[128,8192]{1,0:T(8,128)(2,1)} %get-tuple-element.53.refs_0_.refs_1_), custom_call_target="tpu_custom_call" | custom-call | bytes 4194304 | tf_op jit(solution)/shard_map/cond/branch_1_fun/pack/pallas_call | solution.py:56
  15.4 4.4 %all-to-all-start.2 = ((bf16[8,128,1024]{2,1,0:T(8,128)(2,1)}), bf16[8,128,1024]{2,1,0:T(8,128)(2,1)S(1)}, u32[]{:S(2)}, u32[]{:S(2)}) async-start(bf16[8,128,1024]{2,1,0:T(8,128)(2,1)} %pack.5), calls=%async_computation.2 | async-start | bytes 4194304 | tf_op jit(solution)/shard_map/cond/branch_1_fun/all_to_all | solution.py:242
  21.6 3.0 %all_gather.9.near_ref = bf16[512,512]{1,0:T(8,128)(2,1)S(1)} all-gather(bf16[256,512]{1,0:T(8,128)(2,1)S(1)} %rounded_rows.5), channel_id=1, replica_groups=mesh['replica'=16,'yh'=2,'z'=8,'core'=2] {'core'}, dimensions={0}, use_global_device_ids=true | all-gather | bytes 786432 | tf_op jit(solution)/shard_map/cond/branch_1_fun/all_gather | solution.py:248
  24.6 7.4 %collective-permute-start.10 = (bf16[512,512]{1,0:T(8,128)(2,1)S(1)}, bf16[512,512]{1,0:T(8,128)(2,1)}, u32[]{:S(2)}, u32[]{:S(2)}) collective-permute-start(bf16[512,512]{1,0:T(8,128)(2,1)S(1)} %all_gather.9.near_ref), channel_id=1, source_target_pairs={{0,16},{16,0},{1,17},{17,1},{2,18},{18,2},{3,19},{19,3},{4,20},{20... | collective-permute-start | bytes 1572872 | tf_op jit(solution)/shard_map/cond/branch_1_fun/ppermute | solution.py:249
  32.1 5.8 %collective-permute-start.14 = (bf16[128,512]{1,0:T(8,128)(2,1)S(1)}, bf16[128,512]{1,0:T(8,128)(2,1)}, u32[]{:S(2)}, u32[]{:S(2)}) collective-permute-start(bf16[128,512]{1,0:T(8,128)(2,1)S(1)} %get-tuple-element.56._), channel_id=1, source_target_pairs={{0,12},{2,14},{4,0},{6,2},{8,4},{10,6},{12,8},{14,10},{1,13},{3,15... | collective-permute-start | bytes 393224 | tf_op jit(solution)/shard_map/cond/branch_1_fun/ppermute | solution.py:239
  37.9 1.9 %collective-permute-start.13 = (bf16[128,512]{1,0:T(8,128)(2,1)S(1)}, bf16[128,512]{1,0:T(8,128)(2,1)}, u32[]{:S(2)}, u32[]{:S(2)}) collective-permute-start(bf16[128,512]{1,0:T(8,128)(2,1)S(1)} %get-tuple-element.56._), channel_id=1, source_target_pairs={{0,4},{2,6},{4,8},{6,10},{8,12},{10,14},{12,0},{14,2},{1,5},{3,7},... | collective-permute-start | bytes 393224 | tf_op jit(solution)/shard_map/cond/branch_1_fun/ppermute | solution.py:239
  39.8 4.6 %collective-permute-start.12 = (bf16[256,512]{1,0:T(8,128)(2,1)S(1)}, bf16[256,512]{1,0:T(8,128)(2,1)S(1)}, u32[]{:S(2)}, u32[]{:S(2)}) collective-permute-start(bf16[256,512]{1,0:T(8,128)(2,1)S(1)} %get-tuple-element.58.refs_0_), channel_id=1, source_target_pairs={{0,14},{2,0},{4,2},{6,4},{8,6},{10,8},{12,10},{14,12},{1,15},{3,1}... | collective-permute-start | bytes 786440 | tf_op jit(solution)/shard_map/cond/branch_1_fun/ppermute | solution.py:239
  44.4 1.9 %collective-permute-start.11 = (bf16[256,512]{1,0:T(8,128)(2,1)S(1)}, bf16[256,512]{1,0:T(8,128)(2,1)S(1)}, u32[]{:S(2)}, u32[]{:S(2)}) collective-permute-start(bf16[256,512]{1,0:T(8,128)(2,1)S(1)} %get-tuple-element.58.refs_0_), channel_id=1, source_target_pairs={{0,2},{2,4},{4,6},{6,8},{8,10},{10,12},{12,14},{14,0},{1,3},{3,5},... | collective-permute-start | bytes 786440 | tf_op jit(solution)/shard_map/cond/branch_1_fun/ppermute | solution.py:239
  46.3 3.1 %collective-permute-done.10.far_ref = bf16[512,512]{1,0:T(8,128)(2,1)} collective-permute-done((bf16[512,512]{1,0:T(8,128)(2,1)S(1)}, bf16[512,512]{1,0:T(8,128)(2,1)}, u32[]{:S(2)}, u32[]{:S(2)}) %collective-permute-start.10) | collective-permute-done | bytes 524320 | tf_op jit(solution)/shard_map/cond/branch_1_fun/ppermute | solution.py:249
  49.4 21.4 %all-to-all-done.2.x_ref = bf16[8,128,1024]{2,1,0:T(8,128)(2,1)S(1)} async-done(((bf16[8,128,1024]{2,1,0:T(8,128)(2,1)}), bf16[8,128,1024]{2,1,0:T(8,128)(2,1)S(1)}, u32[]{:S(2)}, u32[]{:S(2)}) %all-to-all-start.2) | async-done | bytes 2097184 | tf_op jit(solution)/shard_map/cond/branch_1_fun/all_to_all | solution.py:242
  70.9 3.3 %out_part.5.refs_3_ = bf16[8,128,512]{2,1,0:T(8,128)(2,1)} custom-call(s32[3]{0:T(128)S(1)} %pad_add_fusion.1.place_ref, bf16[8,128,1024]{2,1,0:T(8,128)(2,1)S(1)} %all-to-all-done.2.x_ref, bf16[512,512]{1,0:T(8,128)(2,1)S(1)} %all_gather.9.near_ref, bf16[512,512]{1,0:T(8,128)(2,1)} %collective-permute-done.10.far_ref), custom_call_target="tpu_custom_call" | custom-call | flops 49999998976 | bytes 4194304 | tf_op jit(solution)/shard_map/cond/branch_1_fun/out_part/pallas_call | solution.py:105
  74.2 4.7 %all-to-all-start.3 = ((bf16[8,128,512]{2,1,0:T(8,128)(2,1)}), bf16[8,128,512]{2,1,0:T(8,128)(2,1)}, u32[]{:S(2)}, u32[]{:S(2)}) async-start(bf16[8,128,512]{2,1,0:T(8,128)(2,1)} %out_part.5.refs_3_), calls=%async_computation.3 | async-start | bytes 2097152 | tf_op jit(solution)/shard_map/cond/branch_1_fun/all_to_all | solution.py:251
  78.9 1.7 %grad_first.5.refs_2_ = f32[4,256,512]{2,1,0:T(8,128)S(1)} custom-call(s32[3]{0:T(128)S(1)} %pad_add_fusion.1.place_ref, bf16[8,128,1024]{2,1,0:T(8,128)(2,1)S(1)} %all-to-all-done.2.x_ref, bf16[256,512]{1,0:T(8,128)(2,1)S(1)} %get-tuple-element.58.refs_0_, bf16[128,512]{1,0:T(8,128)(2,1)} %collective-permute-done.13.refs_1_, ...), custom_call_target="tpu_custom_call" | custom-call | flops 49999998976 | bytes 3145728 | tf_op jit(solution)/shard_map/cond/branch_1_fun/grad_first/pallas_call | solution.py:23
  80.7 1.0 grad_sent.5
  81.7 3.9 %collective-permute-start.15 = (bf16[2,256,512]{2,1,0:T(8,128)(2,1)S(1)}, bf16[2,256,512]{2,1,0:T(8,128)(2,1)S(1)}, u32[]{:S(2)}, u32[]{:S(2)}) collective-permute-start(bf16[2,256,512]{2,1,0:T(8,128)(2,1)S(1)} %grad_sent.5), channel_id=1, source_target_pairs={{0,1},{1,0},{2,3},{3,2},{4,5},{5,4},{6,7},{7,6},{8,9},{9,8},{10,11... | collective-permute-start | bytes 1572872 | tf_op jit(solution)/shard_map/cond/branch_1_fun/ppermute | solution.py:256
  87.3 7.4 %collective-permute-start.16 = (bf16[256,512]{1,0:T(8,128)(2,1)S(1)}, bf16[256,512]{1,0:T(8,128)(2,1)S(1)}, u32[]{:S(2)}, u32[]{:S(2)}) collective-permute-start(bf16[256,512]{1,0:T(8,128)(2,1)S(1)} %grad_far.5), channel_id=1, source_target_pairs={{0,16},{16,0},{1,17},{17,1},{2,18},{18,2},{3,19},{19,3},{4,20},{20... | collective-permute-start | bytes 786440 | tf_op jit(solution)/shard_map/cond/branch_1_fun/ppermute | solution.py:258
  94.7 7.9 %collective-permute-done.16.got_ref = bf16[256,512]{1,0:T(8,128)(2,1)S(1)} collective-permute-done((bf16[256,512]{1,0:T(8,128)(2,1)S(1)}, bf16[256,512]{1,0:T(8,128)(2,1)S(1)}, u32[]{:S(2)}, u32[]{:S(2)}) %collective-permute-start.16) | collective-permute-done | bytes 262176 | tf_op jit(solution)/shard_map/cond/branch_1_fun/ppermute | solution.py:258
  102.6 1.6 %step.5 = (f32[1,256,512]{2,1,0:T(8,128)}, f32[256,512]{1,0:T(8,128)S(1)}, bf16[272,512]{1,0:T(8,128)(2,1)S(1)}) custom-call(f32[1]{0:T(128)} %get-tuple-element.54.weight_ref.w_ref, f32[2,256,512]{2,1,0:T(8,128)S(1)} %grad_kept.5.kept_ref, bf16[2,256,512]{2,1,0:T(8,128)(2,1)S(1)} %collective-permute-done.15.given_ref, ...), custom_call_target="tpu_custom_call" | custom-call | flops 1048576 | bytes 3145728 | tf_op jit(solution)/shard_map/cond/branch_1_fun/step/pallas_call | solution.py:23
  104.2 8.6 %collective-permute-start.17 = (bf16[272,512]{1,0:T(8,128)(2,1)S(1)}, bf16[272,512]{1,0:T(8,128)(2,1)S(1)}, u32[]{:S(2)}, u32[]{:S(2)}) collective-permute-start(bf16[272,512]{1,0:T(8,128)(2,1)S(1)} %get-tuple-element.61), channel_id=1, source_target_pairs={{448,0},{480,32},{0,64},{32,96},{64,128},{96,160},{128,192},{160,2... | collective-permute-start | bytes 835592 | tf_op jit(solution)/shard_map/cond/branch_1_fun/ppermute | solution.py:262
  112.8 2.0 %sum_parts.5._ = bf16[128,512]{1,0:T(8,128)(2,1)} custom-call(bf16[8,128,512]{2,1,0:T(8,128)(2,1)} %all-to-all-done.3.parts_ref), custom_call_target="tpu_custom_call" | custom-call | flops 524288 | bytes 1048576 | tf_op jit(solution)/shard_map/cond/branch_1_fun/sum_parts/pallas_call | solution.py:23
  114.8 13.2 %collective-permute-done.17.a.tail = bf16[272,512]{1,0:T(8,128)(2,1)S(1)} collective-permute-done((bf16[272,512]{1,0:T(8,128)(2,1)S(1)}, bf16[272,512]{1,0:T(8,128)(2,1)S(1)}, u32[]{:S(2)}, u32[]{:S(2)}) %collective-permute-start.17) | collective-permute-done | bytes 278560 | tf_op jit(solution)/shard_map/cond/branch_1_fun/ppermute | solution.py:262
  127.9 1.7 %mix.5 = (f32[1]{0:T(128)}, f32[1,256,512]{2,1,0:T(8,128)}, f32[1,256,512]{2,1,0:T(8,128)}) custom-call(f32[1]{0:T(128)} %get-tuple-element.54.weight_ref.w_ref, bf16[128,512]{1,0:T(8,128)(2,1)} %sum_parts.5._, f32[256,512]{1,0:T(8,128)S(1)} %get-tuple-element.60.s, bf16[272,512]{1,0:T(8,128)(2,1)S(1)} %collective-permute-done.17.a.tail, ...), custom_call_target="tpu_custom_call" | custom-call | flops 786432 | bytes 2883584 | tf_op jit(solution)/shard_map/cond/branch_1_fun/mix/pallas_call | solution.py:205
  (20 shorter events, 3.3 us)
Async XLA Ops:
  1.3 18.5 %collective-permute-start.9 = (bf16[128,512]{1,0:T(8,128)(2,1)}, bf16[128,512]{1,0:T(8,128)(2,1)S(1)}, u32[]{:S(2)}, u32[]{:S(2)}) collective-permute-start(bf16[128,512]{1,0:T(8,128)(2,1)} %get-tuple-element.55.first_ref), channel_id=1, source_target_pairs={{0,8},{2,10},{4,12},{6,14},{8,0},{10,2},{12,4},{14,6},{1,9},{3,11}... | collective-permute-start | bytes 393224 | tf_op jit(solution)/shard_map/cond/branch_1_fun/ppermute | solution.py:239
  15.4 4.4 %copy-start.13 = (bf16[128,512]{1,0:T(8,128)(2,1)S(1)}, bf16[128,512]{1,0:T(8,128)(2,1)}, u32[]{:S(2)}) copy-start(bf16[128,512]{1,0:T(8,128)(2,1)} %get-tuple-element.55.first_ref) | copy-start | bytes 393220 | tf_op jit(solution)/shard_map/cond
  15.4 55.5 %all-to-all-start.2 = ((bf16[8,128,1024]{2,1,0:T(8,128)(2,1)}), bf16[8,128,1024]{2,1,0:T(8,128)(2,1)S(1)}, u32[]{:S(2)}, u32[]{:S(2)}) async-start(bf16[8,128,1024]{2,1,0:T(8,128)(2,1)} %pack.5), calls=%async_computation.2 | async-start | bytes 4194304 | tf_op jit(solution)/shard_map/cond/branch_1_fun/all_to_all | solution.py:242
  19.8 1.0 copy-start.2
  24.6 24.8 %collective-permute-start.10 = (bf16[512,512]{1,0:T(8,128)(2,1)S(1)}, bf16[512,512]{1,0:T(8,128)(2,1)}, u32[]{:S(2)}, u32[]{:S(2)}) collective-permute-start(bf16[512,512]{1,0:T(8,128)(2,1)S(1)} %all_gather.9.near_ref), channel_id=1, source_target_pairs={{0,16},{16,0},{1,17},{17,1},{2,18},{18,2},{3,19},{19,3},{4,20},{20... | collective-permute-start | bytes 1572872 | tf_op jit(solution)/shard_map/cond/branch_1_fun/ppermute | solution.py:249
  32.1 46.8 %collective-permute-start.14 = (bf16[128,512]{1,0:T(8,128)(2,1)S(1)}, bf16[128,512]{1,0:T(8,128)(2,1)}, u32[]{:S(2)}, u32[]{:S(2)}) collective-permute-start(bf16[128,512]{1,0:T(8,128)(2,1)S(1)} %get-tuple-element.56._), channel_id=1, source_target_pairs={{0,12},{2,14},{4,0},{6,2},{8,4},{10,6},{12,8},{14,10},{1,13},{3,15... | collective-permute-start | bytes 393224 | tf_op jit(solution)/shard_map/cond/branch_1_fun/ppermute | solution.py:239
  37.9 41.0 %collective-permute-start.13 = (bf16[128,512]{1,0:T(8,128)(2,1)S(1)}, bf16[128,512]{1,0:T(8,128)(2,1)}, u32[]{:S(2)}, u32[]{:S(2)}) collective-permute-start(bf16[128,512]{1,0:T(8,128)(2,1)S(1)} %get-tuple-element.56._), channel_id=1, source_target_pairs={{0,4},{2,6},{4,8},{6,10},{8,12},{10,14},{12,0},{14,2},{1,5},{3,7},... | collective-permute-start | bytes 393224 | tf_op jit(solution)/shard_map/cond/branch_1_fun/ppermute | solution.py:239
  39.8 40.9 %collective-permute-start.12 = (bf16[256,512]{1,0:T(8,128)(2,1)S(1)}, bf16[256,512]{1,0:T(8,128)(2,1)S(1)}, u32[]{:S(2)}, u32[]{:S(2)}) collective-permute-start(bf16[256,512]{1,0:T(8,128)(2,1)S(1)} %get-tuple-element.58.refs_0_), channel_id=1, source_target_pairs={{0,14},{2,0},{4,2},{6,4},{8,6},{10,8},{12,10},{14,12},{1,15},{3,1}... | collective-permute-start | bytes 786440 | tf_op jit(solution)/shard_map/cond/branch_1_fun/ppermute | solution.py:239
  44.4 36.3 %collective-permute-start.11 = (bf16[256,512]{1,0:T(8,128)(2,1)S(1)}, bf16[256,512]{1,0:T(8,128)(2,1)S(1)}, u32[]{:S(2)}, u32[]{:S(2)}) collective-permute-start(bf16[256,512]{1,0:T(8,128)(2,1)S(1)} %get-tuple-element.58.refs_0_), channel_id=1, source_target_pairs={{0,2},{2,4},{4,6},{6,8},{8,10},{10,12},{12,14},{14,0},{1,3},{3,5},... | collective-permute-start | bytes 786440 | tf_op jit(solution)/shard_map/cond/branch_1_fun/ppermute | solution.py:239
  74.2 38.6 %all-to-all-start.3 = ((bf16[8,128,512]{2,1,0:T(8,128)(2,1)}), bf16[8,128,512]{2,1,0:T(8,128)(2,1)}, u32[]{:S(2)}, u32[]{:S(2)}) async-start(bf16[8,128,512]{2,1,0:T(8,128)(2,1)} %out_part.5.refs_3_), calls=%async_computation.3 | async-start | bytes 2097152 | tf_op jit(solution)/shard_map/cond/branch_1_fun/all_to_all | solution.py:251
  81.7 5.5 %collective-permute-start.15 = (bf16[2,256,512]{2,1,0:T(8,128)(2,1)S(1)}, bf16[2,256,512]{2,1,0:T(8,128)(2,1)S(1)}, u32[]{:S(2)}, u32[]{:S(2)}) collective-permute-start(bf16[2,256,512]{2,1,0:T(8,128)(2,1)S(1)} %grad_sent.5), channel_id=1, source_target_pairs={{0,1},{1,0},{2,3},{3,2},{4,5},{5,4},{6,7},{7,6},{8,9},{9,8},{10,11... | collective-permute-start | bytes 1572872 | tf_op jit(solution)/shard_map/cond/branch_1_fun/ppermute | solution.py:256
  86.7 15.9 %copy-start.3 = (f32[1,256,512]{2,1,0:T(8,128)S(1)}, f32[1,256,512]{2,1,0:T(8,128)}, u32[]{:S(2)}) copy-start(f32[1,256,512]{2,1,0:T(8,128)} %get-tuple-element.57.numer) | copy-start | bytes 1572868 | tf_op jit(solution)/shard_map/cond
  86.7 15.9 %copy-start.9 = (f32[1,256,512]{2,1,0:T(8,128)S(1)}, f32[1,256,512]{2,1,0:T(8,128)}, u32[]{:S(2)}) copy-start(f32[1,256,512]{2,1,0:T(8,128)} %get-tuple-element.59.moment) | copy-start | bytes 1572868 | tf_op jit(solution)/shard_map/cond
  87.3 15.4 %collective-permute-start.16 = (bf16[256,512]{1,0:T(8,128)(2,1)S(1)}, bf16[256,512]{1,0:T(8,128)(2,1)S(1)}, u32[]{:S(2)}, u32[]{:S(2)}) collective-permute-start(bf16[256,512]{1,0:T(8,128)(2,1)S(1)} %grad_far.5), channel_id=1, source_target_pairs={{0,16},{16,0},{1,17},{17,1},{2,18},{18,2},{3,19},{19,3},{4,20},{20... | collective-permute-start | bytes 786440 | tf_op jit(solution)/shard_map/cond/branch_1_fun/ppermute | solution.py:258
  104.2 23.7 %collective-permute-start.17 = (bf16[272,512]{1,0:T(8,128)(2,1)S(1)}, bf16[272,512]{1,0:T(8,128)(2,1)S(1)}, u32[]{:S(2)}, u32[]{:S(2)}) collective-permute-start(bf16[272,512]{1,0:T(8,128)(2,1)S(1)} %get-tuple-element.61), channel_id=1, source_target_pairs={{448,0},{480,32},{0,64},{32,96},{64,128},{96,160},{128,192},{160,2... | collective-permute-start | bytes 835592 | tf_op jit(solution)/shard_map/cond/branch_1_fun/ppermute | solution.py:262

commit v5 on v4

--- a/solution.py
+++ b/solution.py
@@ -137,7 +137,7 @@
         for i, (dy, dc) in enumerate(which):
             total = grad_block(place_ref, x_ref, refs[: len(cots)], turns, dy, dc, feats)
             if more:
-                total += refs[len(cots)][dc * 2 + dy]
+                total += refs[len(cots)][i]
             out[i] = total.astype(out_type)
 
     return call(
@@ -158,16 +158,17 @@
     return call("grad_far", kernel, [(kept.shape[1:], BF16)], (kept, given), [VMEM] * 2, flops=kept.size)[0]
 
 
-def step(kept, given, got, biased, momentum, weight, rep_tokens):
+def momentum_step(kept, given, got, numer, moment, rep_tokens):
+    g = kept + given.astype(F32) + got.astype(F32)
+    v = MOMENT * moment + g * (1.0 / rep_tokens)
+    return v, numer - LEARN * (g * (1.0 / rep_tokens) + MOMENT * v)
+
+
+def push(kept, given, got, biased, momentum, weight, rep_tokens):
     size, kv = got.shape
 
-    def kernel(w_ref, kept_ref, given_ref, got_ref, numer, moment, velocity, stepped, pushed):
-        g = kept_ref[0] + given_ref[0].astype(F32) + got_ref[...].astype(F32)
-        g = g * (1.0 / rep_tokens)
-        v = MOMENT * moment[0] + g
-        velocity[0] = v
-        s = numer[0] - LEARN * (g + MOMENT * v)
-        stepped[...] = s
+    def kernel(w_ref, kept_ref, given_ref, got_ref, numer, moment, pushed):
+        _, s = momentum_step(kept_ref[0], given_ref[0], got_ref[...], numer[0], moment[0], rep_tokens)
         pushed[:size] = s.astype(BF16)
         whole = jnp.full((TAIL, kv), w_ref[0], F32)
         high = whole.astype(BF16).astype(F32)
@@ -177,12 +178,31 @@
         pushed[size:] = jnp.where(row == 0, high, jnp.where(row == 1, middle, low)).astype(BF16)
 
     return call(
-        "step",
-        kernel,
-        [((1, size, kv), F32), ((size, kv), F32), ((size + TAIL, kv), BF16)],
+        "push",
+        kernel,
+        [((size + TAIL, kv), BF16)],
         (weight, kept, given, got, biased, momentum),
         [SMEM] + [VMEM] * 5,
         flops=8 * size * kv,
+        moved=24 * size * kv,
+    )[0]
+
+
+def step(kept, given, got, biased, momentum, rep_tokens, after):
+    size, kv = got.shape
+
+    def kernel(_, kept_ref, given_ref, got_ref, numer, moment, velocity, stepped):
+        v, s = momentum_step(kept_ref[0], given_ref[0], got_ref[...], numer[0], moment[0], rep_tokens)
+        velocity[0] = v
+        stepped[...] = s
+
+    return call(
+        "step",
+        kernel,
+        [((1, size, kv), F32), ((size, kv), F32)],
+        (after, kept, given, got, biased, momentum),
+        [ANY] + [VMEM] * 5,
+        flops=0,
         moved=24 * size * kv,
     )
 
@@ -251,14 +271,15 @@
     parts = lax.all_to_all(part, "z", 0, 0, tiled=True)
 
     mine, other = ((0, 0), (1, 0)), ((0, 1), (1, 1))
-    start = grad_part("grad_first", x, first, first_turns, place, feats, mine + other, None, F32, WAIT, [part])
+    start = grad_part("grad_first", x, first, first_turns, place, feats, other, None, F32, WAIT, [part])
     given = grad_part("grad_sent", x, last, last_turns, place, feats, other, start, BF16, 2 * WAIT, [])
     given = lax.ppermute(given, "core", swap)
-    kept = grad_part("grad_kept", x, last, last_turns, place, feats, mine, start, F32, 0, [])
+    kept = grad_part("grad_kept", x, first + last, first_turns + last_turns, place, feats, mine, None, F32, 0, [])
     got = lax.ppermute(grad_far(kept, given), "yh", swap)
     output = sum_parts(parts)
 
-    velocity, stepped, pushed = step(kept, given, got, biased, momentum, weight, rep_tokens)
+    pushed = push(kept, given, got, biased, momentum, weight, rep_tokens)
+    velocity, stepped = step(kept, given, got, biased, momentum, rep_tokens, pushed)
     arrived = lax.ppermute(pushed, "replica", ahead)
     weight_out, mixed, debiased = mix(stepped, arrived, weight, output)
     return output, mixed, weight_out, velocity, debiased

time: 130 us -> 122 us (0.938)
  the two profiles are of different devices: /device:TPU:1 before, /device:TPU:20 now
where the time goes in v5:
time: 122 us; the launch traced here: 121 us
  starting transfers between devices  53.1 us (44%)
  waiting for transfers between devices  46.6 us (38%)
  Pallas kernels  16.4 us (13%)
  blocking collectives  2.18 us (2%)
  between operations  1.36 us (1%)
    ppermute x5, starting transfers between devices, along(): return lax.ppermute(block, 'z', [(i, (i + turn) % nz) for i in range(nz)])  25.9 us
    all_to_all x1, waiting for transfers between devices, push_round(): x = lax.all_to_all(pack(tokens, ny, nz), 'z', 0, 0, tiled=True)  15.5 us
    ppermute x1, waiting for transfers between devices, push_round(): got = lax.ppermute(grad_far(kept, given), 'yh', swap)  14.2 us
    ppermute x1, waiting for transfers between devices, push_round(): far = lax.ppermute(near, 'yh', swap)  10.2 us
    pallas_call x9, Pallas kernels, call(): pl.pallas_call(kernel, in_specs=specs, out_specs=[VMEM] * len(outs), out_...  8.75 us
    ppermute x1, waiting for transfers between devices, push_round(): arrived = lax.ppermute(pushed, 'replica', ahead)  6.62 us
    all_to_all x1, starting transfers between devices, push_round(): parts = lax.all_to_all(part, 'z', 0, 0, tiled=True)  5.97 us
    ppermute x1, starting transfers between devices, push_round(): got = lax.ppermute(grad_far(kept, given), 'yh', swap)  5.96 us
  transfers between devices with their start and end apart: 11, of which 5 were waited for; matrix products, arithmetic and copies ran while one was open for 0% of the time, Pallas kernels for 12%

profile of v5, /device:TPU:20, one launch (start us, length us, event | category | flops | bytes accessed | tf_op | source)
XLA Modules:
  0.0 120.9 jit_solution(16730464514807042092)
XLA Ops:
  1.3 119.5 %conditional.1 = (f32[1,256,512]{2,1,0:T(8,128)}, f32[1]{0:T(128)}, f32[1,256,512]{2,1,0:T(8,128)}, f32[1,256,512]{2,1,0:T(8,128)}, bf16[128,512]{1,0:T(8,128)(2,1)}) conditional(s32[]{:T(128)} %clamp.3, (bf16[128,8192]{1,0:T(8,128)(2,1)}, bf16[128,512]{1,0:T(8,128)(2,1)}, f32[1]{0:T(128)}, f32[1,256,512]{2,1,0:T(8,128)}, ...), branch_computations={%region_0.1_spmd, %region_1.2_spmd, %region_2.3_spmd, %region_3.4_... | conditional | flops 250002604032 | bytes 55116460 | solution.py:292
  1.3 10.9 %collective-permute-start.27 = (bf16[128,512]{1,0:T(8,128)(2,1)}, bf16[128,512]{1,0:T(8,128)(2,1)S(1)}, u32[]{:S(2)}, u32[]{:S(2)}) collective-permute-start(bf16[128,512]{1,0:T(8,128)(2,1)} %get-tuple-element.78.first_ref), channel_id=1, source_target_pairs={{0,8},{2,10},{4,12},{6,14},{8,0},{10,2},{12,4},{14,6},{1,9},{3,11}... | collective-permute-start | bytes 393224 | tf_op jit(solution)/shard_map/cond/branch_3_fun/ppermute | solution.py:259
  12.3 2.6 %pack.7 = bf16[8,128,1024]{2,1,0:T(8,128)(2,1)} custom-call(bf16[128,8192]{1,0:T(8,128)(2,1)} %get-tuple-element.76.refs_0_.refs_1_, bf16[128,8192]{1,0:T(8,128)(2,1)} %get-tuple-element.76.refs_0_.refs_1_), custom_call_target="tpu_custom_call" | custom-call | bytes 4194304 | tf_op jit(solution)/shard_map/cond/branch_3_fun/pack/pallas_call | solution.py:56
  14.9 4.9 %all-to-all-start.6 = ((bf16[8,128,1024]{2,1,0:T(8,128)(2,1)}), bf16[8,128,1024]{2,1,0:T(8,128)(2,1)S(1)}, u32[]{:S(2)}, u32[]{:S(2)}) async-start(bf16[8,128,1024]{2,1,0:T(8,128)(2,1)} %pack.7), calls=%async_computation.6 | async-start | bytes 4194304 | tf_op jit(solution)/shard_map/cond/branch_3_fun/all_to_all | solution.py:262
  21.5 2.2 %all_gather.11.near_ref = bf16[512,512]{1,0:T(8,128)(2,1)S(1)} all-gather(bf16[256,512]{1,0:T(8,128)(2,1)S(1)} %rounded_rows.7), channel_id=1, replica_groups=mesh['replica'=16,'yh'=2,'z'=8,'core'=2] {'core'}, dimensions={0}, use_global_device_ids=true | all-gather | bytes 786432 | tf_op jit(solution)/shard_map/cond/branch_3_fun/all_gather | solution.py:268
  23.7 5.9 %collective-permute-start.28 = (bf16[512,512]{1,0:T(8,128)(2,1)S(1)}, bf16[512,512]{1,0:T(8,128)(2,1)}, u32[]{:S(2)}, u32[]{:S(2)}) collective-permute-start(bf16[512,512]{1,0:T(8,128)(2,1)S(1)} %all_gather.11.near_ref), channel_id=1, source_target_pairs={{0,16},{16,0},{1,17},{17,1},{2,18},{18,2},{3,19},{19,3},{4,20},{20... | collective-permute-start | bytes 1572872 | tf_op jit(solution)/shard_map/cond/branch_3_fun/ppermute | solution.py:269
  29.7 4.8 %collective-permute-start.29 = (bf16[128,512]{1,0:T(8,128)(2,1)S(1)}, bf16[128,512]{1,0:T(8,128)(2,1)}, u32[]{:S(2)}, u32[]{:S(2)}) collective-permute-start(bf16[128,512]{1,0:T(8,128)(2,1)S(1)} %get-tuple-element.79._), channel_id=1, source_target_pairs={{0,4},{2,6},{4,8},{6,10},{8,12},{10,14},{12,0},{14,2},{1,5},{3,7},... | collective-permute-start | bytes 393224 | tf_op jit(solution)/shard_map/cond/branch_3_fun/ppermute | solution.py:259
  34.5 3.1 %collective-permute-start.30 = (bf16[128,512]{1,0:T(8,128)(2,1)S(1)}, bf16[128,512]{1,0:T(8,128)(2,1)}, u32[]{:S(2)}, u32[]{:S(2)}) collective-permute-start(bf16[128,512]{1,0:T(8,128)(2,1)S(1)} %get-tuple-element.79._), channel_id=1, source_target_pairs={{0,12},{2,14},{4,0},{6,2},{8,4},{10,6},{12,8},{14,10},{1,13},{3,15... | collective-permute-start | bytes 393224 | tf_op jit(solution)/shard_map/cond/branch_3_fun/ppermute | solution.py:259
  37.6 3.9 %collective-permute-start.31 = (bf16[256,512]{1,0:T(8,128)(2,1)S(1)}, bf16[256,512]{1,0:T(8,128)(2,1)S(1)}, u32[]{:S(2)}, u32[]{:S(2)}) collective-permute-start(bf16[256,512]{1,0:T(8,128)(2,1)S(1)} %get-tuple-element.81.refs_0_), channel_id=1, source_target_pairs={{0,2},{2,4},{4,6},{6,8},{8,10},{10,12},{12,14},{14,0},{1,3},{3,5},... | collective-permute-start | bytes 786440 | tf_op jit(solution)/shard_map/cond/branch_3_fun/ppermute | solution.py:259
  41.6 3.1 %collective-permute-start.32 = (bf16[256,512]{1,0:T(8,128)(2,1)S(1)}, bf16[256,512]{1,0:T(8,128)(2,1)S(1)}, u32[]{:S(2)}, u32[]{:S(2)}) collective-permute-start(bf16[256,512]{1,0:T(8,128)(2,1)S(1)} %get-tuple-element.81.refs_0_), channel_id=1, source_target_pairs={{0,14},{2,0},{4,2},{6,4},{8,6},{10,8},{12,10},{14,12},{1,15},{3,1}... | collective-permute-start | bytes 786440 | tf_op jit(solution)/shard_map/cond/branch_3_fun/ppermute | solution.py:259
  44.7 10.2 %collective-permute-done.28.far_ref = bf16[512,512]{1,0:T(8,128)(2,1)} collective-permute-done((bf16[512,512]{1,0:T(8,128)(2,1)S(1)}, bf16[512,512]{1,0:T(8,128)(2,1)}, u32[]{:S(2)}, u32[]{:S(2)}) %collective-permute-start.28) | collective-permute-done | bytes 524320 | tf_op jit(solution)/shard_map/cond/branch_3_fun/ppermute | solution.py:269
  54.9 15.5 %all-to-all-done.6.x_ref = bf16[8,128,1024]{2,1,0:T(8,128)(2,1)S(1)} async-done(((bf16[8,128,1024]{2,1,0:T(8,128)(2,1)}), bf16[8,128,1024]{2,1,0:T(8,128)(2,1)S(1)}, u32[]{:S(2)}, u32[]{:S(2)}) %all-to-all-start.6) | async-done | bytes 2097184 | tf_op jit(solution)/shard_map/cond/branch_3_fun/all_to_all | solution.py:262
  70.4 3.3 %out_part.7.refs_3_ = bf16[8,128,512]{2,1,0:T(8,128)(2,1)} custom-call(s32[3]{0:T(128)S(1)} %pad_add_fusion.3.place_ref, bf16[8,128,1024]{2,1,0:T(8,128)(2,1)S(1)} %all-to-all-done.6.x_ref, bf16[512,512]{1,0:T(8,128)(2,1)S(1)} %all_gather.11.near_ref, bf16[512,512]{1,0:T(8,128)(2,1)} %collective-permute-done.28.far_ref), custom_call_target="tpu_custom_call" | custom-call | flops 49999998976 | bytes 4194304 | tf_op jit(solution)/shard_map/cond/branch_3_fun/out_part/pallas_call | solution.py:105
  73.7 6.0 %all-to-all-start.7 = ((bf16[8,128,512]{2,1,0:T(8,128)(2,1)}), bf16[8,128,512]{2,1,0:T(8,128)(2,1)}, u32[]{:S(2)}, u32[]{:S(2)}) async-start(bf16[8,128,512]{2,1,0:T(8,128)(2,1)} %out_part.7.refs_3_), calls=%async_computation.7 | async-start | bytes 2097152 | tf_op jit(solution)/shard_map/cond/branch_3_fun/all_to_all | solution.py:271
  79.7 1.5 %grad_first.7.refs_2_ = f32[2,256,512]{2,1,0:T(8,128)S(1)} custom-call(s32[3]{0:T(128)S(1)} %pad_add_fusion.3.place_ref, bf16[8,128,1024]{2,1,0:T(8,128)(2,1)S(1)} %all-to-all-done.6.x_ref, bf16[256,512]{1,0:T(8,128)(2,1)S(1)} %get-tuple-element.81.refs_0_, bf16[128,512]{1,0:T(8,128)(2,1)} %collective-permute-done.29.refs_1_, ...), custom_call_target="tpu_custom_call" | custom-call | flops 49999998976 | bytes 3145728 | tf_op jit(solution)/shard_map/cond/branch_3_fun/grad_first/pallas_call | solution.py:23
  81.1 1.0 grad_sent.7
  82.2 2.1 %collective-permute-start.33 = (bf16[2,256,512]{2,1,0:T(8,128)(2,1)S(1)}, bf16[2,256,512]{2,1,0:T(8,128)(2,1)S(1)}, u32[]{:S(2)}, u32[]{:S(2)}) collective-permute-start(bf16[2,256,512]{2,1,0:T(8,128)(2,1)S(1)} %grad_sent.7), channel_id=1, source_target_pairs={{0,1},{1,0},{2,3},{3,2},{4,5},{5,4},{6,7},{7,6},{8,9},{9,8},{10,11... | collective-permute-start | bytes 1572872 | tf_op jit(solution)/shard_map/cond/branch_3_fun/ppermute | solution.py:276
  84.2 1.7 %grad_kept.7.kept_ref = f32[2,256,512]{2,1,0:T(8,128)S(1)} custom-call(s32[3]{0:T(128)S(1)} %pad_add_fusion.3.place_ref, bf16[8,128,1024]{2,1,0:T(8,128)(2,1)S(1)} %all-to-all-done.6.x_ref, bf16[256,512]{1,0:T(8,128)(2,1)S(1)} %get-tuple-element.81.refs_0_, bf16[128,512]{1,0:T(8,128)(2,1)} %collective-permute-done.29.refs_1_, ...), custom_call_target="tpu_custom_call" | custom-call | bytes 3145728 | tf_op jit(solution)/shard_map/cond/branch_3_fun/grad_kept/pallas_call | solution.py:23
  86.2 6.0 %collective-permute-start.34 = (bf16[256,512]{1,0:T(8,128)(2,1)S(1)}, bf16[256,512]{1,0:T(8,128)(2,1)S(1)}, u32[]{:S(2)}, u32[]{:S(2)}) collective-permute-start(bf16[256,512]{1,0:T(8,128)(2,1)S(1)} %grad_far.7), channel_id=1, source_target_pairs={{0,16},{16,0},{1,17},{17,1},{2,18},{18,2},{3,19},{19,3},{4,20},{20... | collective-permute-start | bytes 786440 | tf_op jit(solution)/shard_map/cond/branch_3_fun/ppermute | solution.py:278
  92.1 14.2 %collective-permute-done.34.got_ref = bf16[256,512]{1,0:T(8,128)(2,1)S(1)} collective-permute-done((bf16[256,512]{1,0:T(8,128)(2,1)S(1)}, bf16[256,512]{1,0:T(8,128)(2,1)S(1)}, u32[]{:S(2)}, u32[]{:S(2)}) %collective-permute-start.34) | collective-permute-done | bytes 262176 | tf_op jit(solution)/shard_map/cond/branch_3_fun/ppermute | solution.py:278
  107.2 2.4 %collective-permute-start.35 = (bf16[272,512]{1,0:T(8,128)(2,1)S(1)}, bf16[272,512]{1,0:T(8,128)(2,1)S(1)}, u32[]{:S(2)}, u32[]{:S(2)}) collective-permute-start(bf16[272,512]{1,0:T(8,128)(2,1)S(1)} %push.7._), channel_id=1, source_target_pairs={{256,0},{288,32},{320,64},{352,96},{384,128},{416,160},{448,192},{... | collective-permute-start | bytes 835592 | tf_op jit(solution)/shard_map/cond/branch_3_fun/ppermute | solution.py:283
  110.5 2.0 %sum_parts.7._ = bf16[128,512]{1,0:T(8,128)(2,1)} custom-call(bf16[8,128,512]{2,1,0:T(8,128)(2,1)} %all-to-all-done.7.parts_ref), custom_call_target="tpu_custom_call" | custom-call | flops 524288 | bytes 1048576 | tf_op jit(solution)/shard_map/cond/branch_3_fun/sum_parts/pallas_call | solution.py:23
  112.5 6.6 %collective-permute-done.35.a.tail = bf16[272,512]{1,0:T(8,128)(2,1)S(1)} collective-permute-done((bf16[272,512]{1,0:T(8,128)(2,1)S(1)}, bf16[272,512]{1,0:T(8,128)(2,1)S(1)}, u32[]{:S(2)}, u32[]{:S(2)}) %collective-permute-start.35) | collective-permute-done | bytes 278560 | tf_op jit(solution)/shard_map/cond/branch_3_fun/ppermute | solution.py:283
  119.1 1.7 %mix.7 = (f32[1]{0:T(128)}, f32[1,256,512]{2,1,0:T(8,128)}, f32[1,256,512]{2,1,0:T(8,128)}) custom-call(f32[1]{0:T(128)} %get-tuple-element.77.weight_ref.w_ref, bf16[128,512]{1,0:T(8,128)(2,1)} %sum_parts.7._, f32[256,512]{1,0:T(8,128)S(1)} %get-tuple-element.83.s, bf16[272,512]{1,0:T(8,128)(2,1)S(1)} %collective-permute-done.35.a.tail, ...), custom_call_target="tpu_custom_call" | custom-call | flops 786432 | bytes 2883584 | tf_op jit(solution)/shard_map/cond/branch_3_fun/mix/pallas_call | solution.py:225
  (21 shorter events, 3.8 us)
Async XLA Ops:
  1.3 18.4 %collective-permute-start.27 = (bf16[128,512]{1,0:T(8,128)(2,1)}, bf16[128,512]{1,0:T(8,128)(2,1)S(1)}, u32[]{:S(2)}, u32[]{:S(2)}) collective-permute-start(bf16[128,512]{1,0:T(8,128)(2,1)} %get-tuple-element.78.first_ref), channel_id=1, source_target_pairs={{0,8},{2,10},{4,12},{6,14},{8,0},{10,2},{12,4},{14,6},{1,9},{3,11}... | collective-permute-start | bytes 393224 | tf_op jit(solution)/shard_map/cond/branch_3_fun/ppermute | solution.py:259
  14.9 4.9 %copy-start.15 = (bf16[128,512]{1,0:T(8,128)(2,1)S(1)}, bf16[128,512]{1,0:T(8,128)(2,1)}, u32[]{:S(2)}) copy-start(bf16[128,512]{1,0:T(8,128)(2,1)} %get-tuple-element.78.first_ref) | copy-start | bytes 393220 | tf_op jit(solution)/shard_map/cond
  14.9 55.5 %all-to-all-start.6 = ((bf16[8,128,1024]{2,1,0:T(8,128)(2,1)}), bf16[8,128,1024]{2,1,0:T(8,128)(2,1)S(1)}, u32[]{:S(2)}, u32[]{:S(2)}) async-start(bf16[8,128,1024]{2,1,0:T(8,128)(2,1)} %pack.7), calls=%async_computation.6 | async-start | bytes 4194304 | tf_op jit(solution)/shard_map/cond/branch_3_fun/all_to_all | solution.py:262
  19.7 1.0 copy-start.6
  23.7 31.2 %collective-permute-start.28 = (bf16[512,512]{1,0:T(8,128)(2,1)S(1)}, bf16[512,512]{1,0:T(8,128)(2,1)}, u32[]{:S(2)}, u32[]{:S(2)}) collective-permute-start(bf16[512,512]{1,0:T(8,128)(2,1)S(1)} %all_gather.11.near_ref), channel_id=1, source_target_pairs={{0,16},{16,0},{1,17},{17,1},{2,18},{18,2},{3,19},{19,3},{4,20},{20... | collective-permute-start | bytes 1572872 | tf_op jit(solution)/shard_map/cond/branch_3_fun/ppermute | solution.py:269
  29.7 50.0 %collective-permute-start.29 = (bf16[128,512]{1,0:T(8,128)(2,1)S(1)}, bf16[128,512]{1,0:T(8,128)(2,1)}, u32[]{:S(2)}, u32[]{:S(2)}) collective-permute-start(bf16[128,512]{1,0:T(8,128)(2,1)S(1)} %get-tuple-element.79._), channel_id=1, source_target_pairs={{0,4},{2,6},{4,8},{6,10},{8,12},{10,14},{12,0},{14,2},{1,5},{3,7},... | collective-permute-start | bytes 393224 | tf_op jit(solution)/shard_map/cond/branch_3_fun/ppermute | solution.py:259
  34.5 45.1 %collective-permute-start.30 = (bf16[128,512]{1,0:T(8,128)(2,1)S(1)}, bf16[128,512]{1,0:T(8,128)(2,1)}, u32[]{:S(2)}, u32[]{:S(2)}) collective-permute-start(bf16[128,512]{1,0:T(8,128)(2,1)S(1)} %get-tuple-element.79._), channel_id=1, source_target_pairs={{0,12},{2,14},{4,0},{6,2},{8,4},{10,6},{12,8},{14,10},{1,13},{3,15... | collective-permute-start | bytes 393224 | tf_op jit(solution)/shard_map/cond/branch_3_fun/ppermute | solution.py:259
  37.6 43.5 %collective-permute-start.31 = (bf16[256,512]{1,0:T(8,128)(2,1)S(1)}, bf16[256,512]{1,0:T(8,128)(2,1)S(1)}, u32[]{:S(2)}, u32[]{:S(2)}) collective-permute-start(bf16[256,512]{1,0:T(8,128)(2,1)S(1)} %get-tuple-element.81.refs_0_), channel_id=1, source_target_pairs={{0,2},{2,4},{4,6},{6,8},{8,10},{10,12},{12,14},{14,0},{1,3},{3,5},... | collective-permute-start | bytes 786440 | tf_op jit(solution)/shard_map/cond/branch_3_fun/ppermute | solution.py:259
  41.6 39.6 %collective-permute-start.32 = (bf16[256,512]{1,0:T(8,128)(2,1)S(1)}, bf16[256,512]{1,0:T(8,128)(2,1)S(1)}, u32[]{:S(2)}, u32[]{:S(2)}) collective-permute-start(bf16[256,512]{1,0:T(8,128)(2,1)S(1)} %get-tuple-element.81.refs_0_), channel_id=1, source_target_pairs={{0,14},{2,0},{4,2},{6,4},{8,6},{10,8},{12,10},{14,12},{1,15},{3,1}... | collective-permute-start | bytes 786440 | tf_op jit(solution)/shard_map/cond/branch_3_fun/ppermute | solution.py:259
  73.7 36.8 %all-to-all-start.7 = ((bf16[8,128,512]{2,1,0:T(8,128)(2,1)}), bf16[8,128,512]{2,1,0:T(8,128)(2,1)}, u32[]{:S(2)}, u32[]{:S(2)}) async-start(bf16[8,128,512]{2,1,0:T(8,128)(2,1)} %out_part.7.refs_3_), calls=%async_computation.7 | async-start | bytes 2097152 | tf_op jit(solution)/shard_map/cond/branch_3_fun/all_to_all | solution.py:271
  82.2 24.1 %copy-start.7 = (f32[1,256,512]{2,1,0:T(8,128)S(1)}, f32[1,256,512]{2,1,0:T(8,128)}, u32[]{:S(2)}) copy-start(f32[1,256,512]{2,1,0:T(8,128)} %get-tuple-element.80.numer) | copy-start | bytes 1572868 | tf_op jit(solution)/shard_map/cond
  82.2 24.1 %copy-start.11 = (f32[1,256,512]{2,1,0:T(8,128)S(1)}, f32[1,256,512]{2,1,0:T(8,128)}, u32[]{:S(2)}) copy-start(f32[1,256,512]{2,1,0:T(8,128)} %get-tuple-element.82.moment) | copy-start | bytes 1572868 | tf_op jit(solution)/shard_map/cond
  82.2 3.9 %collective-permute-start.33 = (bf16[2,256,512]{2,1,0:T(8,128)(2,1)S(1)}, bf16[2,256,512]{2,1,0:T(8,128)(2,1)S(1)}, u32[]{:S(2)}, u32[]{:S(2)}) collective-permute-start(bf16[2,256,512]{2,1,0:T(8,128)(2,1)S(1)} %grad_sent.7), channel_id=1, source_target_pairs={{0,1},{1,0},{2,3},{3,2},{4,5},{5,4},{6,7},{7,6},{8,9},{9,8},{10,11... | collective-permute-start | bytes 1572872 | tf_op jit(solution)/shard_map/cond/branch_3_fun/ppermute | solution.py:276
  86.2 20.1 %collective-permute-start.34 = (bf16[256,512]{1,0:T(8,128)(2,1)S(1)}, bf16[256,512]{1,0:T(8,128)(2,1)S(1)}, u32[]{:S(2)}, u32[]{:S(2)}) collective-permute-start(bf16[256,512]{1,0:T(8,128)(2,1)S(1)} %grad_far.7), channel_id=1, source_target_pairs={{0,16},{16,0},{1,17},{17,1},{2,18},{18,2},{3,19},{19,3},{4,20},{20... | collective-permute-start | bytes 786440 | tf_op jit(solution)/shard_map/cond/branch_3_fun/ppermute | solution.py:278
  107.2 12.0 %collective-permute-start.35 = (bf16[272,512]{1,0:T(8,128)(2,1)S(1)}, bf16[272,512]{1,0:T(8,128)(2,1)S(1)}, u32[]{:S(2)}, u32[]{:S(2)}) collective-permute-start(bf16[272,512]{1,0:T(8,128)(2,1)S(1)} %push.7._), channel_id=1, source_target_pairs={{256,0},{288,32},{320,64},{352,96},{384,128},{416,160},{448,192},{... | collective-permute-start | bytes 835592 | tf_op jit(solution)/shard_map/cond/branch_3_fun/ppermute | solution.py:283

commit v6 on v5

--- a/solution.py
+++ b/solution.py
@@ -287,7 +287,7 @@
 
 def shards(tokens, cotangent, biased, momentum, weight, round_index):
     hops = lax.axis_size("replica").bit_length() - 1
-    power = round_index[0] % hops
+    power = round_index[0] & (hops - 1)
     branches = [partial(push_round, 1 << level) for level in range(hops)]
     return lax.switch(power, branches, tokens, cotangent, biased, momentum, weight)
 

time: 122 us -> 122 us (level)
  the two profiles are of different devices: /device:TPU:20 before, /device:TPU:96 now
where the time goes in v6:
time: 122 us; the launch traced here: 121 us
  waiting for transfers between devices  58.1 us (48%)
  starting transfers between devices  41.8 us (34%)
  Pallas kernels  16.4 us (13%)
  blocking collectives  2.18 us (2%)
  between operations  1.36 us (1%)
    ppermute x5, starting transfers between devices, along(): return lax.ppermute(block, 'z', [(i, (i + turn) % nz) for i in range(nz)])  23.8 us
    ppermute x1, waiting for transfers between devices, push_round(): got = lax.ppermute(grad_far(kept, given), 'yh', swap)  18 us
    all_to_all x1, waiting for transfers between devices, push_round(): x = lax.all_to_all(pack(tokens, ny, nz), 'z', 0, 0, tiled=True)  17.7 us
    ppermute x1, waiting for transfers between devices, push_round(): far = lax.ppermute(near, 'yh', swap)  15.2 us
    pallas_call x9, Pallas kernels, call(): pl.pallas_call(kernel, in_specs=specs, out_specs=[VMEM] * len(outs), out_...  8.77 us
    ppermute x1, waiting for transfers between devices, push_round(): arrived = lax.ppermute(pushed, 'replica', ahead)  7 us
    all_to_all x1, starting transfers between devices, push_round(): x = lax.all_to_all(pack(tokens, ny, nz), 'z', 0, 0, tiled=True)  5.25 us
    all_to_all x1, starting transfers between devices, push_round(): parts = lax.all_to_all(part, 'z', 0, 0, tiled=True)  4.2 us
  transfers between devices with their start and end apart: 11, of which 5 were waited for; matrix products, arithmetic and copies ran while one was open for 0% of the time, Pallas kernels for 12%

profile of v6, /device:TPU:96, one launch (start us, length us, event | category | flops | bytes accessed | tf_op | source)
XLA Modules:
  0.0 121.1 jit_solution(518168499330822255)
XLA Ops:
  1.3 119.7 %conditional.1 = (f32[1,256,512]{2,1,0:T(8,128)}, f32[1]{0:T(128)}, f32[1,256,512]{2,1,0:T(8,128)}, f32[1,256,512]{2,1,0:T(8,128)}, bf16[128,512]{1,0:T(8,128)(2,1)}) conditional(s32[]{:T(128)} %bitcast.12, (bf16[128,8192]{1,0:T(8,128)(2,1)}, bf16[128,512]{1,0:T(8,128)(2,1)}, f32[1]{0:T(128)}, ...), branch_computations={%region_0.0_spmd, %region_1.0_spmd, %region_2.0_spmd, %region_3.0_... | conditional | flops 250002604032 | bytes 55116460 | solution.py:292
  1.3 10.0 %collective-permute-start = (bf16[128,512]{1,0:T(8,128)(2,1)}, bf16[128,512]{1,0:T(8,128)(2,1)S(1)}, u32[]{:S(2)}, u32[]{:S(2)}) collective-permute-start(bf16[128,512]{1,0:T(8,128)(2,1)} %get-tuple-element.42.first_ref), channel_id=1, source_target_pairs={{0,8},{2,10},{4,12},{6,14},{8,0},{10,2},{12,4},{14,6},{1,9},{3,11}... | collective-permute-start | bytes 393224 | tf_op jit(solution)/shard_map/cond/branch_0_fun/ppermute | solution.py:259
  11.3 2.6 %pack.4 = bf16[8,128,1024]{2,1,0:T(8,128)(2,1)} custom-call(bf16[128,8192]{1,0:T(8,128)(2,1)} %get-tuple-element.40.refs_0_.refs_1_, bf16[128,8192]{1,0:T(8,128)(2,1)} %get-tuple-element.40.refs_0_.refs_1_), custom_call_target="tpu_custom_call" | custom-call | bytes 4194304 | tf_op jit(solution)/shard_map/cond/branch_0_fun/pack/pallas_call | solution.py:56
  13.9 5.2 %all-to-all-start = ((bf16[8,128,1024]{2,1,0:T(8,128)(2,1)}), bf16[8,128,1024]{2,1,0:T(8,128)(2,1)S(1)}, u32[]{:S(2)}, u32[]{:S(2)}) async-start(bf16[8,128,1024]{2,1,0:T(8,128)(2,1)} %pack.4), calls=%async_computation | async-start | bytes 4194304 | tf_op jit(solution)/shard_map/cond/branch_0_fun/all_to_all | solution.py:262
  20.9 2.2 %all_gather.8.near_ref = bf16[512,512]{1,0:T(8,128)(2,1)S(1)} all-gather(bf16[256,512]{1,0:T(8,128)(2,1)S(1)} %rounded_rows.4), channel_id=1, replica_groups=mesh['replica'=16,'yh'=2,'z'=8,'core'=2] {'core'}, dimensions={0}, use_global_device_ids=true | all-gather | bytes 786432 | tf_op jit(solution)/shard_map/cond/branch_0_fun/all_gather | solution.py:268
  23.1 2.0 %collective-permute-start.1 = (bf16[512,512]{1,0:T(8,128)(2,1)S(1)}, bf16[512,512]{1,0:T(8,128)(2,1)}, u32[]{:S(2)}, u32[]{:S(2)}) collective-permute-start(bf16[512,512]{1,0:T(8,128)(2,1)S(1)} %all_gather.8.near_ref), channel_id=1, source_target_pairs={{0,16},{16,0},{1,17},{17,1},{2,18},{18,2},{3,19},{19,3},{4,20},{20... | collective-permute-start | bytes 1572872 | tf_op jit(solution)/shard_map/cond/branch_0_fun/ppermute | solution.py:269
  25.2 4.3 %collective-permute-start.2 = (bf16[128,512]{1,0:T(8,128)(2,1)S(1)}, bf16[128,512]{1,0:T(8,128)(2,1)}, u32[]{:S(2)}, u32[]{:S(2)}) collective-permute-start(bf16[128,512]{1,0:T(8,128)(2,1)S(1)} %get-tuple-element.43._), channel_id=1, source_target_pairs={{0,4},{2,6},{4,8},{6,10},{8,12},{10,14},{12,0},{14,2},{1,5},{3,7},... | collective-permute-start | bytes 393224 | tf_op jit(solution)/shard_map/cond/branch_0_fun/ppermute | solution.py:259
  29.5 3.7 %collective-permute-start.3 = (bf16[128,512]{1,0:T(8,128)(2,1)S(1)}, bf16[128,512]{1,0:T(8,128)(2,1)}, u32[]{:S(2)}, u32[]{:S(2)}) collective-permute-start(bf16[128,512]{1,0:T(8,128)(2,1)S(1)} %get-tuple-element.43._), channel_id=1, source_target_pairs={{0,12},{2,14},{4,0},{6,2},{8,4},{10,6},{12,8},{14,10},{1,13},{3,15... | collective-permute-start | bytes 393224 | tf_op jit(solution)/shard_map/cond/branch_0_fun/ppermute | solution.py:259
  33.2 2.8 %collective-permute-start.4 = (bf16[256,512]{1,0:T(8,128)(2,1)S(1)}, bf16[256,512]{1,0:T(8,128)(2,1)S(1)}, u32[]{:S(2)}, u32[]{:S(2)}) collective-permute-start(bf16[256,512]{1,0:T(8,128)(2,1)S(1)} %get-tuple-element.45.refs_0_), channel_id=1, source_target_pairs={{0,2},{2,4},{4,6},{6,8},{8,10},{10,12},{12,14},{14,0},{1,3},{3,5},... | collective-permute-start | bytes 786440 | tf_op jit(solution)/shard_map/cond/branch_0_fun/ppermute | solution.py:259
  36.0 3.0 %collective-permute-start.5 = (bf16[256,512]{1,0:T(8,128)(2,1)S(1)}, bf16[256,512]{1,0:T(8,128)(2,1)S(1)}, u32[]{:S(2)}, u32[]{:S(2)}) collective-permute-start(bf16[256,512]{1,0:T(8,128)(2,1)S(1)} %get-tuple-element.45.refs_0_), channel_id=1, source_target_pairs={{0,14},{2,0},{4,2},{6,4},{8,6},{10,8},{12,10},{14,12},{1,15},{3,1}... | collective-permute-start | bytes 786440 | tf_op jit(solution)/shard_map/cond/branch_0_fun/ppermute | solution.py:259
  39.0 15.2 %collective-permute-done.1.far_ref = bf16[512,512]{1,0:T(8,128)(2,1)} collective-permute-done((bf16[512,512]{1,0:T(8,128)(2,1)S(1)}, bf16[512,512]{1,0:T(8,128)(2,1)}, u32[]{:S(2)}, u32[]{:S(2)}) %collective-permute-start.1) | collective-permute-done | bytes 524320 | tf_op jit(solution)/shard_map/cond/branch_0_fun/ppermute | solution.py:269
  54.3 17.7 %all-to-all-done.x_ref = bf16[8,128,1024]{2,1,0:T(8,128)(2,1)S(1)} async-done(((bf16[8,128,1024]{2,1,0:T(8,128)(2,1)}), bf16[8,128,1024]{2,1,0:T(8,128)(2,1)S(1)}, u32[]{:S(2)}, u32[]{:S(2)}) %all-to-all-start) | async-done | bytes 2097184 | tf_op jit(solution)/shard_map/cond/branch_0_fun/all_to_all | solution.py:262
  72.0 3.3 %out_part.4.refs_3_ = bf16[8,128,512]{2,1,0:T(8,128)(2,1)} custom-call(s32[3]{0:T(128)S(1)} %pad_add_fusion.place_ref, bf16[8,128,1024]{2,1,0:T(8,128)(2,1)S(1)} %all-to-all-done.x_ref, bf16[512,512]{1,0:T(8,128)(2,1)S(1)} %all_gather.8.near_ref, bf16[512,512]{1,0:T(8,128)(2,1)} %collective-permute-done.1.far_ref), custom_call_target="tpu_custom_call" | custom-call | flops 49999998976 | bytes 4194304 | tf_op jit(solution)/shard_map/cond/branch_0_fun/out_part/pallas_call | solution.py:105
  75.3 4.2 %all-to-all-start.1 = ((bf16[8,128,512]{2,1,0:T(8,128)(2,1)}), bf16[8,128,512]{2,1,0:T(8,128)(2,1)}, u32[]{:S(2)}, u32[]{:S(2)}) async-start(bf16[8,128,512]{2,1,0:T(8,128)(2,1)} %out_part.4.refs_3_), calls=%async_computation.1 | async-start | bytes 2097152 | tf_op jit(solution)/shard_map/cond/branch_0_fun/all_to_all | solution.py:271
  79.5 1.5 %grad_first.4.refs_2_ = f32[2,256,512]{2,1,0:T(8,128)S(1)} custom-call(s32[3]{0:T(128)S(1)} %pad_add_fusion.place_ref, bf16[8,128,1024]{2,1,0:T(8,128)(2,1)S(1)} %all-to-all-done.x_ref, bf16[256,512]{1,0:T(8,128)(2,1)S(1)} %get-tuple-element.45.refs_0_, bf16[128,512]{1,0:T(8,128)(2,1)} %collective-permute-done.2.refs_1_, ...), custom_call_target="tpu_custom_call" | custom-call | flops 49999998976 | bytes 3145728 | tf_op jit(solution)/shard_map/cond/branch_0_fun/grad_first/pallas_call | solution.py:23
  81.0 1.0 grad_sent.4
  82.1 2.1 %collective-permute-start.6 = (bf16[2,256,512]{2,1,0:T(8,128)(2,1)S(1)}, bf16[2,256,512]{2,1,0:T(8,128)(2,1)S(1)}, u32[]{:S(2)}, u32[]{:S(2)}) collective-permute-start(bf16[2,256,512]{2,1,0:T(8,128)(2,1)S(1)} %grad_sent.4), channel_id=1, source_target_pairs={{0,1},{1,0},{2,3},{3,2},{4,5},{5,4},{6,7},{7,6},{8,9},{9,8},{10,11... | collective-permute-start | bytes 1572872 | tf_op jit(solution)/shard_map/cond/branch_0_fun/ppermute | solution.py:276
  84.2 1.7 %grad_kept.4.kept_ref = f32[2,256,512]{2,1,0:T(8,128)S(1)} custom-call(s32[3]{0:T(128)S(1)} %pad_add_fusion.place_ref, bf16[8,128,1024]{2,1,0:T(8,128)(2,1)S(1)} %all-to-all-done.x_ref, bf16[256,512]{1,0:T(8,128)(2,1)S(1)} %get-tuple-element.45.refs_0_, bf16[128,512]{1,0:T(8,128)(2,1)} %collective-permute-done.2.refs_1_, ...), custom_call_target="tpu_custom_call" | custom-call | bytes 3145728 | tf_op jit(solution)/shard_map/cond/branch_0_fun/grad_kept/pallas_call | solution.py:23
  86.1 2.0 %collective-permute-start.7 = (bf16[256,512]{1,0:T(8,128)(2,1)S(1)}, bf16[256,512]{1,0:T(8,128)(2,1)S(1)}, u32[]{:S(2)}, u32[]{:S(2)}) collective-permute-start(bf16[256,512]{1,0:T(8,128)(2,1)S(1)} %grad_far.4), channel_id=1, source_target_pairs={{0,16},{16,0},{1,17},{17,1},{2,18},{18,2},{3,19},{19,3},{4,20},{20... | collective-permute-start | bytes 786440 | tf_op jit(solution)/shard_map/cond/branch_0_fun/ppermute | solution.py:278
  88.1 18.0 %collective-permute-done.7.got_ref = bf16[256,512]{1,0:T(8,128)(2,1)S(1)} collective-permute-done((bf16[256,512]{1,0:T(8,128)(2,1)S(1)}, bf16[256,512]{1,0:T(8,128)(2,1)S(1)}, u32[]{:S(2)}, u32[]{:S(2)}) %collective-permute-start.7) | collective-permute-done | bytes 262176 | tf_op jit(solution)/shard_map/cond/branch_0_fun/ppermute | solution.py:278
  107.0 2.4 %collective-permute-start.8 = (bf16[272,512]{1,0:T(8,128)(2,1)S(1)}, bf16[272,512]{1,0:T(8,128)(2,1)S(1)}, u32[]{:S(2)}, u32[]{:S(2)}) collective-permute-start(bf16[272,512]{1,0:T(8,128)(2,1)S(1)} %push.4._), channel_id=1, source_target_pairs={{480,0},{0,32},{32,64},{64,96},{96,128},{128,160},{160,192},{192,2... | collective-permute-start | bytes 835592 | tf_op jit(solution)/shard_map/cond/branch_0_fun/ppermute | solution.py:283
  110.3 2.0 %sum_parts.4._ = bf16[128,512]{1,0:T(8,128)(2,1)} custom-call(bf16[8,128,512]{2,1,0:T(8,128)(2,1)} %all-to-all-done.1.parts_ref), custom_call_target="tpu_custom_call" | custom-call | flops 524288 | bytes 1048576 | tf_op jit(solution)/shard_map/cond/branch_0_fun/sum_parts/pallas_call | solution.py:23
  112.3 7.0 %collective-permute-done.8.a.tail = bf16[272,512]{1,0:T(8,128)(2,1)S(1)} collective-permute-done((bf16[272,512]{1,0:T(8,128)(2,1)S(1)}, bf16[272,512]{1,0:T(8,128)(2,1)S(1)}, u32[]{:S(2)}, u32[]{:S(2)}) %collective-permute-start.8) | collective-permute-done | bytes 278560 | tf_op jit(solution)/shard_map/cond/branch_0_fun/ppermute | solution.py:283
  119.3 1.7 %mix.4 = (f32[1]{0:T(128)}, f32[1,256,512]{2,1,0:T(8,128)}, f32[1,256,512]{2,1,0:T(8,128)}) custom-call(f32[1]{0:T(128)} %get-tuple-element.41.weight_ref.w_ref, bf16[128,512]{1,0:T(8,128)(2,1)} %sum_parts.4._, f32[256,512]{1,0:T(8,128)S(1)} %get-tuple-element.47.s, bf16[272,512]{1,0:T(8,128)(2,1)S(1)} %collective-permute-done.8.a.tail, ...), custom_call_target="tpu_custom_call" | custom-call | flops 786432 | bytes 2883584 | tf_op jit(solution)/shard_map/cond/branch_0_fun/mix/pallas_call | solution.py:225
  (21 shorter events, 3.8 us)
Async XLA Ops:
  1.3 17.9 %collective-permute-start = (bf16[128,512]{1,0:T(8,128)(2,1)}, bf16[128,512]{1,0:T(8,128)(2,1)S(1)}, u32[]{:S(2)}, u32[]{:S(2)}) collective-permute-start(bf16[128,512]{1,0:T(8,128)(2,1)} %get-tuple-element.42.first_ref), channel_id=1, source_target_pairs={{0,8},{2,10},{4,12},{6,14},{8,0},{10,2},{12,4},{14,6},{1,9},{3,11}... | collective-permute-start | bytes 393224 | tf_op jit(solution)/shard_map/cond/branch_0_fun/ppermute | solution.py:259
  13.9 5.3 %copy-start.12 = (bf16[128,512]{1,0:T(8,128)(2,1)S(1)}, bf16[128,512]{1,0:T(8,128)(2,1)}, u32[]{:S(2)}) copy-start(bf16[128,512]{1,0:T(8,128)(2,1)} %get-tuple-element.42.first_ref) | copy-start | bytes 393220 | tf_op jit(solution)/shard_map/cond
  13.9 58.1 %all-to-all-start = ((bf16[8,128,1024]{2,1,0:T(8,128)(2,1)}), bf16[8,128,1024]{2,1,0:T(8,128)(2,1)S(1)}, u32[]{:S(2)}, u32[]{:S(2)}) async-start(bf16[8,128,1024]{2,1,0:T(8,128)(2,1)} %pack.4), calls=%async_computation | async-start | bytes 4194304 | tf_op jit(solution)/shard_map/cond/branch_0_fun/all_to_all | solution.py:262
  19.2 1.0 copy-start
  23.1 31.2 %collective-permute-start.1 = (bf16[512,512]{1,0:T(8,128)(2,1)S(1)}, bf16[512,512]{1,0:T(8,128)(2,1)}, u32[]{:S(2)}, u32[]{:S(2)}) collective-permute-start(bf16[512,512]{1,0:T(8,128)(2,1)S(1)} %all_gather.8.near_ref), channel_id=1, source_target_pairs={{0,16},{16,0},{1,17},{17,1},{2,18},{18,2},{3,19},{19,3},{4,20},{20... | collective-permute-start | bytes 1572872 | tf_op jit(solution)/shard_map/cond/branch_0_fun/ppermute | solution.py:269
  25.2 54.3 %collective-permute-start.2 = (bf16[128,512]{1,0:T(8,128)(2,1)S(1)}, bf16[128,512]{1,0:T(8,128)(2,1)}, u32[]{:S(2)}, u32[]{:S(2)}) collective-permute-start(bf16[128,512]{1,0:T(8,128)(2,1)S(1)} %get-tuple-element.43._), channel_id=1, source_target_pairs={{0,4},{2,6},{4,8},{6,10},{8,12},{10,14},{12,0},{14,2},{1,5},{3,7},... | collective-permute-start | bytes 393224 | tf_op jit(solution)/shard_map/cond/branch_0_fun/ppermute | solution.py:259
  29.5 50.1 %collective-permute-start.3 = (bf16[128,512]{1,0:T(8,128)(2,1)S(1)}, bf16[128,512]{1,0:T(8,128)(2,1)}, u32[]{:S(2)}, u32[]{:S(2)}) collective-permute-start(bf16[128,512]{1,0:T(8,128)(2,1)S(1)} %get-tuple-element.43._), channel_id=1, source_target_pairs={{0,12},{2,14},{4,0},{6,2},{8,4},{10,6},{12,8},{14,10},{1,13},{3,15... | collective-permute-start | bytes 393224 | tf_op jit(solution)/shard_map/cond/branch_0_fun/ppermute | solution.py:259
  33.2 47.9 %collective-permute-start.4 = (bf16[256,512]{1,0:T(8,128)(2,1)S(1)}, bf16[256,512]{1,0:T(8,128)(2,1)S(1)}, u32[]{:S(2)}, u32[]{:S(2)}) collective-permute-start(bf16[256,512]{1,0:T(8,128)(2,1)S(1)} %get-tuple-element.45.refs_0_), channel_id=1, source_target_pairs={{0,2},{2,4},{4,6},{6,8},{8,10},{10,12},{12,14},{14,0},{1,3},{3,5},... | collective-permute-start | bytes 786440 | tf_op jit(solution)/shard_map/cond/branch_0_fun/ppermute | solution.py:259
  36.0 45.0 %collective-permute-start.5 = (bf16[256,512]{1,0:T(8,128)(2,1)S(1)}, bf16[256,512]{1,0:T(8,128)(2,1)S(1)}, u32[]{:S(2)}, u32[]{:S(2)}) collective-permute-start(bf16[256,512]{1,0:T(8,128)(2,1)S(1)} %get-tuple-element.45.refs_0_), channel_id=1, source_target_pairs={{0,14},{2,0},{4,2},{6,4},{8,6},{10,8},{12,10},{14,12},{1,15},{3,1}... | collective-permute-start | bytes 786440 | tf_op jit(solution)/shard_map/cond/branch_0_fun/ppermute | solution.py:259
  75.3 35.0 %all-to-all-start.1 = ((bf16[8,128,512]{2,1,0:T(8,128)(2,1)}), bf16[8,128,512]{2,1,0:T(8,128)(2,1)}, u32[]{:S(2)}, u32[]{:S(2)}) async-start(bf16[8,128,512]{2,1,0:T(8,128)(2,1)} %out_part.4.refs_3_), calls=%async_computation.1 | async-start | bytes 2097152 | tf_op jit(solution)/shard_map/cond/branch_0_fun/all_to_all | solution.py:271
  82.1 24.0 %copy-start.1 = (f32[1,256,512]{2,1,0:T(8,128)S(1)}, f32[1,256,512]{2,1,0:T(8,128)}, u32[]{:S(2)}) copy-start(f32[1,256,512]{2,1,0:T(8,128)} %get-tuple-element.44.numer) | copy-start | bytes 1572868 | tf_op jit(solution)/shard_map/cond
  82.1 24.0 %copy-start.8 = (f32[1,256,512]{2,1,0:T(8,128)S(1)}, f32[1,256,512]{2,1,0:T(8,128)}, u32[]{:S(2)}) copy-start(f32[1,256,512]{2,1,0:T(8,128)} %get-tuple-element.46.moment) | copy-start | bytes 1572868 | tf_op jit(solution)/shard_map/cond
  82.1 3.9 %collective-permute-start.6 = (bf16[2,256,512]{2,1,0:T(8,128)(2,1)S(1)}, bf16[2,256,512]{2,1,0:T(8,128)(2,1)S(1)}, u32[]{:S(2)}, u32[]{:S(2)}) collective-permute-start(bf16[2,256,512]{2,1,0:T(8,128)(2,1)S(1)} %grad_sent.4), channel_id=1, source_target_pairs={{0,1},{1,0},{2,3},{3,2},{4,5},{5,4},{6,7},{7,6},{8,9},{9,8},{10,11... | collective-permute-start | bytes 1572872 | tf_op jit(solution)/shard_map/cond/branch_0_fun/ppermute | solution.py:276
  86.1 20.0 %collective-permute-start.7 = (bf16[256,512]{1,0:T(8,128)(2,1)S(1)}, bf16[256,512]{1,0:T(8,128)(2,1)S(1)}, u32[]{:S(2)}, u32[]{:S(2)}) collective-permute-start(bf16[256,512]{1,0:T(8,128)(2,1)S(1)} %grad_far.4), channel_id=1, source_target_pairs={{0,16},{16,0},{1,17},{17,1},{2,18},{18,2},{3,19},{19,3},{4,20},{20... | collective-permute-start | bytes 786440 | tf_op jit(solution)/shard_map/cond/branch_0_fun/ppermute | solution.py:278
  107.0 12.3 %collective-permute-start.8 = (bf16[272,512]{1,0:T(8,128)(2,1)S(1)}, bf16[272,512]{1,0:T(8,128)(2,1)S(1)}, u32[]{:S(2)}, u32[]{:S(2)}) collective-permute-start(bf16[272,512]{1,0:T(8,128)(2,1)S(1)} %push.4._), channel_id=1, source_target_pairs={{480,0},{0,32},{32,64},{64,96},{96,128},{128,160},{160,192},{192,2... | collective-permute-start | bytes 835592 | tf_op jit(solution)/shard_map/cond/branch_0_fun/ppermute | solution.py:283
